TPU v7x, 32 devices: a whole 2x2x4 slice. The times are simulated.
32 devices in a mesh: tile: 16 (over z, y, x), lev: 2 (over core).
Axes of the slice: x: 2, y: 2, z: 4, core: 2. Of those that a mesh axis runs over, the one named last changes fastest.
Arguments:
- state: bfloat16 [4, 64, 32, 512], P('lev', 'tile'), may hold values from -6 to 6
- w_qkv: bfloat16 [512, 1536], replicated, may hold values from -0.25 to 0.25
- w_out: bfloat16 [512, 512], replicated, may hold values from -0.25 to 0.25
- cotangent: bfloat16 [4, 64, 32, 512], P('lev', 'tile'), may hold values from -6 to 6
- ocean: int32 [16], replicated, may hold values from 0 to 1
- depth: int32 [16], replicated, may hold values from 1 to 4
Outputs:
- output: bfloat16 [4, 64, 32, 512], P('lev', 'tile')
- d_state: bfloat16 [4, 64, 32, 512], P('lev', 'tile')
- d_w_qkv: float32 [512, 1536], P(('tile', 'lev'))
- d_w_out: float32 [512, 512], P(('tile', 'lev'))
All inputs are finite; a program needn't handle non-finite values.
Results may differ from a plain program's by a relative error of at most 0.01.
Values may be sent and summed in bfloat16 or wider, within the bound.
No kernel may reach another device: no remote copies, remote signals or barrier semaphores. Data moves between devices by JAX's collectives and lax.ppermute only.
A program may use at most 128 MiB of HBM per device.

v0:
```python
import jax
import jax.numpy as jnp
from jax import lax
from jax.sharding import PartitionSpec as P

HEADS = 8
BROWS = 4


def with_halo(cells, sides, width):
    for axis, dim in sides:
        count = lax.axis_size(axis)
        ends = count - 1
        head = lax.slice_in_dim(cells, 0, width, axis=dim)
        tail = lax.slice_in_dim(cells, cells.shape[dim] - width, cells.shape[dim], axis=dim)
        cells = jnp.concatenate(
            [
                lax.ppermute(tail, axis, [(i, (i + 1) % count) for i in range(ends)]),
                cells,
                lax.ppermute(head, axis, [((i + 1) % count, i) for i in range(ends)]),
            ],
            axis=dim,
        )
    return cells


def from_behind(block, axis, distance):
    devices = range(lax.axis_size(axis))
    route = [(i - distance, i) for i in devices if i - distance in devices]
    return lax.ppermute(block, axis, route)


def lookup(table, index):
    hits = index[:, None] == jnp.arange(table.shape[0])[None, :]
    return jnp.sum(jnp.where(hits, table[None, :], 0), axis=1)


def halo_rows(field):
    return with_halo(field, (("tile", 1),), 3)


def halo_levels(field):
    return with_halo(field, (("lev", 0),), 1)


def fold_rows(field):
    height = field.shape[1] - 6
    upper = from_behind(field[:, :3].astype(jnp.bfloat16), "tile", -1).astype(jnp.float32)
    lower = from_behind(field[:, height + 3 :].astype(jnp.bfloat16), "tile", 1).astype(jnp.float32)
    inner = field[:, 3 : height + 3]
    inner = inner.at[:, height - 3 :].add(upper)
    return inner.at[:, :3].add(lower)


def fold_levels(field):
    count = field.shape[0] - 2
    upper = from_behind(field[:1].astype(jnp.bfloat16), "lev", -1).astype(jnp.float32)
    lower = from_behind(field[count + 1 :].astype(jnp.bfloat16), "lev", 1).astype(jnp.float32)
    inner = field[1 : count + 1]
    inner = inner.at[count - 1 :].add(upper)
    return inner.at[:1].add(lower)


def attend(queries, keys, values, mask, query_live, upstream, scale):
    scores = jnp.einsum("qhe,khe->hqk", queries, keys, preferred_element_type=jnp.float32) * scale
    scores = jnp.where(mask[None], scores, -1e30)
    top = jnp.max(scores, axis=-1, keepdims=True)
    expo = jnp.exp(scores - top)
    prob = expo / jnp.sum(expo, axis=-1, keepdims=True)
    prob16 = prob.astype(jnp.bfloat16)
    attn = (
        jnp.einsum("hqk,khe->qhe", prob16, values, preferred_element_type=jnp.float32)
        * query_live[:, None, None]
    )
    dprob = jnp.einsum("qhe,khe->hqk", upstream, values, preferred_element_type=jnp.float32)
    dscore = prob * (dprob - jnp.sum(prob * dprob, axis=-1, keepdims=True)) * scale
    ds16 = dscore.astype(jnp.bfloat16)
    dq = jnp.einsum("hqk,khe->qhe", ds16, keys, preferred_element_type=jnp.float32)
    dk = jnp.einsum("hqk,qhe->khe", ds16, queries, preferred_element_type=jnp.float32)
    dv = jnp.einsum("hqk,qhe->khe", prob16, upstream, preferred_element_type=jnp.float32)
    count = queries.shape[0]
    model = queries.shape[1] * queries.shape[2]
    return (
        attn.astype(jnp.bfloat16).reshape(count, model),
        dq.astype(jnp.bfloat16).reshape(count, model),
        jnp.concatenate([dk.reshape(-1, model), dv.reshape(-1, model)], axis=-1),
    )


def local(state, w_qkv, w_out, cotangent, ocean, depth):
    levels_n, height, width, model = state.shape
    heads = HEADS
    head = model // heads
    scale = head ** (-0.5)
    tile_rows = BROWS
    slab_rows = tile_rows + 6
    row_tiles = height // tile_rows
    total_rows = height * lax.axis_size("tile")
    total_levels = levels_n * lax.axis_size("lev")
    key_rows = lax.axis_index("tile") * height - 3 + jnp.arange(height + 6)
    key_levels = lax.axis_index("lev") * levels_n - 1 + jnp.arange(levels_n + 2)
    blocks = jnp.clip(key_rows, 0, total_rows - 1) // BROWS
    sea = lookup(ocean, blocks)
    floor_n = lookup(depth, blocks)
    row_good = (key_rows >= 0) & (key_rows < total_rows) & (sea == 1)
    key_live = row_good[None, :] & (key_levels[:, None] >= 0) & (key_levels[:, None] < total_levels)
    key_live = key_live & (key_levels[:, None] < floor_n[None, :])
    query_live = key_live[1:-1, 3:-3]
    near_rows = jnp.abs(jnp.arange(tile_rows)[:, None] + 3 - jnp.arange(slab_rows)[None, :]) <= 3
    near_cols = jnp.abs(jnp.arange(width)[:, None] - jnp.arange(width)[None, :]) <= 3
    flat = state.reshape(-1, model)
    cot_flat = cotangent.reshape(-1, model)
    qkv = jnp.dot(flat, w_qkv, preferred_element_type=jnp.float32).astype(jnp.bfloat16)
    qkv = qkv.reshape(levels_n, height, width, 3 * model)
    queries = qkv[..., :model]
    pairs = qkv[..., model:]
    upstream = jnp.dot(cot_flat, w_out.T, preferred_element_type=jnp.float32).astype(jnp.bfloat16)
    upstream = upstream.reshape(levels_n, height, width, model) * query_live[
        :, :, None, None
    ].astype(jnp.bfloat16)
    extended = halo_levels(halo_rows(pairs))

    def work(operands):
        return attend(
            operands[0], operands[1], operands[2], operands[3], operands[4], operands[5], scale
        )

    grads = jnp.zeros((levels_n + 2, height + 6, width, 2 * model), jnp.float32)
    attn_list = []
    dq_list = []
    zero = jnp.int32(0)
    for level in range(levels_n):

        def tile_step(index, carry):
            grads, attn_level, dq_level = carry
            row_start = index.astype(jnp.int32) * tile_rows
            lev_at = jnp.int32(level)
            q_now = lax.dynamic_slice(
                queries, (lev_at, row_start, zero, zero), (1, tile_rows, width, model)
            ).reshape(-1, heads, head)
            u_now = lax.dynamic_slice(
                upstream, (lev_at, row_start, zero, zero), (1, tile_rows, width, model)
            ).reshape(-1, heads, head)
            slab = lax.dynamic_slice(
                extended, (lev_at, row_start, zero, zero), (3, slab_rows, width, 2 * model)
            )
            keys = slab[..., :model].reshape(-1, heads, head)
            values = slab[..., model:].reshape(-1, heads, head)
            live_slab = lax.dynamic_slice(key_live, (lev_at, row_start), (3, slab_rows))
            mask = (
                near_rows[:, None, None, :, None]
                & near_cols[None, :, None, None, :]
                & live_slab[None, None, :, :, None]
            )
            mask = mask.reshape(tile_rows * width, -1)
            live_rows = lax.dynamic_slice(query_live, (lev_at, row_start), (1, tile_rows))[0]
            live_now = (
                jnp.broadcast_to(live_rows[:, None], (tile_rows, width))
                .reshape(-1)
                .astype(jnp.float32)
            )
            operands = (q_now, keys, values, mask, live_now, u_now)
            attn, dq, dkv = work(operands)
            start = (lev_at, row_start, zero, zero)
            current = lax.dynamic_slice(grads, start, (3, slab_rows, width, 2 * model))
            grads = lax.dynamic_update_slice(
                grads, current + dkv.reshape(3, slab_rows, width, 2 * model), start
            )
            attn_level = attn.reshape(tile_rows, width, model)
            dq_level = dq.reshape(tile_rows, width, model)
            return (grads, attn_level, dq_level)

        empty = jnp.zeros((height, width, model), jnp.bfloat16)
        grads, attn_level, dq_level = lax.fori_loop(0, row_tiles, tile_step, (grads, empty, empty))
        attn_list.append(attn_level.reshape(-1, model))
        dq_list.append(dq_level.reshape(-1, model))
    folded = fold_rows(fold_levels(grads))
    dkv16 = folded.astype(jnp.bfloat16).reshape(-1, 2 * model)
    attn_flat = jnp.concatenate(attn_list, axis=0)
    dq_flat = jnp.concatenate(dq_list, axis=0)
    dqkv = jnp.concatenate([dq_flat, dkv16], axis=-1)
    output = (
        flat.astype(jnp.float32) + jnp.dot(attn_flat, w_out, preferred_element_type=jnp.float32)
    ).astype(jnp.bfloat16)
    d_state = (
        cot_flat.astype(jnp.float32) + jnp.dot(dqkv, w_qkv.T, preferred_element_type=jnp.float32)
    ).astype(jnp.bfloat16)
    piece = flat
    d_w_qkv = lax.psum_scatter(
        jnp.dot(piece.T, dqkv, preferred_element_type=jnp.float32),
        ("tile", "lev"),
        scatter_dimension=0,
        tiled=True,
    )
    piece = attn_flat
    d_w_out = lax.psum_scatter(
        jnp.dot(piece.T, cot_flat, preferred_element_type=jnp.float32),
        ("tile", "lev"),
        scatter_dimension=0,
        tiled=True,
    )
    shape = (levels_n, height, width, model)
    return (output.reshape(shape), d_state.reshape(shape), d_w_qkv, d_w_out)


def solution(mesh):
    placed = (P("lev", "tile", None, None), P(), P(), P("lev", "tile", None, None), P(), P())
    return jax.shard_map(
        local,
        mesh=mesh,
        in_specs=placed,
        out_specs=(
            P("lev", "tile", None, None),
            P("lev", "tile", None, None),
            P(("tile", "lev"), None),
            P(("tile", "lev"), None),
        ),
        check_vma=False,
    )
```

profile of v0, /device:TPU:0, one launch (start us, length us, event | category | flops | bytes accessed | tf_op | source)
XLA Modules:
  0.0 408.7 jit_solution(10711349020179498024)
XLA Ops:
  8.6 1.5 convolution_convert_fusion
  11.1 4.9 %collective-permute-start = (bf16[2,3,32,1024]{3,2,1,0:T(8,128)(2,1)}, bf16[2,3,32,1024]{3,2,1,0:T(8,128)(2,1)S(1)}, u32[]{:S(2)}, u32[]{:S(2)}) collective-permute-start(bf16[2,3,32,1024]{3,2,1,0:T(8,128)(2,1)} %get-tuple-element.150), channel_id=1, source_target_pairs={{0,2},{2,4},{4,6},{6,8},{8,10},{10,12},{12,14},{14,16},{16,18},{18... | collective-permute-start | bytes 1179656 | tf_op jit(solution)/shard_map/ppermute | solution.py:18
  20.0 1.4 convolution_convert_fusion.1
  26.8 6.2 %collective-permute-done = bf16[2,3,32,1024]{3,2,1,0:T(8,128)(2,1)S(1)} collective-permute-done((bf16[2,3,32,1024]{3,2,1,0:T(8,128)(2,1)}, bf16[2,3,32,1024]{3,2,1,0:T(8,128)(2,1)S(1)}, u32[]{:S(2)}, u32[]{:S(2)}) %collective-permute-start) | collective-permute-done | bytes 393248 | tf_op jit(solution)/shard_map/ppermute | solution.py:18
  33.0 1.9 collective-permute-done.1
  37.3 2.1 collective-permute-start.2
  45.2 2.3 maximum_maximum_fusion
  47.5 2.1 fusion.82
  49.6 2.7 reshape.413
  52.3 2.6 copy.66
  54.9 2.7 reshape.411
  57.6 2.6 copy.67
  60.2 2.7 reshape.415
  62.9 2.6 copy.70
  65.5 2.7 reshape.417
  68.2 2.6 copy.69
  70.8 4.0 fusion.93
  74.8 3.4 fusion.90
  78.2 4.5 %convolution_bitcast_fusion.1 = f32[960,8,64]{0,2,1:T(8,128)} fusion(bf16[128,8,64]{0,2,1:T(8,128)(2,1)S(1)} %copy-done.12, f32[8,128,960]{1,2,0:T(8,128)} %get-tuple-element.161, f32[8,128]{1,0:T(8,128)S(1)} %get-tuple-element.160), kind=kOutput, calls=%fused_computation.40 | convolution fusion | flops 127795200 | bytes 6033408 | tf_op jit(solution)/shard_map/while/body/eval_jaxpr/hqk,qhe->khe/dot_general | solution.py:80
  84.0 3.8 copy.86
  87.8 3.5 concatenate.56
  91.3 8.3 %fusion.35 = f32[960,8,64]{0,2,1:T(8,128)} fusion(bf16[128,8,64]{0,2,1:T(8,128)(2,1)} %copy.68, f32[8,128,960]{1,2,0:T(8,128)} %fusion.93, f32[8,128,960]{1,2,0:T(8,128)} %get-tuple-element.161, f32[8,128]{1,0:T(8,128)S(1)} %get-tuple-element.160), kind=kOutput, calls=%fused_computation.38 | convolution fusion | flops 132712384 | bytes 9965568 | tf_op jit(solution)/shard_map/while/body/eval_jaxpr/hqk,qhe->khe/dot_general | solution.py:79
  99.7 3.8 copy.84
  103.5 4.6 %concatenate.55 = f32[3,10,32,512]{3,2,1,0:T(8,128)} reshape(f32[960,8,64]{2,1,0:T(8,128)} %copy.84) | data formatting | bytes 3932160 | tf_op jit(solution)/shard_map/while/body/eval_jaxpr/concatenate | solution.py:86
  108.1 4.7 %fusion.91 = (f32[8,128]{1,0:T(8,128)S(1)}, f32[8,128,960]{1,2,0:T(8,128)}) fusion(pred[128,960]{0,1:T(8,128)(4,1)} %get-tuple-element.154, bf16[128,8,64]{0,2,1:T(8,128)(2,1)} %copy.65, bf16[960,8,64]{0,2,1:T(8,128)(2,1)} %copy.66), kind=kOutput, calls=%fused_computation.125 | convolution fusion | flops 129762240 | bytes 5173248 | tf_op jit(solution)/shard_map/while/body/eval_jaxpr/sub | solution.py:68
  112.8 4.4 %convolution_bitcast_fusion.2 = f32[960,8,64]{0,2,1:T(8,128)} fusion(bf16[128,8,64]{0,2,1:T(8,128)(2,1)} %copy.71, f32[8,128,960]{1,2,0:T(8,128)} %get-tuple-element.163, f32[8,128]{1,0:T(8,128)S(1)} %get-tuple-element.162), kind=kOutput, calls=%fused_computation.41 | convolution fusion | flops 127795200 | bytes 6033408 | tf_op jit(solution)/shard_map/while/body/eval_jaxpr/hqk,qhe->khe/dot_general | solution.py:80
  117.1 3.8 copy.82
  120.9 4.6 %concatenate.53 = f32[3,10,32,512]{3,2,1,0:T(8,128)} reshape(f32[960,8,64]{2,1,0:T(8,128)} %copy.82) | data formatting | bytes 3932160 | tf_op jit(solution)/shard_map/while/body/eval_jaxpr/concatenate | solution.py:86
  125.6 4.0 fusion.92
  129.6 8.3 %fusion.38 = f32[960,8,64]{0,2,1:T(8,128)} fusion(bf16[128,8,64]{0,2,1:T(8,128)(2,1)} %copy.65, f32[8,128,960]{1,2,0:T(8,128)} %fusion.92, f32[8,128,960]{1,2,0:T(8,128)} %get-tuple-element.163, f32[8,128]{1,0:T(8,128)S(1)} %get-tuple-element.162), kind=kOutput, calls=%fused_computation.39 | convolution fusion | flops 132712384 | bytes 9965568 | tf_op jit(solution)/shard_map/while/body/eval_jaxpr/hqk,qhe->khe/dot_general | solution.py:79
  137.9 3.8 copy.80
  141.6 4.6 %concatenate.52 = f32[3,10,32,512]{3,2,1,0:T(8,128)} reshape(f32[960,8,64]{2,1,0:T(8,128)} %copy.80) | data formatting | bytes 3932160 | tf_op jit(solution)/shard_map/while/body/eval_jaxpr/concatenate | solution.py:86
  146.2 1.9 constant_dynamic-update-slice_fusion.1
  150.4 4.2 %collective-permute-start.5 = (bf16[1,10,32,1024]{3,2,1,0:T(8,128)(2,1)S(1)}, bf16[1,10,32,1024]{3,2,1,0:T(8,128)(2,1)S(1)}, u32[]{:S(2)}, u32[]{:S(2)}) collective-permute-start(bf16[1,10,32,1024]{3,2,1,0:T(8,128)(2,1)S(1)} %slice.257), channel_id=1, source_target_pairs={{0,1},{2,3},{4,5},{6,7},{8,9},{10,11},{12,13},{14,15},{16,17},{18,... | collective-permute-start | bytes 1966088 | tf_op jit(solution)/shard_map/ppermute | solution.py:30
  156.6 1.7 slice.232
  160.0 2.8 fusion.42
  162.8 2.6 fusion.41
  165.5 1.9 convert.14
  168.2 1.4 collective-permute-start.6
  169.6 7.2 %fusion.45 = bf16[8,64,128]{2,1,0:T(8,128)(2,1)S(1)} fusion(bf16[960,8,64]{0,2,1:T(8,128)(2,1)} %copy.69, f32[8,128,960]{1,2,0:T(8,128)} %fusion.93, f32[8,128,960]{1,2,0:T(8,128)} %get-tuple-element.161, f32[8,128]{1,0:T(8,128)S(1)} %get-tuple-element.160), kind=kOutput, calls=%fused_computation.56 | convolution fusion | flops 132777920 | bytes 8982528 | tf_op jit(solution)/shard_map/while/body/eval_jaxpr/hqk,khe->qhe/dot_general | solution.py:78
  176.9 5.3 %collective-permute-start.7 = (bf16[2,3,32,1024]{3,2,1,0:T(8,128)(2,1)S(1)}, bf16[2,3,32,1024]{3,2,1,0:T(8,128)(2,1)}, u32[]{:S(2)}, u32[]{:S(2)}) collective-permute-start(bf16[2,3,32,1024]{3,2,1,0:T(8,128)(2,1)S(1)} %get-tuple-element.142), channel_id=1, source_target_pairs={{0,2},{2,4},{4,6},{6,8},{8,10},{10,12},{12,14},{14,16},{16,18},{18... | collective-permute-start | bytes 1179656 | tf_op jit(solution)/shard_map/ppermute | solution.py:30
  182.2 7.0 %fusion.48 = bf16[8,64,128]{2,1,0:T(8,128)(2,1)S(1)} fusion(bf16[960,8,64]{0,2,1:T(8,128)(2,1)S(1)} %copy-done.7, f32[8,128,960]{1,2,0:T(8,128)} %fusion.92, f32[8,128,960]{1,2,0:T(8,128)} %get-tuple-element.163, f32[8,128]{1,0:T(8,128)S(1)} %get-tuple-element.162), kind=kOutput, calls=%fused_computation.57 | convolution fusion | flops 132777920 | bytes 8982528 | tf_op jit(solution)/shard_map/while/body/eval_jaxpr/hqk,khe->qhe/dot_general | solution.py:78
  190.8 1.4 fusion.58
  193.4 2.3 convolution_bitcast_fusion
  195.7 3.6 copy.88
  199.4 1.9 fusion.43
  202.6 94.8 %reduce-scatter.5.cloned.1.call-done = f32[16,512]{1,0:T(8,128)} async-done(((f32[512,512]{1,0:T(8,128)}), f32[16,512]{1,0:T(8,128)}) %reduce-scatter.5.cloned.1.call-update) | async-done | bytes 32784 | tf_op jit(solution)/shard_map/reduce_scatter | solution.py:196
  297.5 104.4 %reduce-scatter.7.cloned.1.call-done = f32[16,1536]{1,0:T(8,128)} async-done(((f32[512,1536]{1,0:T(8,128)}), f32[16,1536]{1,0:T(8,128)}) %reduce-scatter.7.cloned.1.call-update) | async-done | bytes 98320
  (116 shorter events, 31.9 us)
Async XLA Ops:
  7.2 1.4 copy-start
  7.2 10.1 %copy-start.20 = (s32[16]{0:T(128)S(1)}, s32[16]{0:T(128)}, u32[]{:S(2)}) copy-start(s32[16]{0:T(128)} %param.19) | copy-start | bytes 196
  7.2 10.1 %copy-start.19 = (s32[16]{0:T(128)S(1)}, s32[16]{0:T(128)}, u32[]{:S(2)}) copy-start(s32[16]{0:T(128)} %param.18) | copy-start | bytes 196
  7.2 12.8 %copy-start.10 = (bf16[2,4,32,512]{3,2,1,0:T(8,128)(2,1)S(1)}, bf16[2,4,32,512]{3,2,1,0:T(8,128)(2,1)}, u32[]{:S(2)}) copy-start(bf16[2,4,32,512]{3,2,1,0:T(8,128)(2,1)} %param.17) | copy-start | bytes 786436
  7.2 290.3 %reduce-scatter.5.cloned.1.call-start = ((), (), s32[]{:S(2)}) async-start(), calls=%async_computation.2 | async-start | bytes 1081344 | tf_op jit(solution)/shard_map/reduce_scatter | solution.py:196
  11.1 21.9 %collective-permute-start = (bf16[2,3,32,1024]{3,2,1,0:T(8,128)(2,1)}, bf16[2,3,32,1024]{3,2,1,0:T(8,128)(2,1)S(1)}, u32[]{:S(2)}, u32[]{:S(2)}) collective-permute-start(bf16[2,3,32,1024]{3,2,1,0:T(8,128)(2,1)} %get-tuple-element.150), channel_id=1, source_target_pairs={{0,2},{2,4},{4,6},{6,8},{8,10},{10,12},{12,14},{14,16},{16,18},{18... | collective-permute-start | bytes 1179656 | tf_op jit(solution)/shard_map/ppermute | solution.py:18
  16.0 19.0 %collective-permute-start.1 = (bf16[2,3,32,1024]{3,2,1,0:T(8,128)(2,1)}, bf16[2,3,32,1024]{3,2,1,0:T(8,128)(2,1)}, u32[]{:S(2)}, u32[]{:S(2)}) collective-permute-start(bf16[2,3,32,1024]{3,2,1,0:T(8,128)(2,1)} %get-tuple-element.151), channel_id=1, source_target_pairs={{2,0},{4,2},{6,4},{8,6},{10,8},{12,10},{14,12},{16,14},{18,16},{20... | collective-permute-start | bytes 1179656 | tf_op jit(solution)/shard_map/ppermute | solution.py:20
  33.0 7.7 %copy-start.6 = (bf16[2,3,32,1024]{3,2,1,0:T(8,128)(2,1)}, bf16[2,3,32,1024]{3,2,1,0:T(8,128)(2,1)S(1)}, u32[]{:S(2)}) copy-start(bf16[2,3,32,1024]{3,2,1,0:T(8,128)(2,1)S(1)} %collective-permute-done) | copy-start | bytes 1179652
  37.3 7.9 %collective-permute-start.2 = (bf16[1,10,32,1024]{3,2,1,0:T(8,128)(2,1)}, bf16[1,10,32,1024]{3,2,1,0:T(8,128)(2,1)}, u32[]{:S(2)}, u32[]{:S(2)}) collective-permute-start(bf16[1,10,32,1024]{3,2,1,0:T(8,128)(2,1)} %get-tuple-element.146), channel_id=1, source_target_pairs={{0,1},{2,3},{4,5},{6,7},{8,9},{10,11},{12,13},{14,15},{16,17},{18,... | collective-permute-start | bytes 1966088 | tf_op jit(solution)/shard_map/ppermute | solution.py:18
  39.4 5.8 %collective-permute-start.3 = (bf16[1,10,32,1024]{3,2,1,0:T(8,128)(2,1)}, bf16[1,10,32,1024]{3,2,1,0:T(8,128)(2,1)}, u32[]{:S(2)}, u32[]{:S(2)}) collective-permute-start(bf16[1,10,32,1024]{3,2,1,0:T(8,128)(2,1)} %get-tuple-element.147), channel_id=1, source_target_pairs={{1,0},{3,2},{5,4},{7,6},{9,8},{11,10},{13,12},{15,14},{17,16},{19,... | collective-permute-start | bytes 1966088 | tf_op jit(solution)/shard_map/ppermute | solution.py:20
  70.8 4.0 copy-start.8
  70.8 4.0 copy-start.17
  70.8 4.0 copy-start.18
  74.8 3.4 copy-start.12
  78.2 4.5 %copy-start.5 = (bf16[960,8,64]{0,2,1:T(8,128)(2,1)S(1)}, bf16[960,8,64]{0,2,1:T(8,128)(2,1)}, u32[]{:S(2)}) copy-start(bf16[960,8,64]{0,2,1:T(8,128)(2,1)} %copy.70) | copy-start | bytes 2949124
  78.2 4.5 %copy-start.22 = (f32[128]{0:T(128)S(1)}, f32[128]{0:T(128)}, u32[]{:S(2)}) copy-start(f32[128]{0:T(128)} %convert_element_type.126) | copy-start | bytes 1540
  78.2 4.5 %copy-start.23 = (f32[8,128,960]{1,2,0:T(8,128)S(1)}, f32[8,128,960]{1,2,0:T(8,128)}, u32[]{:S(2)}) copy-start(f32[8,128,960]{1,2,0:T(8,128)} %get-tuple-element.161) | copy-start | bytes 11796484
  146.2 2.1 copy-start.3
  146.2 3.3 copy-start.2
  149.5 6.4 %copy-start.4 = (bf16[960,8,64]{0,2,1:T(8,128)(2,1)S(1)}, bf16[960,8,64]{0,2,1:T(8,128)(2,1)}, u32[]{:S(2)}) copy-start(bf16[960,8,64]{0,2,1:T(8,128)(2,1)} %copy.67) | copy-start | bytes 2949124
  149.5 6.4 %copy-start.21 = (f32[128]{0:T(128)S(1)}, f32[128]{0:T(128)}, u32[]{:S(2)}) copy-start(f32[128]{0:T(128)} %convert_element_type.120) | copy-start | bytes 1540
  149.5 6.4 %copy-start.24 = (f32[8,128,960]{1,2,0:T(8,128)S(1)}, f32[8,128,960]{1,2,0:T(8,128)}, u32[]{:S(2)}) copy-start(f32[8,128,960]{1,2,0:T(8,128)} %get-tuple-element.163) | copy-start | bytes 11796484
  150.3 6.3 %copy-start.1 = (f32[3,10,32,1024]{3,2,1,0:T(8,128)}, f32[3,10,32,1024]{3,2,1,0:T(8,128)S(1)}, u32[]{:S(2)}) copy-start(f32[3,10,32,1024]{3,2,1,0:T(8,128)S(1)} %fusion.4) | copy-start | bytes 11796484
  150.4 12.4 %collective-permute-start.5 = (bf16[1,10,32,1024]{3,2,1,0:T(8,128)(2,1)S(1)}, bf16[1,10,32,1024]{3,2,1,0:T(8,128)(2,1)S(1)}, u32[]{:S(2)}, u32[]{:S(2)}) collective-permute-start(bf16[1,10,32,1024]{3,2,1,0:T(8,128)(2,1)S(1)} %slice.257), channel_id=1, source_target_pairs={{0,1},{2,3},{4,5},{6,7},{8,9},{10,11},{12,13},{14,15},{16,17},{18,... | collective-permute-start | bytes 1966088 | tf_op jit(solution)/shard_map/ppermute | solution.py:30
  154.6 5.4 %collective-permute-start.4 = (bf16[1,10,32,1024]{3,2,1,0:T(8,128)(2,1)}, bf16[1,10,32,1024]{3,2,1,0:T(8,128)(2,1)}, u32[]{:S(2)}, u32[]{:S(2)}) collective-permute-start(bf16[1,10,32,1024]{3,2,1,0:T(8,128)(2,1)} %slice.258), channel_id=1, source_target_pairs={{1,0},{3,2},{5,4},{7,6},{9,8},{11,10},{13,12},{15,14},{17,16},{19,... | collective-permute-start | bytes 1966088 | tf_op jit(solution)/shard_map/ppermute | solution.py:30
  156.6 3.1 copy-start.16
  156.6 1.8 copy-start.11
  156.6 1.7 copy-start.14
  159.7 242.1 %reduce-scatter.7.cloned.1.call-start = ((), (), s32[]{:S(2)}) async-start(), calls=%async_computation.3 | async-start | bytes 3244032
  168.2 14.0 %copy-start.7 = (bf16[960,8,64]{0,2,1:T(8,128)(2,1)S(1)}, bf16[960,8,64]{0,2,1:T(8,128)(2,1)}, u32[]{:S(2)}) copy-start(bf16[960,8,64]{0,2,1:T(8,128)(2,1)} %copy.66) | copy-start | bytes 2949124
  168.2 22.6 %collective-permute-start.6 = (bf16[2,3,32,1024]{3,2,1,0:T(8,128)(2,1)}, bf16[2,3,32,1024]{3,2,1,0:T(8,128)(2,1)}, u32[]{:S(2)}, u32[]{:S(2)}) collective-permute-start(bf16[2,3,32,1024]{3,2,1,0:T(8,128)(2,1)} %get-tuple-element.143), channel_id=1, source_target_pairs={{2,0},{4,2},{6,4},{8,6},{10,8},{12,10},{14,12},{16,14},{18,16},{20... | collective-permute-start | bytes 1179656 | tf_op jit(solution)/shard_map/ppermute | solution.py:30
  176.9 15.3 %collective-permute-start.7 = (bf16[2,3,32,1024]{3,2,1,0:T(8,128)(2,1)S(1)}, bf16[2,3,32,1024]{3,2,1,0:T(8,128)(2,1)}, u32[]{:S(2)}, u32[]{:S(2)}) collective-permute-start(bf16[2,3,32,1024]{3,2,1,0:T(8,128)(2,1)S(1)} %get-tuple-element.142), channel_id=1, source_target_pairs={{0,2},{2,4},{4,6},{6,8},{8,10},{10,12},{12,14},{14,16},{16,18},{18... | collective-permute-start | bytes 1179656 | tf_op jit(solution)/shard_map/ppermute | solution.py:30
  189.3 4.1 %copy-start.9 = (bf16[2,4,32,512]{3,2,1,0:T(8,128)(2,1)S(1)}, bf16[2,4,32,512]{3,2,1,0:T(8,128)(2,1)}, u32[]{:S(2)}) copy-start(bf16[2,4,32,512]{3,2,1,0:T(8,128)(2,1)} %param.14) | copy-start | bytes 786436
  195.7 3.6 copy-start.13
  195.7 3.6 copy-start.15
Sparse Core Ops, SparseCore 0:
  159.8 137.6 reduce-scatter.4
  304.4 97.4 reduce-scatter.6
where the time goes:
time: 410 us; the launch traced here: 409 us
  waiting for transfers between devices  207 us (50%)
  local copies, waits for them, and re-layouts  79.8 us (19%)
  matrix products  67.5 us (16%)
  starting transfers between devices  22.1 us (5%)
  other arithmetic  17.2 us (4%)
  between operations  14.6 us (4%)
    unnamed x3, waiting for transfers between devices  104 us
    reduce_scatter x1, waiting for transfers between devices, local(): lax.psum_scatter(jnp.dot(piece.T, cot_flat, preferred_element_type=jnp.fl...  94.8 us
    concatenate x5, local copies, waits for them, and re-layouts, attend(): jnp.concatenate([dk.reshape(-1, model), dv.reshape(-1, model)], axis=-1)  17.5 us
    dot_general x2, matrix products, attend(): jnp.einsum('hqk,qhe->khe', ds16, queries, preferred_element_type=jnp.floa...  16.6 us
    dot_general x2, matrix products, attend(): jnp.einsum('hqk,khe->qhe', ds16, keys, preferred_element_type=jnp.float32)  14.2 us
    ppermute x4, starting transfers between devices, from_behind(): return lax.ppermute(block, axis, route)  12.2 us
    reshape x4, local copies, waits for them, and re-layouts, tile_step(): values = slab[..., model:].reshape(-1, heads, head)  10.6 us
    reshape x4, local copies, waits for them, and re-layouts, tile_step(): keys = slab[..., :model].reshape(-1, heads, head)  10.5 us
  transfers between devices with their start and end apart: 10, of which 4 were waited for; matrix products, arithmetic and copies ran while one was open for 13% of the time, Pallas kernels for 0%

commit v1 on v0

v1 whole, which is shorter than its diff:
```python
import jax
import jax.numpy as jnp
from jax import lax
from jax.experimental import pallas as pl
from jax.experimental.pallas import tpu as pltpu
from jax.sharding import PartitionSpec as P

HEADS = 8
BROWS = 4
REACH = 3
GROUP = 4
PAIR = 2
LOW = -1e30
F32 = jnp.float32
BF16 = jnp.bfloat16


def dot(a, b, ca, cb):
    return lax.dot_general(a, b, (((ca,), (cb,)), ((), ())), preferred_element_type=F32)


def swap_pairs(count, first):
    route = []
    for i in range(first, count - 1, 2):
        route += [(i, i + 1), (i + 1, i)]
    return route


def kernel(with_odd, tiles, levs, *refs):
    ocean, depth, state, rows_e, rows_o, near_e, far_e = refs[:7]
    refs = refs[7:]
    if with_odd:
        near_o, far_o = refs[:2]
        refs = refs[2:]
    w_qkv, w_out, cot = refs[:3]
    out, own, dext, dw = refs[3:7]
    ext, kv, qs, us, attn, dq, dkv, dkv16, bias, live = refs[7:]
    levels_n, height, width, model = state.shape
    tall = height + 2 * REACH
    span = PAIR + 2 * REACH
    keys_n = 3 * span * width
    block = PAIR * width
    head = model // HEADS
    lanes_n = GROUP * head
    tile = lax.axis_index("tile")
    lev = lax.axis_index("lev")
    tile_odd = lax.rem(tile, 2)
    lev_odd = lax.rem(lev, 2)

    total_rows = height * tiles
    total_levels = levels_n * levs
    for r in range(tall):
        row = tile * height - REACH + r
        block_at = lax.div(jnp.clip(row, 0, total_rows - 1), BROWS)
        good = (row >= 0) & (row < total_rows) & (ocean[block_at] == 1)
        deep = depth[block_at]
        for l in range(levels_n + 2):
            at = lev * levels_n - 1 + l
            ok = good & (at >= 0) & (at < total_levels) & (at < deep)
            live[l * tall + r] = ok.astype(jnp.int32)

    ext[1 : levels_n + 1, REACH : height + REACH] = state[...]
    at_e = jnp.where(tile_odd == 0, height + REACH, 0)
    at_o = jnp.where(tile_odd == 0, 0, height + REACH)
    ext[1 : levels_n + 1, pl.ds(at_e, REACH)] = rows_e[...]
    ext[1 : levels_n + 1, pl.ds(at_o, REACH)] = rows_o[...]
    slot_e = jnp.where(lev_odd == 0, levels_n + 1, 0)
    slot_o = jnp.where(lev_odd == 0, 0, levels_n + 1)
    ext[slot_e, REACH : height + REACH] = near_e[...]
    ext[slot_e, pl.ds(at_e, REACH)] = far_e[0]
    ext[slot_e, pl.ds(at_o, REACH)] = far_e[1]
    if with_odd:
        ext[slot_o, REACH : height + REACH] = near_o[...]
        ext[slot_o, pl.ds(at_e, REACH)] = far_o[0]
        ext[slot_o, pl.ds(at_o, REACH)] = far_o[1]
    else:
        ext[slot_o] = jnp.zeros((tall, width, model), BF16)

    @pl.loop(0, levels_n + 2)
    def _(l):
        cells = ext[l].reshape(tall * width, model)
        pairs = dot(cells, w_qkv[:, model:], 1, 0).astype(BF16)
        kv[l] = pairs.reshape(tall, width, 2 * model)
        dkv[l] = jnp.zeros((tall, width, 2 * model), F32)

    for l in range(levels_n):
        flat = state[l].reshape(height * width, model)
        q = dot(flat, w_qkv[:, :model], 1, 0).astype(BF16) * jnp.asarray(head**-0.5, BF16)
        qs[l] = q.reshape(height, width, model)
        u = dot(cot[l].reshape(height * width, model), w_out[...], 1, 1).astype(BF16)
        u = u.reshape(height, width, model)
        for r in range(height):
            alive = live[(l + 1) * tall + REACH + r].astype(F32).astype(BF16)
            us[l, r] = u[r] * alive

    lane_head = lax.broadcasted_iota(jnp.int32, (block, lanes_n), 1) // head
    query = lax.broadcasted_iota(jnp.int32, (width, GROUP * block), 1) % block
    query_row = query // width
    query_col = query % width
    key_col = lax.broadcasted_iota(jnp.int32, (width, GROUP * block), 0)
    near_col = jnp.abs(key_col - query_col) <= REACH

    def spread(x):
        return jnp.concatenate(
            [jnp.where(lane_head == h, x, jnp.zeros_like(x)) for h in range(GROUP)], axis=0
        )

    def gather(x):
        total = jnp.where(lane_head == 0, x[:block], 0.0)
        for h in range(1, GROUP):
            total = jnp.where(lane_head == h, x[h * block : (h + 1) * block], total)
        return total

    pairs_n = height // PAIR

    @pl.loop(0, levels_n * pairs_n)
    def _(combo):
        l = combo // pairs_n
        r0 = (combo % pairs_n) * PAIR
        for dl in range(3):
            for kr in range(span):
                alive = live[(l + dl) * tall + r0 + kr] == 1
                near = near_col & (jnp.abs(query_row + REACH - kr) <= REACH)
                at = (dl * span + kr) * width
                bias[at : at + width] = jnp.where(near & alive, 0.0, LOW)
        for g in range(HEADS // GROUP):
            lanes = slice(g * lanes_n, (g + 1) * lanes_n)
            lanes_v = slice(model + g * lanes_n, model + (g + 1) * lanes_n)
            q = spread(qs[l, pl.ds(r0, PAIR), :, lanes].reshape(block, lanes_n))
            u = spread(us[l, pl.ds(r0, PAIR), :, lanes].reshape(block, lanes_n))
            k = kv[pl.ds(l, 3), pl.ds(r0, span), :, lanes].reshape(keys_n, lanes_n)
            v = kv[pl.ds(l, 3), pl.ds(r0, span), :, lanes_v].reshape(keys_n, lanes_n)
            s = dot(k, q, 1, 1) + bias[...]
            e = jnp.exp(s - jnp.max(s, axis=0, keepdims=True))
            p = e * (1.0 / jnp.sum(e, axis=0, keepdims=True))
            p16 = p.astype(BF16)
            dp = dot(v, u, 1, 1)
            ds = p * (dp - jnp.sum(p * dp, axis=0, keepdims=True))
            ds16 = ds.astype(BF16)
            a = gather(dot(p16, v, 0, 0))
            for r in range(PAIR):
                alive = live[(l + 1) * tall + REACH + r0 + r].astype(F32)
                attn[l, r0 + r, :, lanes] = (a[r * width : (r + 1) * width] * alive).astype(BF16)
            b = gather(dot(ds16, k, 0, 0)) * (head**-0.5)
            dq[l, pl.ds(r0, PAIR), :, lanes] = b.astype(BF16).reshape(PAIR, width, lanes_n)
            dk = dot(ds16, q, 1, 0).reshape(3, span, width, lanes_n)
            dkv[pl.ds(l, 3), pl.ds(r0, span), :, lanes] += dk
            dv = dot(p16, u, 1, 0).reshape(3, span, width, lanes_n)
            dkv[pl.ds(l, 3), pl.ds(r0, span), :, lanes_v] += dv

    for l in range(levels_n):
        flat = state[l].reshape(height * width, model)
        o = flat.astype(F32) + dot(attn[l].reshape(height * width, model), w_out[...], 1, 0)
        out[l] = o.astype(BF16).reshape(height, width, model)
        c = cot[l].reshape(height * width, model).astype(F32)
        c = c + dot(dq[l].reshape(height * width, model), w_qkv[:, :model], 1, 1)
        own[l] = c.reshape(height, width, model)

    @pl.loop(0, levels_n + 2)
    def _(l):
        d = dkv[l].astype(BF16)
        dkv16[l] = d
        part = dot(d.reshape(tall * width, 2 * model), w_qkv[:, model:], 1, 1)
        part = part.reshape(tall, width, model)
        dext[l] = part.astype(BF16)

        @pl.when((l > 0) & (l <= levels_n))
        def _():
            own[l - 1] += part[REACH : REACH + height]

    cells = levels_n * height * width
    dw[:, :model] = dot(state[...].reshape(cells, model), dq[...].reshape(cells, model), 0, 0)
    dw[:, 3 * model :] = dot(attn[...].reshape(cells, model), cot[...].reshape(cells, model), 0, 0)
    wide = (levels_n + 2) * tall * width
    for j in range(2):
        cols = slice(j * model, (j + 1) * model)
        dw[:, model + j * model : 2 * model + j * model] = dot(
            ext[...].reshape(wide, model), dkv16[:, :, :, cols].reshape(wide, model), 0, 0
        )


def pick(x, index, dim):
    return lax.dynamic_index_in_dim(x, index, dim, keepdims=False)


def scatter_stage(x, axis, dim, stride):
    radix = x.shape[dim]
    if radix == 1:
        return lax.index_in_dim(x, 0, dim, keepdims=False)
    count = lax.axis_size(axis)
    digit = lax.rem(lax.div(lax.axis_index(axis), stride), radix)
    total = pick(x, digit, dim)
    parts = []
    for k in range(1, radix):
        piece = pick(x, jnp.bitwise_xor(digit, k), dim).astype(BF16)
        parts.append(lax.ppermute(piece, axis, [(i, i ^ (k * stride)) for i in range(count)]))
    for part in parts:
        total = total + part.astype(F32)
    return total


def digits(count):
    sizes = []
    while count > 1:
        radix = 4 if count % 4 == 0 else 2
        sizes.append(radix)
        count //= radix
    return sizes


def scatter_sum(x):
    tiles, levs = lax.axis_size("tile"), lax.axis_size("lev")
    rows, cols = x.shape
    low_t, low_l = digits(tiles), digits(levs)
    shape = low_t[::-1] + low_l[::-1] + [rows // (tiles * levs), cols]
    x = x.reshape(shape)
    stride = 1
    for i, radix in enumerate(low_l):
        x = scatter_stage(x, "lev", len(low_t) + len(low_l) - 1 - i, stride)
        stride *= radix
    stride = 1
    for i, radix in enumerate(low_t):
        x = scatter_stage(x, "tile", len(low_t) - 1 - i, stride)
        stride *= radix
    return x


def local(state, w_qkv, w_out, cotangent, ocean, depth):
    levels_n, height, width, model = state.shape
    tiles, levs = lax.axis_size("tile"), lax.axis_size("lev")
    tile_odd = lax.rem(lax.axis_index("tile"), 2)
    lev_odd = lax.rem(lax.axis_index("lev"), 2)
    tall = height + 2 * REACH
    with_odd = levs > 2

    def swap(block, axis, first):
        return lax.ppermute(block, axis, swap_pairs(lax.axis_size(axis), first))

    top = height - REACH
    send_e = lax.dynamic_slice_in_dim(state, jnp.where(tile_odd == 0, top, 0), REACH, 1)
    send_o = lax.dynamic_slice_in_dim(state, jnp.where(tile_odd == 0, 0, top), REACH, 1)
    rows_e = swap(send_e, "tile", 0)
    rows_o = swap(send_o, "tile", 1)
    edge_e = jnp.where(lev_odd == 0, levels_n - 1, 0)
    edge_o = jnp.where(lev_odd == 0, 0, levels_n - 1)

    def far(edge):
        return jnp.stack([pick(rows_e, edge, 0), pick(rows_o, edge, 0)])

    levels = [swap(pick(state, edge_e, 0), "lev", 0), swap(far(edge_e), "lev", 0)]
    if with_odd:
        levels += [swap(pick(state, edge_o, 0), "lev", 1), swap(far(edge_o), "lev", 1)]

    smem = pl.BlockSpec(memory_space=pltpu.SMEM)
    vmem = pl.BlockSpec(memory_space=pltpu.VMEM)
    wide = (levels_n + 2, tall, width)
    own_cells = (levels_n, height, width, model)
    keys_n = 3 * (PAIR + 2 * REACH) * width
    out, own, dext, dw = pl.pallas_call(
        lambda *refs: kernel(with_odd, tiles, levs, *refs),
        out_shape=(
            jax.ShapeDtypeStruct(own_cells, BF16),
            jax.ShapeDtypeStruct(own_cells, F32),
            jax.ShapeDtypeStruct(wide + (model,), BF16),
            jax.ShapeDtypeStruct((model, 4 * model), F32),
        ),
        in_specs=[smem, smem] + [vmem] * (6 + len(levels)),
        out_specs=(vmem, vmem, vmem, vmem),
        scratch_shapes=[
            pltpu.VMEM(wide + (model,), BF16),
            pltpu.VMEM(wide + (2 * model,), BF16),
            pltpu.VMEM(own_cells, BF16),
            pltpu.VMEM(own_cells, BF16),
            pltpu.VMEM(own_cells, BF16),
            pltpu.VMEM(own_cells, BF16),
            pltpu.VMEM(wide + (2 * model,), F32),
            pltpu.VMEM(wide + (2 * model,), BF16),
            pltpu.VMEM((keys_n, GROUP * PAIR * width), F32),
            pltpu.SMEM(((levels_n + 2) * tall,), jnp.int32),
        ],
        compiler_params=pltpu.CompilerParams(vmem_limit_bytes=56 * 2**20),
    )(ocean, depth, state, rows_e, rows_o, *levels, w_qkv, w_out, cotangent)

    def onto(part, level):
        zero = jnp.zeros_like(part)
        return jnp.stack([jnp.where(level == l, part, zero) for l in range(levels_n)])

    slot_e = jnp.where(lev_odd == 0, levels_n + 1, 0)
    slot_o = jnp.where(lev_odd == 0, 0, levels_n + 1)
    across = onto(swap(pick(dext, slot_e, 0), "lev", 0).astype(F32), edge_e)
    if with_odd:
        across = across + onto(swap(pick(dext, slot_o, 0), "lev", 1).astype(F32), edge_o)
    at_e = jnp.where(tile_odd == 0, height + REACH, 0)
    at_o = jnp.where(tile_odd == 0, 0, height + REACH)

    def halo(at):
        mine = lax.dynamic_slice_in_dim(dext[1 : levels_n + 1], at, REACH, 1).astype(F32)
        return (mine + lax.dynamic_slice_in_dim(across, at, REACH, 1)).astype(BF16)

    back_e = swap(halo(at_e), "tile", 0).astype(F32)
    back_o = swap(halo(at_o), "tile", 1).astype(F32)
    above = jnp.where(tile_odd == 0, back_e, back_o)
    below = jnp.where(tile_odd == 0, back_o, back_e)
    rest = ((0, 0), (0, 0))
    d_state = own + across[:, REACH : REACH + height]
    d_state = d_state + jnp.pad(above, ((0, 0), (top, 0)) + rest)
    d_state = d_state + jnp.pad(below, ((0, 0), (0, top)) + rest)
    grads = scatter_sum(dw)
    return (out, d_state.astype(BF16), grads[:, : 3 * model], grads[:, 3 * model :])


def solution(mesh):
    placed = (P("lev", "tile", None, None), P(), P(), P("lev", "tile", None, None), P(), P())
    return jax.shard_map(
        local,
        mesh=mesh,
        in_specs=placed,
        out_specs=(
            P("lev", "tile", None, None),
            P("lev", "tile", None, None),
            P(("tile", "lev"), None),
            P(("tile", "lev"), None),
        ),
        check_vma=False,
    )
```

time: 410 us -> 85.2 us (0.21)
  waiting for transfers between devices: 207 us -> 29.8 us
  local copies, waits for them, and re-layouts: 79.8 us -> 7.43 us
  matrix products: 67.5 us -> 0 us
  Pallas kernels: 0 us -> 20.9 us
  between operations: 14.6 us -> 0.77 us
  other arithmetic: 17.2 us -> 5.78 us
    unnamed x3 -> x0, waiting for transfers between devices: 104 us -> none
    reduce_scatter x1 -> x0, waiting for transfers between devices: 94.8 us -> none  [local(): lax.psum_scatter(jnp.dot(piece.T, cot_flat, preferred_element_type=jnp.fl...]
    dot_general x16 -> x0, matrix products: 59.4 us -> none  [the longest x2 16.6 us: attend(): jnp.einsum('hqk,qhe->khe', ds16, queries, preferred_element_type=jnp.floa...]
    reshape x18 -> x0, local copies, waits for them, and re-layouts: 27.2 us -> none  [the longest x4 10.6 us: tile_step(): values = slab[..., model:].reshape(-1, heads, head)]
    ppermute x8 -> x14, waiting for transfers between devices: 8.21 us -> 29.8 us  [the longest x7 16.7 us: scatter_stage(): lax.ppermute(piece, axis, [(i, i ^ k * stride) for i in range(count)])]
    pallas_call x0 -> x1, Pallas kernels: none -> 20.9 us  [local(): pl.pallas_call(lambda *refs: kernel(with_odd, tiles, levs, *refs), out_sh...]
    concatenate x5 -> x0, local copies, waits for them, and re-layouts: 17.5 us -> none  [attend(): jnp.concatenate([dk.reshape(-1, model), dv.reshape(-1, model)], axis=-1)]
    transpose x4 -> x0, local copies, waits for them, and re-layouts: 15.2 us -> none  [the longest x2 7.6 us: attend(): jnp.einsum('hqk,qhe->khe', prob16, upstream, preferred_element_type=jnp.f...]
  transfers between devices with their start and end apart: 10 -> 14, of which waited for: 4 -> 9; matrix products, arithmetic and copies ran while one was open for 13% -> 8% of each run, Pallas kernels for 0% -> 0%
where the time goes in v1:
time: 85.2 us; the launch traced here: 85 us
  waiting for transfers between devices  29.8 us (35%)
  Pallas kernels  20.9 us (25%)
  starting transfers between devices  20.3 us (24%)
  local copies, waits for them, and re-layouts  7.43 us (9%)
  other arithmetic  5.78 us (7%)
    pallas_call x1, Pallas kernels, local(): pl.pallas_call(lambda *refs: kernel(with_odd, tiles, levs, *refs), out_sh...  20.9 us
    ppermute x7, waiting for transfers between devices, scatter_stage(): lax.ppermute(piece, axis, [(i, i ^ k * stride) for i in range(count)])  16.7 us
    ppermute x7, waiting for transfers between devices, swap(): return lax.ppermute(block, axis, swap_pairs(lax.axis_size(axis), first))  13.1 us
    ppermute x7, starting transfers between devices, swap(): return lax.ppermute(block, axis, swap_pairs(lax.axis_size(axis), first))  10.4 us
    ppermute x7, starting transfers between devices, scatter_stage(): lax.ppermute(piece, axis, [(i, i ^ k * stride) for i in range(count)])  9.86 us
    convert_element_type x3, local copies, waits for them, and re-layouts, scatter_stage(): piece = pick(x, jnp.bitwise_xor(digit, k), dim).astype(BF16)  2.78 us
    add x3, other arithmetic, scatter_stage(): total = total + part.astype(F32)  2.76 us
  transfers between devices with their start and end apart: 14, of which 9 were waited for; matrix products, arithmetic and copies ran while one was open for 8% of the time, Pallas kernels for 0%

profile of v1, /device:TPU:0, one launch (start us, length us, event | category | flops | bytes accessed | tf_op | source)
XLA Modules:
  0.0 85.0 jit_solution(8748018439892861364)
XLA Ops:
  0.6 1.1 %constant_dynamic-slice_fusion.4 = (bf16[2,3,32,512]{3,2,1,0:T(8,128)(2,1)S(1)}, bf16[2,3,32,512]{3,2,1,0:T(8,128)(2,1)S(1)}) fusion(bf16[2,4,32,512]{3,2,1,0:T(8,128)(2,1)} %refs_2_.1, s32[]{:T(128)S(6)} %select_n.92, s32[]{:T(128)S(6)} %select_n.91), kind=kLoop, calls=%fused_computation.51 | loop fusion | bytes 786440 | tf_op jit(solution)/shard_map/dynamic_slice | solution.py:241
  1.7 0.7 collective-permute-start.1
  2.4 5.7 %collective-permute-start = (bf16[2,3,32,512]{3,2,1,0:T(8,128)(2,1)S(1)}, bf16[2,3,32,512]{3,2,1,0:T(8,128)(2,1)S(1)}, u32[]{:S(2)}, u32[]{:S(2)}) collective-permute-start(bf16[2,3,32,512]{3,2,1,0:T(8,128)(2,1)S(1)} %get-tuple-element.25), channel_id=1, source_target_pairs={{0,2},{2,0},{4,6},{6,4},{8,10},{10,8},{12,14},{14,12},{16,18},{18,... | collective-permute-start | bytes 589832 | tf_op jit(solution)/shard_map/ppermute | solution.py:237
  8.1 0.0 collective-permute-done.1.refs_4_
  8.1 8.7 %collective-permute-done.refs_3_ = bf16[2,3,32,512]{3,2,1,0:T(8,128)(2,1)S(1)} collective-permute-done((bf16[2,3,32,512]{3,2,1,0:T(8,128)(2,1)S(1)}, bf16[2,3,32,512]{3,2,1,0:T(8,128)(2,1)S(1)}, u32[]{:S(2)}, u32[]{:S(2)}) %collective-permute-start) | collective-permute-done | bytes 196640 | tf_op jit(solution)/shard_map/ppermute | solution.py:237
  16.9 0.1 collective-permute-start.3
  17.0 0.9 %dynamic-slice_bitcast_fusion.1 = bf16[4,32,512]{2,1,0:T(8,128)(2,1)S(1)} fusion(bf16[2,4,32,512]{3,2,1,0:T(8,128)(2,1)} %refs_2_.1, s32[]{:T(128)S(6)} %select_n.93), kind=kLoop, calls=%fused_computation.43 | loop fusion | bytes 262148 | tf_op jit(solution)/shard_map/jit(dynamic_index_in_dim)/squeeze | solution.py:183
  17.9 0.6 collective-permute-start.2
  18.5 1.0 %collective-permute-done.2.refs_5_ = bf16[4,32,512]{2,1,0:T(8,128)(2,1)S(1)} collective-permute-done((bf16[4,32,512]{2,1,0:T(8,128)(2,1)S(1)}, bf16[4,32,512]{2,1,0:T(8,128)(2,1)S(1)}, u32[]{:S(2)}, u32[]{:S(2)}) %collective-permute-start.2) | collective-permute-done | bytes 131104 | tf_op jit(solution)/shard_map/ppermute | solution.py:237
  19.5 0.0 collective-permute-done.3.refs_6_
  19.5 0.0 copy-done.3
  19.5 0.0 copy-done.4
  19.5 0.6 copy-done.6
  20.1 0.7 copy-done.5
  20.8 20.9 %shard_map.93 = (bf16[2,4,32,512]{3,2,1,0:T(8,128)(2,1)}, f32[2,4,32,512]{3,2,1,0:T(8,128)}, bf16[4,10,32,512]{3,2,1,0:T(8,128)(2,1)}, f32[512,2048]{1,0:T(8,128)}) custom-call(s32[16]{0:T(128)} %refs_0_.1, s32[16]{0:T(128)} %refs_1_.1, bf16[2,4,32,512]{3,2,1,0:T(8,128)(2,1)} %refs_2_.1, bf16[2,3,32,512]{3,2,1,0:T(8,128)(2,1)} %copy-done.4, ...), custom_call_target="tpu_custom_call" | custom-call | tf_op jit(solution)/shard_map/pallas_call | solution.py:259
  41.7 1.8 %fusion = bf16[4,4,16,2048]{3,2,0,1:T(8,128)(2,1)S(1)} fusion(f32[4,4,2,16,2048]{4,3,2,1,0:T(8,128)} %bitcast.37, s32[]{:T(128)S(6)} %select_n.105), kind=kLoop, calls=%fused_computation.8 | loop fusion | bytes 2097156 | tf_op jit(solution)/shard_map/convert_element_type | solution.py:195
  43.5 0.4 collective-permute-start.7
  44.0 0.0 copy-done.1
  44.0 0.2 collective-permute-start.4
  44.3 2.5 %collective-permute-done.4 = bf16[10,32,512]{2,1,0:T(8,128)(2,1)S(1)} collective-permute-done((bf16[10,32,512]{2,1,0:T(8,128)(2,1)S(1)}, bf16[10,32,512]{2,1,0:T(8,128)(2,1)S(1)}, u32[]{:S(2)}, u32[]{:S(2)}) %collective-permute-start.4) | collective-permute-done | bytes 327712 | tf_op jit(solution)/shard_map/ppermute | solution.py:237
  46.7 0.2 fusion.2
  46.9 0.9 %fusion.15 = (bf16[2,3,32,512]{3,2,1,0:T(8,128)(2,1)}, bf16[2,3,32,512]{3,2,1,0:T(8,128)(2,1)}) fusion(s32[]{:T(128)S(6)} %select_n.100, f32[1,10,32,512]{3,2,1,0:T(8,128)S(1)} %get-tuple-element.23, f32[1,10,32,512]{3,2,1,0:T(8,128)S(1)} %get-tuple-element.22, bf16[2,10,32,512]{3,2,1,0:T(8,128)(2,1)S(1)} %slice.14, s32[]{:T(128)S(6)} %select_n.101), kind=kLoop, calls=%fused_computation.31 | loop fusion | flops 786432 | bytes 2097160 | tf_op jit(solution)/shard_map/convert_element_type | solution.py:298
  47.8 1.8 %collective-permute-start.5 = (bf16[2,3,32,512]{3,2,1,0:T(8,128)(2,1)}, bf16[2,3,32,512]{3,2,1,0:T(8,128)(2,1)}, u32[]{:S(2)}, u32[]{:S(2)}) collective-permute-start(bf16[2,3,32,512]{3,2,1,0:T(8,128)(2,1)} %get-tuple-element.15), channel_id=1, source_target_pairs={{0,2},{2,0},{4,6},{6,4},{8,10},{10,8},{12,14},{14,12},{16,18},{18,... | collective-permute-start | bytes 589832 | tf_op jit(solution)/shard_map/ppermute | solution.py:237
  49.6 1.3 %collective-permute-start.6 = (bf16[2,3,32,512]{3,2,1,0:T(8,128)(2,1)}, bf16[2,3,32,512]{3,2,1,0:T(8,128)(2,1)}, u32[]{:S(2)}, u32[]{:S(2)}) collective-permute-start(bf16[2,3,32,512]{3,2,1,0:T(8,128)(2,1)} %get-tuple-element.16), channel_id=1, source_target_pairs={{2,4},{4,2},{6,8},{8,6},{10,12},{12,10},{14,16},{16,14},{18,20},{2... | collective-permute-start | bytes 589832 | tf_op jit(solution)/shard_map/ppermute | solution.py:237
  51.0 0.0 collective-permute-done.7
  51.0 0.0 copy-done
  51.0 1.5 %bitcast_add_fusion = f32[4,4,16,2048]{3,2,0,1:T(8,128)S(1)} fusion(bf16[4,4,16,2048]{3,2,0,1:T(8,128)(2,1)} %collective-permute-done.7, f32[4,4,2,16,2048]{4,3,2,1,0:T(8,128)S(1)} %bitcast.38, s32[]{:T(128)S(6)} %select_n.104), kind=kLoop, calls=%fused_computation.1 | loop fusion | flops 1048576 | bytes 5242884 | tf_op jit(solution)/shard_map/add | solution.py:198
  52.5 0.9 %fusion.16 = (bf16[4,16,2048]{2,1,0:T(8,128)(2,1)}, bf16[4,16,2048]{2,1,0:T(8,128)(2,1)}, bf16[4,16,2048]{2,1,0:T(8,128)(2,1)}) fusion(f32[4,4,16,2048]{3,2,0,1:T(8,128)S(1)} %bitcast_add_fusion, s32[]{:T(128)S(6)} %select_n.107, s32[]{:T(128)S(6)} %select_n.109, s32[]{:T(128)S(6)} %select_n.108), kind=kLoop, calls=%fused_computation.33 | loop fusion | bytes 1572876 | tf_op jit(solution)/shard_map/convert_element_type | solution.py:195
  53.4 2.2 %collective-permute-start.8 = (bf16[4,16,2048]{2,1,0:T(8,128)(2,1)}, bf16[4,16,2048]{2,1,0:T(8,128)(2,1)}, u32[]{:S(2)}, u32[]{:S(2)}) collective-permute-start(bf16[4,16,2048]{2,1,0:T(8,128)(2,1)} %get-tuple-element.12), channel_id=1, source_target_pairs={{0,2},{2,0},{4,6},{6,4},{8,10},{10,8},{12,14},{14,12},{16,18},{18,... | collective-permute-start | bytes 786440 | tf_op jit(solution)/shard_map/ppermute | solution.py:196
  55.6 2.3 %collective-permute-start.10 = (bf16[4,16,2048]{2,1,0:T(8,128)(2,1)}, bf16[4,16,2048]{2,1,0:T(8,128)(2,1)}, u32[]{:S(2)}, u32[]{:S(2)}) collective-permute-start(bf16[4,16,2048]{2,1,0:T(8,128)(2,1)} %get-tuple-element.13), channel_id=1, source_target_pairs={{0,6},{2,4},{4,2},{6,0},{8,14},{10,12},{12,10},{14,8},{16,22},{18,... | collective-permute-start | bytes 786440 | tf_op jit(solution)/shard_map/ppermute | solution.py:196
  57.9 0.6 collective-permute-start.9
  58.5 0.9 %collective-permute-done.5 = bf16[2,3,32,512]{3,2,1,0:T(8,128)(2,1)} collective-permute-done((bf16[2,3,32,512]{3,2,1,0:T(8,128)(2,1)}, bf16[2,3,32,512]{3,2,1,0:T(8,128)(2,1)}, u32[]{:S(2)}, u32[]{:S(2)}) %collective-permute-start.5) | collective-permute-done | bytes 196640 | tf_op jit(solution)/shard_map/ppermute | solution.py:237
  59.4 0.0 collective-permute-done.6
  59.4 1.1 %convert_select_fusion.3 = (f32[2,3,32,512]{3,2,1,0:T(8,128)S(1)}, f32[2,3,32,512]{3,2,1,0:T(8,128)S(1)}) fusion(bf16[2,3,32,512]{3,2,1,0:T(8,128)(2,1)} %collective-permute-done.6, bf16[2,3,32,512]{3,2,1,0:T(8,128)(2,1)} %collective-permute-done.5, pred[]{:T(512)S(6)} %eq.8), kind=kLoop, calls=%fused_computation.25 | loop fusion | flops 393216 | bytes 1179649 | tf_op jit(solution)/shard_map/jit(_where)/select_n | solution.py:302
  60.5 5.1 %collective-permute-done.8 = bf16[4,16,2048]{2,1,0:T(8,128)(2,1)} collective-permute-done((bf16[4,16,2048]{2,1,0:T(8,128)(2,1)}, bf16[4,16,2048]{2,1,0:T(8,128)(2,1)}, u32[]{:S(2)}, u32[]{:S(2)}) %collective-permute-start.8) | collective-permute-done | bytes 262176 | tf_op jit(solution)/shard_map/ppermute | solution.py:196
  65.6 4.6 %collective-permute-done.10 = bf16[4,16,2048]{2,1,0:T(8,128)(2,1)} collective-permute-done((bf16[4,16,2048]{2,1,0:T(8,128)(2,1)}, bf16[4,16,2048]{2,1,0:T(8,128)(2,1)}, u32[]{:S(2)}, u32[]{:S(2)}) %collective-permute-start.10) | collective-permute-done | bytes 262176 | tf_op jit(solution)/shard_map/ppermute | solution.py:196
  70.2 1.4 %collective-permute-done.9 = bf16[4,16,2048]{2,1,0:T(8,128)(2,1)} collective-permute-done((bf16[4,16,2048]{2,1,0:T(8,128)(2,1)}, bf16[4,16,2048]{2,1,0:T(8,128)(2,1)}, u32[]{:S(2)}, u32[]{:S(2)}) %collective-permute-start.9) | collective-permute-done | bytes 262176 | tf_op jit(solution)/shard_map/ppermute | solution.py:196
  71.6 1.2 %fusion.9 = f32[4,16,2048]{2,1,0:T(8,128)S(1)} fusion(bf16[4,16,2048]{2,1,0:T(8,128)(2,1)} %collective-permute-done.10, bf16[4,16,2048]{2,1,0:T(8,128)(2,1)} %collective-permute-done.9, bf16[4,16,2048]{2,1,0:T(8,128)(2,1)} %collective-permute-done.8, f32[4,4,16,2048]{3,2,0,1:T(8,128)S(1)} %bitcast_add_fusion, s32[]{:T(128)S(6)} %select_n.106), kind=kLoop, calls=%fused_computation.20 | loop fusion | flops 786432 | bytes 1835012 | tf_op jit(solution)/shard_map/add | solution.py:198
  72.8 1.9 %collective-permute-start.11 = (bf16[16,2048]{1,0:T(8,128)(2,1)S(1)}, bf16[16,2048]{1,0:T(8,128)(2,1)S(1)}, u32[]{:S(2)}, u32[]{:S(2)}) collective-permute-start(bf16[16,2048]{1,0:T(8,128)(2,1)S(1)} %get-tuple-element.17), channel_id=1, source_target_pairs={{0,8},{2,10},{4,12},{6,14},{8,0},{10,2},{12,4},{14,6},{16,24},{18,... | collective-permute-start | bytes 196616 | tf_op jit(solution)/shard_map/ppermute | solution.py:196
  74.7 2.5 %collective-permute-start.13 = (bf16[16,2048]{1,0:T(8,128)(2,1)S(1)}, bf16[16,2048]{1,0:T(8,128)(2,1)S(1)}, u32[]{:S(2)}, u32[]{:S(2)}) collective-permute-start(bf16[16,2048]{1,0:T(8,128)(2,1)S(1)} %get-tuple-element.18), channel_id=1, source_target_pairs={{0,24},{2,26},{4,28},{6,30},{8,16},{10,18},{12,20},{14,22},{16,8},... | collective-permute-start | bytes 196616 | tf_op jit(solution)/shard_map/ppermute | solution.py:196
  77.2 0.0 collective-permute-start.12
  77.2 0.0 copy-done.2
  77.2 0.8 fusion.7
  78.1 0.0 collective-permute-done.11
  78.1 3.6 %collective-permute-done.13 = bf16[16,2048]{1,0:T(8,128)(2,1)S(1)} collective-permute-done((bf16[16,2048]{1,0:T(8,128)(2,1)S(1)}, bf16[16,2048]{1,0:T(8,128)(2,1)S(1)}, u32[]{:S(2)}, u32[]{:S(2)}) %collective-permute-start.13) | collective-permute-done | bytes 65568 | tf_op jit(solution)/shard_map/ppermute | solution.py:196
  81.6 2.0 %collective-permute-done.12 = bf16[16,2048]{1,0:T(8,128)(2,1)S(1)} collective-permute-done((bf16[16,2048]{1,0:T(8,128)(2,1)S(1)}, bf16[16,2048]{1,0:T(8,128)(2,1)S(1)}, u32[]{:S(2)}, u32[]{:S(2)}) %collective-permute-start.12) | collective-permute-done | bytes 65568 | tf_op jit(solution)/shard_map/ppermute | solution.py:196
  83.7 0.6 slice.20
  84.3 0.6 slice.19
  (14 shorter events, 0.2 us)
Async XLA Ops:
  1.7 6.4 %collective-permute-start.1 = (bf16[2,3,32,512]{3,2,1,0:T(8,128)(2,1)S(1)}, bf16[2,3,32,512]{3,2,1,0:T(8,128)(2,1)S(1)}, u32[]{:S(2)}, u32[]{:S(2)}) collective-permute-start(bf16[2,3,32,512]{3,2,1,0:T(8,128)(2,1)S(1)} %get-tuple-element.24), channel_id=1, source_target_pairs={{2,4},{4,2},{6,8},{8,6},{10,12},{12,10},{14,16},{16,14},{18,20},{2... | collective-permute-start | bytes 589832 | tf_op jit(solution)/shard_map/ppermute | solution.py:237
  2.4 14.5 %collective-permute-start = (bf16[2,3,32,512]{3,2,1,0:T(8,128)(2,1)S(1)}, bf16[2,3,32,512]{3,2,1,0:T(8,128)(2,1)S(1)}, u32[]{:S(2)}, u32[]{:S(2)}) collective-permute-start(bf16[2,3,32,512]{3,2,1,0:T(8,128)(2,1)S(1)} %get-tuple-element.25), channel_id=1, source_target_pairs={{0,2},{2,0},{4,6},{6,4},{8,10},{10,8},{12,14},{14,12},{16,18},{18,... | collective-permute-start | bytes 589832 | tf_op jit(solution)/shard_map/ppermute | solution.py:237
  8.1 11.3 %copy-start.3 = (bf16[2,3,32,512]{3,2,1,0:T(8,128)(2,1)}, bf16[2,3,32,512]{3,2,1,0:T(8,128)(2,1)S(1)}, u32[]{:S(2)}) copy-start(bf16[2,3,32,512]{3,2,1,0:T(8,128)(2,1)S(1)} %collective-permute-done.1.refs_4_) | copy-start | bytes 589828
  16.9 2.6 %copy-start.4 = (bf16[2,3,32,512]{3,2,1,0:T(8,128)(2,1)}, bf16[2,3,32,512]{3,2,1,0:T(8,128)(2,1)S(1)}, u32[]{:S(2)}) copy-start(bf16[2,3,32,512]{3,2,1,0:T(8,128)(2,1)S(1)} %collective-permute-done.refs_3_) | copy-start | bytes 589828
  16.9 2.5 %collective-permute-start.3 = (bf16[2,3,32,512]{3,2,1,0:T(8,128)(2,1)S(1)}, bf16[2,3,32,512]{3,2,1,0:T(8,128)(2,1)S(1)}, u32[]{:S(2)}, u32[]{:S(2)}) collective-permute-start(bf16[2,3,32,512]{3,2,1,0:T(8,128)(2,1)S(1)} %pad_maximum_fusion), channel_id=1, source_target_pairs={{0,1},{1,0},{2,3},{3,2},{4,5},{5,4},{6,7},{7,6},{8,9},{9,8},{10,11... | collective-permute-start | bytes 589832 | tf_op jit(solution)/shard_map/ppermute | solution.py:237
  17.9 1.5 %collective-permute-start.2 = (bf16[4,32,512]{2,1,0:T(8,128)(2,1)S(1)}, bf16[4,32,512]{2,1,0:T(8,128)(2,1)S(1)}, u32[]{:S(2)}, u32[]{:S(2)}) collective-permute-start(bf16[4,32,512]{2,1,0:T(8,128)(2,1)S(1)} %dynamic-slice_bitcast_fusion.1), channel_id=1, source_target_pairs={{0,1},{1,0},{2,3},{3,2},{4,5},{5,4},{6,7},{7,6},{8,9},{9,8},{10,11... | collective-permute-start | bytes 393224 | tf_op jit(solution)/shard_map/ppermute | solution.py:237
  19.4 0.7 copy-start.6
  20.1 0.7 copy-start.5
  41.7 2.3 %copy-start.1 = (bf16[4,10,32,512]{3,2,1,0:T(8,128)(2,1)S(1)}, bf16[4,10,32,512]{3,2,1,0:T(8,128)(2,1)}, u32[]{:S(2)}) copy-start(bf16[4,10,32,512]{3,2,1,0:T(8,128)(2,1)} %get-tuple-element.10) | copy-start | bytes 3932164
  43.5 7.4 %collective-permute-start.7 = (bf16[4,4,16,2048]{3,2,0,1:T(8,128)(2,1)S(1)}, bf16[4,4,16,2048]{3,2,0,1:T(8,128)(2,1)}, u32[]{:S(2)}, u32[]{:S(2)}) collective-permute-start(bf16[4,4,16,2048]{3,2,0,1:T(8,128)(2,1)S(1)} %fusion), channel_id=1, source_target_pairs={{0,1},{1,0},{2,3},{3,2},{4,5},{5,4},{6,7},{7,6},{8,9},{9,8},{10,11... | collective-permute-start | bytes 3145736 | tf_op jit(solution)/shard_map/ppermute | solution.py:196
  44.0 2.8 %collective-permute-start.4 = (bf16[10,32,512]{2,1,0:T(8,128)(2,1)S(1)}, bf16[10,32,512]{2,1,0:T(8,128)(2,1)S(1)}, u32[]{:S(2)}, u32[]{:S(2)}) collective-permute-start(bf16[10,32,512]{2,1,0:T(8,128)(2,1)S(1)} %dynamic-slice_bitcast_fusion), channel_id=1, source_target_pairs={{0,1},{1,0},{2,3},{3,2},{4,5},{5,4},{6,7},{7,6},{8,9},{9,8},{10,11... | collective-permute-start | bytes 983048 | tf_op jit(solution)/shard_map/ppermute | solution.py:237
  44.2 6.8 %copy-start = (f32[512,2048]{1,0:T(8,128)S(1)}, f32[512,2048]{1,0:T(8,128)}, u32[]{:S(2)}) copy-start(f32[512,2048]{1,0:T(8,128)} %get-tuple-element.11) | copy-start | bytes 12582916
  47.8 11.6 %collective-permute-start.5 = (bf16[2,3,32,512]{3,2,1,0:T(8,128)(2,1)}, bf16[2,3,32,512]{3,2,1,0:T(8,128)(2,1)}, u32[]{:S(2)}, u32[]{:S(2)}) collective-permute-start(bf16[2,3,32,512]{3,2,1,0:T(8,128)(2,1)} %get-tuple-element.15), channel_id=1, source_target_pairs={{0,2},{2,0},{4,6},{6,4},{8,10},{10,8},{12,14},{14,12},{16,18},{18,... | collective-permute-start | bytes 589832 | tf_op jit(solution)/shard_map/ppermute | solution.py:237
  49.6 9.8 %collective-permute-start.6 = (bf16[2,3,32,512]{3,2,1,0:T(8,128)(2,1)}, bf16[2,3,32,512]{3,2,1,0:T(8,128)(2,1)}, u32[]{:S(2)}, u32[]{:S(2)}) collective-permute-start(bf16[2,3,32,512]{3,2,1,0:T(8,128)(2,1)} %get-tuple-element.16), channel_id=1, source_target_pairs={{2,4},{4,2},{6,8},{8,6},{10,12},{12,10},{14,16},{16,14},{18,20},{2... | collective-permute-start | bytes 589832 | tf_op jit(solution)/shard_map/ppermute | solution.py:237
  53.4 12.2 %collective-permute-start.8 = (bf16[4,16,2048]{2,1,0:T(8,128)(2,1)}, bf16[4,16,2048]{2,1,0:T(8,128)(2,1)}, u32[]{:S(2)}, u32[]{:S(2)}) collective-permute-start(bf16[4,16,2048]{2,1,0:T(8,128)(2,1)} %get-tuple-element.12), channel_id=1, source_target_pairs={{0,2},{2,0},{4,6},{6,4},{8,10},{10,8},{12,14},{14,12},{16,18},{18,... | collective-permute-start | bytes 786440 | tf_op jit(solution)/shard_map/ppermute | solution.py:196
  55.6 14.6 %collective-permute-start.10 = (bf16[4,16,2048]{2,1,0:T(8,128)(2,1)}, bf16[4,16,2048]{2,1,0:T(8,128)(2,1)}, u32[]{:S(2)}, u32[]{:S(2)}) collective-permute-start(bf16[4,16,2048]{2,1,0:T(8,128)(2,1)} %get-tuple-element.13), channel_id=1, source_target_pairs={{0,6},{2,4},{4,2},{6,0},{8,14},{10,12},{12,10},{14,8},{16,22},{18,... | collective-permute-start | bytes 786440 | tf_op jit(solution)/shard_map/ppermute | solution.py:196
  57.9 13.7 %collective-permute-start.9 = (bf16[4,16,2048]{2,1,0:T(8,128)(2,1)}, bf16[4,16,2048]{2,1,0:T(8,128)(2,1)}, u32[]{:S(2)}, u32[]{:S(2)}) collective-permute-start(bf16[4,16,2048]{2,1,0:T(8,128)(2,1)} %get-tuple-element.14), channel_id=1, source_target_pairs={{0,4},{2,6},{4,0},{6,2},{8,12},{10,14},{12,8},{14,10},{16,20},{18,... | collective-permute-start | bytes 786440 | tf_op jit(solution)/shard_map/ppermute | solution.py:196
  58.5 18.7 %copy-start.2 = (f32[2,4,32,512]{3,2,1,0:T(8,128)S(1)}, f32[2,4,32,512]{3,2,1,0:T(8,128)}, u32[]{:S(2)}) copy-start(f32[2,4,32,512]{3,2,1,0:T(8,128)} %get-tuple-element.9) | copy-start | bytes 1572868
  72.8 5.2 %collective-permute-start.11 = (bf16[16,2048]{1,0:T(8,128)(2,1)S(1)}, bf16[16,2048]{1,0:T(8,128)(2,1)S(1)}, u32[]{:S(2)}, u32[]{:S(2)}) collective-permute-start(bf16[16,2048]{1,0:T(8,128)(2,1)S(1)} %get-tuple-element.17), channel_id=1, source_target_pairs={{0,8},{2,10},{4,12},{6,14},{8,0},{10,2},{12,4},{14,6},{16,24},{18,... | collective-permute-start | bytes 196616 | tf_op jit(solution)/shard_map/ppermute | solution.py:196
  74.7 6.9 %collective-permute-start.13 = (bf16[16,2048]{1,0:T(8,128)(2,1)S(1)}, bf16[16,2048]{1,0:T(8,128)(2,1)S(1)}, u32[]{:S(2)}, u32[]{:S(2)}) collective-permute-start(bf16[16,2048]{1,0:T(8,128)(2,1)S(1)} %get-tuple-element.18), channel_id=1, source_target_pairs={{0,24},{2,26},{4,28},{6,30},{8,16},{10,18},{12,20},{14,22},{16,8},... | collective-permute-start | bytes 196616 | tf_op jit(solution)/shard_map/ppermute | solution.py:196
  77.2 6.5 %collective-permute-start.12 = (bf16[16,2048]{1,0:T(8,128)(2,1)S(1)}, bf16[16,2048]{1,0:T(8,128)(2,1)S(1)}, u32[]{:S(2)}, u32[]{:S(2)}) collective-permute-start(bf16[16,2048]{1,0:T(8,128)(2,1)S(1)} %get-tuple-element.19), channel_id=1, source_target_pairs={{0,16},{2,18},{4,20},{6,22},{8,24},{10,26},{12,28},{14,30},{16,0},... | collective-permute-start | bytes 196616 | tf_op jit(solution)/shard_map/ppermute | solution.py:196

commit v2 on v1

v2 whole, which is shorter than its diff:
```python
import jax
import jax.numpy as jnp
from jax import lax
from jax.experimental import pallas as pl
from jax.experimental.pallas import tpu as pltpu
from jax.sharding import PartitionSpec as P

HEADS = 8
BROWS = 4
REACH = 3
GROUP = 4
PAIR = 2
LOW = -1e30
F32 = jnp.float32
BF16 = jnp.bfloat16
SMEM = pl.BlockSpec(memory_space=pltpu.SMEM)
VMEM = pl.BlockSpec(memory_space=pltpu.VMEM)


def dot(a, b, ca, cb):
    return lax.dot_general(a, b, (((ca,), (cb,)), ((), ())), preferred_element_type=F32)


def swap_pairs(count, first):
    route = []
    for i in range(first, count - 1, 2):
        route += [(i, i + 1), (i + 1, i)]
    return route


def call(body, name, outs, ins, scratch=(), mib=8, cost=10**6):
    return pl.pallas_call(
        body,
        name=name,
        out_shape=[jax.ShapeDtypeStruct(shape, kind) for shape, kind in outs],
        in_specs=[SMEM if x.dtype == jnp.int32 else VMEM for x in ins],
        out_specs=[VMEM] * len(outs),
        scratch_shapes=list(scratch),
        compiler_params=pltpu.CompilerParams(vmem_limit_bytes=mib * 2**20),
        cost_estimate=pl.CostEstimate(flops=cost, bytes_accessed=2**20, transcendentals=0),
    )(*ins)


class Plan:
    def __init__(self, shape, tiles, levs):
        self.levels_n, self.height, self.width, self.model = shape
        self.tiles, self.levs = tiles, levs
        self.tall = self.height + 2 * REACH
        self.compact = levs == 2 and self.levels_n == 2
        self.slots_n = self.levels_n + 2 - self.compact
        self.own = (self.levels_n, self.height, self.width)
        self.wide = (self.slots_n, self.tall, self.width)
        self.edge = (self.levels_n, REACH, self.width, self.model)

    def places(self):
        tile_odd = lax.rem(lax.axis_index("tile"), 2)
        lev_odd = lax.rem(lax.axis_index("lev"), 2)
        end = self.height + REACH
        self.even = tile_odd == 0
        self.at_e = jnp.where(tile_odd == 0, end, 0)
        self.at_o = jnp.where(tile_odd == 0, 0, end)
        self.off = 1 - lev_odd if self.compact else 0
        last = self.levels_n + 1
        self.slot_e = jnp.where(lev_odd == 0, last, 0) - self.off
        self.slot_o = jnp.where(lev_odd == 0, 0, last)
        self.first = 1 - self.off
        self.edge_e = jnp.where(lev_odd == 0, self.levels_n - 1, 0)
        self.edge_o = jnp.where(lev_odd == 0, 0, self.levels_n - 1)

    def liveness(self, ocean, depth, live):
        tile = lax.axis_index("tile")
        lev = lax.axis_index("lev")
        total_rows = self.height * self.tiles
        total_levels = self.levels_n * self.levs
        for r in range(self.tall):
            row = tile * self.height - REACH + r
            block_at = lax.div(jnp.clip(row, 0, total_rows - 1), BROWS)
            good = (row >= 0) & (row < total_rows) & (ocean[block_at] == 1)
            deep = depth[block_at]
            for l in range(self.levels_n + 2):
                at = lev * self.levels_n - 1 + l
                ok = good & (at >= 0) & (at < total_levels) & (at < deep)
                live[l * self.tall + r] = ok.astype(jnp.int32)

    def alive(self, live, level, row):
        return live[level * self.tall + row]


def stage_own(plan, ocean, depth, state, w_qkv, w_out, cot, *refs):
    near, (qs, us, mid, live) = refs[:-4], refs[-4:]
    height, width, model = plan.own[1:] + (plan.model,)
    cells = height * width
    head = model // HEADS
    plan.places()
    plan.liveness(ocean, depth, live)

    def pairs(x):
        y = dot(x.reshape(cells, model), w_qkv[:, model:], 1, 0).astype(BF16)
        return y.reshape(height, width, 2 * model)

    for l in range(plan.levels_n):
        mid[plan.first + l] = pairs(state[l])
        flat = state[l].reshape(cells, model)
        q = dot(flat, w_qkv[:, :model], 1, 0).astype(BF16) * jnp.asarray(head**-0.5, BF16)
        qs[l] = q.reshape(height, width, model)
        u = dot(cot[l].reshape(cells, model), w_out[...], 1, 1).astype(BF16)
        u = u.reshape(height, width, model)
        for r in range(height):
            us[l, r] = u[r] * plan.alive(live, l + 1, REACH + r).astype(F32).astype(BF16)
    mid[plan.slot_e] = pairs(near[0][plan.edge_o])
    if not plan.compact:
        mid[plan.slot_o] = pairs(near[1][plan.edge_e])


def stage_attend(plan, sums_n, ocean, depth, state, rows_e, rows_o, qs, us, mid, w_qkv, cot, *refs):
    sides = 1 if plan.compact else 2
    lev_in, refs = refs[: 3 * sides], refs[3 * sides :]
    attn, dq, dkv16 = refs[:3]
    sums, (ext, kv, dkv, bias, live) = refs[3 : 3 + sums_n], refs[3 + sums_n :]
    levels_n, height, width = plan.own
    model, tall = plan.model, plan.tall
    span = PAIR + 2 * REACH
    block = PAIR * width
    head = model // HEADS
    lanes_n = GROUP * head
    plan.places()
    plan.liveness(ocean, depth, live)

    inner = pl.ds(plan.first, levels_n)
    ext[inner, REACH : height + REACH] = state[...]
    ext[inner, pl.ds(plan.at_e, REACH)] = rows_e[...]
    ext[inner, pl.ds(plan.at_o, REACH)] = rows_o[...]
    for side, (slot, level) in enumerate(((plan.slot_e, plan.edge_o), (plan.slot_o, plan.edge_e))):
        if side < sides:
            near, far_e, far_o = lev_in[3 * side : 3 * side + 3]
            ext[slot, REACH : height + REACH] = near[level]
            ext[slot, pl.ds(plan.at_e, REACH)] = far_e[level]
            ext[slot, pl.ds(plan.at_o, REACH)] = far_o[level]

    @pl.loop(0, plan.slots_n)
    def _(l):
        edge = REACH * width
        cells = [ext[l, :REACH].reshape(edge, model), ext[l, height + REACH :].reshape(edge, model)]
        pairs = dot(jnp.concatenate(cells, axis=0), w_qkv[:, model:], 1, 0).astype(BF16)
        kv[l, :REACH] = pairs[:edge].reshape(REACH, width, 2 * model)
        kv[l, height + REACH :] = pairs[edge:].reshape(REACH, width, 2 * model)
        kv[l, REACH : height + REACH] = mid[l]
        dkv[l] = jnp.zeros((tall, width, 2 * model), F32)

    lane_head = lax.broadcasted_iota(jnp.int32, (block, lanes_n), 1) // head
    query = lax.broadcasted_iota(jnp.int32, (width, GROUP * block), 1) % block
    query_row = query // width
    query_col = query % width
    key_col = lax.broadcasted_iota(jnp.int32, (width, GROUP * block), 0)
    near_col = jnp.abs(key_col - query_col) <= REACH

    def spread(x):
        return jnp.concatenate(
            [jnp.where(lane_head == h, x, jnp.zeros_like(x)) for h in range(GROUP)], axis=0
        )

    def gather(x):
        total = jnp.where(lane_head == 0, x[:block], 0.0)
        for h in range(1, GROUP):
            total = jnp.where(lane_head == h, x[h * block : (h + 1) * block], total)
        return total

    def tile_step(l, r0, depth_n, base, base_level):
        keys_n = depth_n * span * width
        for dl in range(depth_n):
            for kr in range(span):
                alive = plan.alive(live, base_level + dl, r0 + kr) == 1
                near = near_col & (jnp.abs(query_row + REACH - kr) <= REACH)
                at = (dl * span + kr) * width
                bias[at : at + width] = jnp.where(near & alive, 0.0, LOW)
        for g in range(HEADS // GROUP):
            lanes = slice(g * lanes_n, (g + 1) * lanes_n)
            lanes_v = slice(model + g * lanes_n, model + (g + 1) * lanes_n)
            q = spread(qs[l, pl.ds(r0, PAIR), :, lanes].reshape(block, lanes_n))
            u = spread(us[l, pl.ds(r0, PAIR), :, lanes].reshape(block, lanes_n))
            k = kv[pl.ds(base, depth_n), pl.ds(r0, span), :, lanes].reshape(keys_n, lanes_n)
            v = kv[pl.ds(base, depth_n), pl.ds(r0, span), :, lanes_v].reshape(keys_n, lanes_n)
            s = dot(k, q, 1, 1) + bias[:keys_n]
            e = jnp.exp(s - jnp.max(s, axis=0, keepdims=True))
            p = e * (1.0 / jnp.sum(e, axis=0, keepdims=True))
            p16 = p.astype(BF16)
            dp = dot(v, u, 1, 1)
            ds = p * (dp - jnp.sum(p * dp, axis=0, keepdims=True))
            ds16 = ds.astype(BF16)
            a = gather(dot(p16, v, 0, 0))
            for r in range(PAIR):
                alive = plan.alive(live, l + 1, REACH + r0 + r).astype(F32)
                attn[l, r0 + r, :, lanes] = (a[r * width : (r + 1) * width] * alive).astype(BF16)
            b = gather(dot(ds16, k, 0, 0)) * (head**-0.5)
            dq[l, pl.ds(r0, PAIR), :, lanes] = b.astype(BF16).reshape(PAIR, width, lanes_n)
            dk = dot(ds16, q, 1, 0).reshape(depth_n, span, width, lanes_n)
            dkv[pl.ds(base, depth_n), pl.ds(r0, span), :, lanes] += dk
            dv = dot(p16, u, 1, 0).reshape(depth_n, span, width, lanes_n)
            dkv[pl.ds(base, depth_n), pl.ds(r0, span), :, lanes_v] += dv

    pairs_n = height // PAIR
    if plan.compact:

        @pl.loop(0, pairs_n)
        def _(pair):
            tile_step(plan.edge_e, pair * PAIR, 3, 0, plan.off)
            tile_step(plan.edge_o, pair * PAIR, 2, plan.first, 1)

    else:

        @pl.loop(0, levels_n * pairs_n)
        def _(combo):
            l = combo // pairs_n
            tile_step(l, (combo % pairs_n) * PAIR, 3, l, l)

    @pl.loop(0, plan.slots_n)
    def _(l):
        dkv16[l] = dkv[l].astype(BF16)

    cells = levels_n * height * width
    wide = plan.slots_n * tall * width

    def emit(at, x):
        n = x.shape[1]
        if sums_n == 1:
            sums[0][:, at : at + n] = x
            return
        keep, send = sums
        rows = model // (plan.tiles * plan.levs)
        x = x.reshape(plan.tiles, plan.levs, rows, n)
        mine = lax.axis_index("lev") == 0
        keep[:, :, at : at + n] = jnp.where(mine, x[:, 0], x[:, 1])
        send[:, :, at : at + n] = jnp.where(mine, x[:, 1], x[:, 0]).astype(BF16)

    emit(0, dot(state[...].reshape(cells, model), dq[...].reshape(cells, model), 0, 0))
    emit(3 * model, dot(attn[...].reshape(cells, model), cot[...].reshape(cells, model), 0, 0))
    for j in range(2):
        part = dkv16[:, :, :, j * model : (j + 1) * model].reshape(wide, model)
        emit((j + 1) * model, dot(ext[...].reshape(wide, model), part, 0, 0))


def stage_out(plan, state, cot, attn, dq, dkv16, w_qkv, w_out, out, own, rows_e, rows_o, *refs):
    edges, tmp = refs[:-1], refs[-1]
    levels_n, height, width = plan.own
    model, tall = plan.model, plan.tall
    cells = height * width
    plan.places()

    def back(slot):
        x = dot(dkv16[slot].reshape(tall * width, 2 * model), w_qkv[:, model:], 1, 1)
        return x.reshape(tall, width, model)

    for edge, slot in zip(edges, (plan.slot_e, plan.slot_o)):
        edge[...] = back(slot).astype(BF16)
    for l in range(levels_n):
        tmp[...] = back(plan.first + l)
        rows_e[l] = tmp[pl.ds(plan.at_e, REACH)]
        rows_o[l] = tmp[pl.ds(plan.at_o, REACH)]
        x = cot[l].reshape(cells, model).astype(F32)
        x = x + dot(dq[l].reshape(cells, model), w_qkv[:, :model], 1, 1)
        own[l] = x.reshape(height, width, model) + tmp[REACH : REACH + height]
        x = state[l].reshape(cells, model).astype(F32)
        x = x + dot(attn[l].reshape(cells, model), w_out[...], 1, 0)
        out[l] = x.astype(BF16).reshape(height, width, model)


def stage_fold(plan, rows_e, rows_o, *refs):
    edges, (send_e, send_o, acc) = refs[:-3], refs[-3:]
    plan.places()
    for rows, at, send in ((rows_e, plan.at_e, send_e), (rows_o, plan.at_o, send_o)):
        acc[...] = rows[...]
        for edge, level in zip(edges, (plan.edge_e, plan.edge_o)):
            acc[level] += edge[pl.ds(at, REACH)].astype(F32)
        send[...] = acc[...].astype(BF16)


def stage_last(plan, own, back_e, back_o, *refs):
    edges, (d_state, acc) = refs[:-2], refs[-2:]
    plan.places()
    height = plan.height
    acc[...] = own[...]
    for edge, level in zip(edges, (plan.edge_e, plan.edge_o)):
        acc[level] += edge[REACH : REACH + height].astype(F32)
    top = height - REACH
    acc[:, pl.ds(jnp.where(plan.even, top, 0), REACH)] += back_e[...].astype(F32)
    acc[:, pl.ds(jnp.where(plan.even, 0, top), REACH)] += back_o[...].astype(F32)
    d_state[...] = acc[...].astype(BF16)


def stage_split(parts_n, radix, stride, x, *refs):
    parts, (own, *pieces) = refs[:parts_n], refs[parts_n:]
    digit = lax.rem(lax.div(lax.axis_index("tile"), stride), radix)
    for h in range(x.shape[0] // radix):
        for k in range(radix):
            at = h * radix + jnp.bitwise_xor(digit, k)
            y = x[at]
            for part in parts:
                y = y + part[at].astype(F32)
            if k == 0:
                own[h] = y
            else:
                pieces[k - 1][h] = y.astype(BF16)


def stage_sum(parts_n, x, *refs):
    parts, (qkv, rest) = refs[:parts_n], refs[parts_n:]
    y = x[0]
    for part in parts:
        y = y + part[0].astype(F32)
    cut = qkv.shape[1]
    qkv[...] = y[:, :cut]
    rest[...] = y[:, cut:]


def digits(count):
    sizes = []
    while count > 1:
        radix = 4 if count % 4 == 0 else 2
        sizes.append(radix)
        count //= radix
    return sizes


def xor_route(count, step):
    return [(i, i ^ step) for i in range(count)]


def reduce_levels(x, tiles, levs):
    rows, cols = x.shape
    x = x.reshape([tiles] + digits(levs)[::-1] + [rows // (tiles * levs), cols])
    stride = 1
    for radix in digits(levs):
        dim = x.ndim - 3
        digit = lax.rem(lax.div(lax.axis_index("lev"), stride), radix)
        total = lax.dynamic_index_in_dim(x, digit, dim, keepdims=False)
        for k in range(1, radix):
            piece = lax.dynamic_index_in_dim(x, jnp.bitwise_xor(digit, k), dim, keepdims=False)
            piece = lax.ppermute(piece.astype(BF16), "lev", xor_route(levs, k * stride))
            total = total + piece.astype(F32)
        x = total
        stride *= radix
    return x


def local(state, w_qkv, w_out, cotangent, ocean, depth):
    tiles, levs = lax.axis_size("tile"), lax.axis_size("lev")
    plan = Plan(state.shape, tiles, levs)
    height, width, model = plan.height, plan.width, plan.model
    sides = 1 if plan.compact else 2

    def bind(body, *first):
        return lambda *refs: body(*first, *refs)

    def swap(block, axis, first):
        return lax.ppermute(block, axis, swap_pairs(lax.axis_size(axis), first))

    top = height - REACH
    even = lax.rem(lax.axis_index("tile"), 2) == 0
    rows_e = lax.dynamic_slice_in_dim(state, jnp.where(even, top, 0), REACH, 1)
    rows_o = lax.dynamic_slice_in_dim(state, jnp.where(even, 0, top), REACH, 1)
    near = [swap(state, "lev", side) for side in range(sides)]
    rows_e = swap(rows_e, "tile", 0)
    rows_o = swap(rows_o, "tile", 1)
    live = pltpu.SMEM(((plan.levels_n + 2) * plan.tall,), jnp.int32)
    own_cells = plan.own + (model,)
    qs, us, mid = call(
        bind(stage_own, plan),
        "stage_own",
        [(own_cells, BF16), (own_cells, BF16), ((plan.slots_n,) + plan.own[1:] + (2 * model,), BF16)],
        [ocean, depth, state, w_qkv, w_out, cotangent, *near],
        [live],
        cost=4 * 10**9,
    )
    rows_e, rows_o, qs = lax.optimization_barrier((rows_e, rows_o, qs))
    lev_in = []
    for side in range(sides):
        lev_in += [near[side], swap(rows_e, "lev", side), swap(rows_o, "lev", side)]
    rows = model // (tiles * levs)
    if levs == 2 and rows % 8 == 0:
        share = (tiles, rows, 4 * model)
        sums = [(share, F32), (share, BF16)]
    else:
        sums = [((model, 4 * model), F32)]
    keys_n = 3 * (PAIR + 2 * REACH) * width
    attn, dq, dkv16, *sums = call(
        bind(stage_attend, plan, len(sums)),
        "stage_attend",
        [(own_cells, BF16), (own_cells, BF16), (plan.wide + (2 * model,), BF16)] + sums,
        [ocean, depth, state, rows_e, rows_o, qs, us, mid, w_qkv, cotangent, *lev_in],
        [
            pltpu.VMEM(plan.wide + (model,), BF16),
            pltpu.VMEM(plan.wide + (2 * model,), BF16),
            pltpu.VMEM(plan.wide + (2 * model,), F32),
            pltpu.VMEM((keys_n, GROUP * PAIR * width), F32),
            live,
        ],
        mib=24,
        cost=16 * 10**9,
    )
    edge_kind = (plan.wide[1:] + (model,), BF16)
    out, own, part_e, part_o, *edges = call(
        bind(stage_out, plan),
        "stage_out",
        [(own_cells, BF16), (own_cells, F32), (plan.edge, F32), (plan.edge, F32)] + [edge_kind] * sides,
        [state, cotangent, attn, dq, dkv16, w_qkv, w_out],
        [pltpu.VMEM(plan.wide[1:] + (model,), F32)],
        cost=4 * 10**9,
    )
    edges = [swap(edge, "lev", side) for side, edge in enumerate(edges)]
    send_e, send_o = call(
        bind(stage_fold, plan),
        "stage_fold",
        [(plan.edge, BF16)] * 2,
        [part_e, part_o, *edges],
        [pltpu.VMEM(plan.edge, F32)],
    )

    if len(sums) == 2:
        x, parts = sums[0], [lax.ppermute(sums[1], "lev", swap_pairs(levs, 0))]
    else:
        x, parts = reduce_levels(sums[0], tiles, levs), []
    stride = 1
    for radix in digits(tiles):
        share = (x.shape[0] // radix,) + x.shape[1:]
        x, *pieces = call(
            bind(stage_split, len(parts), radix, stride),
            "stage_split",
            [(share, F32)] + [(share, BF16)] * (radix - 1),
            [x, *parts],
        )
        if stride > 1:
            send_e, send_o, *pieces = lax.optimization_barrier((send_e, send_o, *pieces))
        parts = [
            lax.ppermute(piece, "tile", xor_route(tiles, (k + 1) * stride))
            for k, piece in enumerate(pieces)
        ]
        stride *= radix
    d_qkv, d_out = call(
        bind(stage_sum, len(parts)),
        "stage_sum",
        [((rows, 3 * model), F32), ((rows, model), F32)],
        [x, *parts],
    )
    back_e = swap(send_e, "tile", 0)
    back_o = swap(send_o, "tile", 1)
    (d_state,) = call(
        bind(stage_last, plan),
        "stage_last",
        [(own_cells, BF16)],
        [own, back_e, back_o, *edges],
        [pltpu.VMEM(own_cells, F32)],
    )
    return (out, d_state, d_qkv, d_out)


def solution(mesh):
    placed = (P("lev", "tile", None, None), P(), P(), P("lev", "tile", None, None), P(), P())
    return jax.shard_map(
        local,
        mesh=mesh,
        in_specs=placed,
        out_specs=(
            P("lev", "tile", None, None),
            P("lev", "tile", None, None),
            P(("tile", "lev"), None),
            P(("tile", "lev"), None),
        ),
        check_vma=False,
    )
```

time: 85.2 us -> 67 us (0.79)
  waiting for transfers between devices: 29.8 us -> 22.7 us
  other arithmetic: 5.78 us -> 0 us
  Pallas kernels: 20.9 us -> 17.5 us
  starting transfers between devices: 20.3 us -> 19 us
    ppermute x7 -> x8, waiting for transfers between devices: 13.1 us -> 3.28 us  [swap(): return lax.ppermute(block, axis, swap_pairs(lax.axis_size(axis), first))]
    unnamed x14 -> x24, local copies, waits for them, and re-layouts: 1.33 us -> 5.69 us
    pallas_call x1 -> x8, Pallas kernels: 20.9 us -> 17.5 us  [call(): pl.pallas_call(body, name=name, out_shape=[jax.ShapeDtypeStruct(shape, ki...]
    ppermute x7, waiting for transfers between devices: 16.7 us -> 19.5 us  [the longest x6 19.5 us: local(): lax.ppermute(piece, 'tile', xor_route(tiles, (k + 1) * stride))]
    convert_element_type x3 -> x0, local copies, waits for them, and re-layouts: 2.78 us -> none  [scatter_stage(): piece = pick(x, jnp.bitwise_xor(digit, k), dim).astype(BF16)]
    add x3 -> x0, other arithmetic: 2.76 us -> none  [scatter_stage(): total = total + part.astype(F32)]
    ppermute x7 -> x8, starting transfers between devices: 10.4 us -> 8.38 us  [swap(): return lax.ppermute(block, axis, swap_pairs(lax.axis_size(axis), first))]
    convert_element_type x2 -> x0, other arithmetic: 1.73 us -> none  [the longest x1 0.88 us: halo(): return (mine + lax.dynamic_slice_in_dim(across, at, REACH, 1)).astype(BF16)]
  transfers between devices with their start and end apart: 14 -> 15, of which waited for: 9 -> 8; matrix products, arithmetic and copies ran while one was open for 8% -> 2% of each run, Pallas kernels for 0% -> 8%
where the time goes in v2:
time: 67 us; the launch traced here: 66.7 us
  waiting for transfers between devices  22.7 us (34%)
  starting transfers between devices  19 us (28%)
  Pallas kernels  17.5 us (26%)
  local copies, waits for them, and re-layouts  6.74 us (10%)
  between operations  0.75 us (1%)
    ppermute x6, waiting for transfers between devices, local(): lax.ppermute(piece, 'tile', xor_route(tiles, (k + 1) * stride))  19.5 us
    pallas_call x8, Pallas kernels, call(): pl.pallas_call(body, name=name, out_shape=[jax.ShapeDtypeStruct(shape, ki...  17.5 us
    ppermute x6, starting transfers between devices, local(): lax.ppermute(piece, 'tile', xor_route(tiles, (k + 1) * stride))  10.3 us
    ppermute x8, starting transfers between devices, swap(): return lax.ppermute(block, axis, swap_pairs(lax.axis_size(axis), first))  8.38 us
    unnamed x24, local copies, waits for them, and re-layouts  5.69 us
    ppermute x8, waiting for transfers between devices, swap(): return lax.ppermute(block, axis, swap_pairs(lax.axis_size(axis), first))  3.28 us
  transfers between devices with their start and end apart: 15, of which 8 were waited for; matrix products, arithmetic and copies ran while one was open for 2% of the time, Pallas kernels for 8%

profile of v2, /device:TPU:0, one launch (start us, length us, event | category | flops | bytes accessed | tf_op | source)
XLA Modules:
  0.0 66.7 jit_solution(7779498550072780976)
XLA Ops:
  0.6 0.5 collective-permute-start.2
  1.1 1.0 %constant_dynamic-slice_fusion = (bf16[2,3,32,512]{3,2,1,0:T(8,128)(2,1)S(1)}, bf16[2,3,32,512]{3,2,1,0:T(8,128)(2,1)S(1)}) fusion(bf16[2,4,32,512]{3,2,1,0:T(8,128)(2,1)} %refs_0_.5, s32[]{:T(128)S(6)} %select_n.10, s32[]{:T(128)S(6)} %select_n.9), kind=kLoop, calls=%fused_computation | loop fusion | bytes 786440 | tf_op jit(solution)/shard_map/dynamic_slice | solution.py:360
  2.2 0.7 %collective-permute-start.1 = (bf16[2,3,32,512]{3,2,1,0:T(8,128)(2,1)S(1)}, bf16[2,3,32,512]{3,2,1,0:T(8,128)(2,1)S(1)}, u32[]{:S(2)}, u32[]{:S(2)}) collective-permute-start(bf16[2,3,32,512]{3,2,1,0:T(8,128)(2,1)S(1)} %get-tuple-element.70), channel_id=1, source_target_pairs={{2,4},{4,2},{6,8},{8,6},{10,12},{12,10},{14,16},{16,14},{18,20},{2... | collective-permute-start | bytes 589832 | tf_op jit(solution)/shard_map/ppermute | solution.py:355
  2.9 0.0 copy-start.9
  2.9 0.0 copy-start.11
  2.9 5.3 %collective-permute-start = (bf16[2,3,32,512]{3,2,1,0:T(8,128)(2,1)S(1)}, bf16[2,3,32,512]{3,2,1,0:T(8,128)(2,1)S(1)}, u32[]{:S(2)}, u32[]{:S(2)}) collective-permute-start(bf16[2,3,32,512]{3,2,1,0:T(8,128)(2,1)S(1)} %get-tuple-element.71), channel_id=1, source_target_pairs={{0,2},{2,0},{4,6},{6,4},{8,10},{10,8},{12,14},{14,12},{16,18},{18,... | collective-permute-start | bytes 589832 | tf_op jit(solution)/shard_map/ppermute | solution.py:355
  8.2 0.0 collective-permute-done.2.refs_6_.refs_10_
  8.2 0.9 %copy-done = bf16[2,4,32,512]{3,2,1,0:T(8,128)(2,1)S(1)} copy-done((bf16[2,4,32,512]{3,2,1,0:T(8,128)(2,1)S(1)}, bf16[2,4,32,512]{3,2,1,0:T(8,128)(2,1)}, u32[]{:S(2)}) %copy-start) | copy-done | bytes 262168
  9.2 1.4 %copy-done.2 = bf16[512,1536]{1,0:T(8,128)(2,1)S(1)} copy-done((bf16[512,1536]{1,0:T(8,128)(2,1)S(1)}, bf16[512,1536]{1,0:T(8,128)(2,1)}, u32[]{:S(2)}) %copy-start.2) | copy-done | bytes 1572888
  10.6 1.0 %copy-done.4 = bf16[512,512]{1,0:T(8,128)(2,1)S(1)} copy-done((bf16[512,512]{1,0:T(8,128)(2,1)S(1)}, bf16[512,512]{1,0:T(8,128)(2,1)}, u32[]{:S(2)}) %copy-start.4) | copy-done | bytes 524312
  11.6 0.9 %copy-done.6 = bf16[2,4,32,512]{3,2,1,0:T(8,128)(2,1)S(1)} copy-done((bf16[2,4,32,512]{3,2,1,0:T(8,128)(2,1)S(1)}, bf16[2,4,32,512]{3,2,1,0:T(8,128)(2,1)}, u32[]{:S(2)}) %copy-start.6) | copy-done | bytes 262168
  12.6 0.7 copy-done.8
  13.2 0.7 copy-done.10
  13.9 1.6 %stage_own.1 = (bf16[2,4,32,512]{3,2,1,0:T(8,128)(2,1)S(1)}, bf16[2,4,32,512]{3,2,1,0:T(8,128)(2,1)S(1)}, bf16[3,4,32,1024]{3,2,1,0:T(8,128)(2,1)S(1)}) custom-call(s32[16]{0:T(128)S(1)} %copy-done.8, s32[16]{0:T(128)S(1)} %copy-done.10, bf16[2,4,32,512]{3,2,1,0:T(8,128)(2,1)S(1)} %copy-done, bf16[512,1536]{1,0:T(8,128)(2,1)S(1)} %copy-done.2, ...), custom_call_target="tpu_custom_call" | custom-call | flops 4000000000 | bytes 1048576 | tf_op jit(solution)/shard_map/stage_own/pallas_call | solution.py:32
  15.5 0.0 collective-permute-done.1.refs_4_
  15.5 2.1 %collective-permute-done.refs_3_ = bf16[2,3,32,512]{3,2,1,0:T(8,128)(2,1)S(1)} collective-permute-done((bf16[2,3,32,512]{3,2,1,0:T(8,128)(2,1)S(1)}, bf16[2,3,32,512]{3,2,1,0:T(8,128)(2,1)S(1)}, u32[]{:S(2)}, u32[]{:S(2)}) %collective-permute-start) | collective-permute-done | bytes 196640 | tf_op jit(solution)/shard_map/ppermute | solution.py:355
  17.6 0.0 collective-permute-start.3
  17.6 0.5 collective-permute-start.4
  18.1 0.9 %collective-permute-done.3.refs_11_ = bf16[2,3,32,512]{3,2,1,0:T(8,128)(2,1)S(1)} collective-permute-done((bf16[2,3,32,512]{3,2,1,0:T(8,128)(2,1)S(1)}, bf16[2,3,32,512]{3,2,1,0:T(8,128)(2,1)S(1)}, u32[]{:S(2)}, u32[]{:S(2)}) %collective-permute-start.3) | collective-permute-done | bytes 196640 | tf_op jit(solution)/shard_map/ppermute | solution.py:355
  19.0 0.3 collective-permute-done.4.refs_12_
  19.3 0.0 copy-start.5
  19.3 11.4 %stage_attend.1 = (bf16[2,4,32,512]{3,2,1,0:T(8,128)(2,1)S(1)}, bf16[2,4,32,512]{3,2,1,0:T(8,128)(2,1)S(1)}, bf16[3,10,32,1024]{3,2,1,0:T(8,128)(2,1)S(1)}, f32[...) custom-call(s32[16]{0:T(128)S(1)} %copy-done.9, s32[16]{0:T(128)S(1)} %copy-done.11, ...), custom_call_target="tpu_custom_call" | custom-call | flops 16000000000 | bytes 1048576 | tf_op jit(solution)/shard_map/stage_attend/pallas_call | solution.py:32
  30.8 0.3 collective-permute-start.6
  31.1 2.5 %stage_out.1 = (bf16[2,4,32,512]{3,2,1,0:T(8,128)(2,1)}, f32[2,4,32,512]{3,2,1,0:T(8,128)S(1)}, f32[2,3,32,512]{3,2,1,0:T(8,128)S(1)}, f32[2,3,32,512]{3,2,1,0:T(8,128)S(1)}, bf16[10,32,512]{2,1,0:T(8,128)(2,1)S(1)}) custom-call(bf16[2,4,32,512]{3,2,1,0:T(8,128)(2,1)S(1)} %copy-done.1, bf16[2,4,32,512]{3,2,1,0:T(8,128)(2,1)S(1)} %copy-done.7, ...), custom_call_target="tpu_custom_call" | custom-call | flops 4000000000 | bytes 1048576 | tf_op jit(solution)/shard_map/stage_out/pallas_call | solution.py:32
  33.5 0.3 collective-permute-start.5
  33.8 0.0 collective-permute-done.6.refs_1_
  33.8 0.2 stage_split.2
  34.1 1.9 %collective-permute-start.7 = (bf16[4,16,2048]{2,1,0:T(8,128)(2,1)S(1)}, bf16[4,16,2048]{2,1,0:T(8,128)(2,1)S(1)}, u32[]{:S(2)}, u32[]{:S(2)}) collective-permute-start(bf16[4,16,2048]{2,1,0:T(8,128)(2,1)S(1)} %get-tuple-element.56), channel_id=1, source_target_pairs={{0,2},{2,0},{4,6},{6,4},{8,10},{10,8},{12,14},{14,12},{16,18},{18,... | collective-permute-start | bytes 786440 | tf_op jit(solution)/shard_map/ppermute | solution.py:434
  36.0 0.1 collective-permute-start.8
  36.1 1.5 %collective-permute-start.9 = (bf16[4,16,2048]{2,1,0:T(8,128)(2,1)S(1)}, bf16[4,16,2048]{2,1,0:T(8,128)(2,1)S(1)}, u32[]{:S(2)}, u32[]{:S(2)}) collective-permute-start(bf16[4,16,2048]{2,1,0:T(8,128)(2,1)S(1)} %get-tuple-element.58), channel_id=1, source_target_pairs={{0,6},{2,4},{4,2},{6,0},{8,14},{10,12},{12,10},{14,8},{16,22},{18,... | collective-permute-start | bytes 786440 | tf_op jit(solution)/shard_map/ppermute | solution.py:434
  37.6 0.0 collective-permute-done.5.refs_2_.refs_3_
  37.6 0.1 stage_fold.1
  37.8 5.5 %collective-permute-done.7.refs_1_ = bf16[4,16,2048]{2,1,0:T(8,128)(2,1)S(1)} collective-permute-done((bf16[4,16,2048]{2,1,0:T(8,128)(2,1)S(1)}, bf16[4,16,2048]{2,1,0:T(8,128)(2,1)S(1)}, u32[]{:S(2)}, u32[]{:S(2)}) %collective-permute-start.7) | collective-permute-done | bytes 262176 | tf_op jit(solution)/shard_map/ppermute | solution.py:434
  43.2 6.5 %collective-permute-done.8.refs_2_ = bf16[4,16,2048]{2,1,0:T(8,128)(2,1)S(1)} collective-permute-done((bf16[4,16,2048]{2,1,0:T(8,128)(2,1)S(1)}, bf16[4,16,2048]{2,1,0:T(8,128)(2,1)S(1)}, u32[]{:S(2)}, u32[]{:S(2)}) %collective-permute-start.8) | collective-permute-done | bytes 262176 | tf_op jit(solution)/shard_map/ppermute | solution.py:434
  49.8 0.0 collective-permute-done.9.refs_3_
  49.8 0.1 stage_split.3
  49.9 0.4 collective-permute-start.10
  50.3 0.7 collective-permute-start.11
  51.0 4.1 %collective-permute-start.12 = (bf16[1,16,2048]{2,1,0:T(8,128)(2,1)S(1)}, bf16[1,16,2048]{2,1,0:T(8,128)(2,1)S(1)}, u32[]{:S(2)}, u32[]{:S(2)}) collective-permute-start(bf16[1,16,2048]{2,1,0:T(8,128)(2,1)S(1)} %get-tuple-element.65), channel_id=1, source_target_pairs={{0,8},{2,10},{4,12},{6,14},{8,0},{10,2},{12,4},{14,6},{16,24},{18,... | collective-permute-start | bytes 196616 | tf_op jit(solution)/shard_map/ppermute | solution.py:434
  55.1 2.6 %collective-permute-start.13 = (bf16[1,16,2048]{2,1,0:T(8,128)(2,1)S(1)}, bf16[1,16,2048]{2,1,0:T(8,128)(2,1)S(1)}, u32[]{:S(2)}, u32[]{:S(2)}) collective-permute-start(bf16[1,16,2048]{2,1,0:T(8,128)(2,1)S(1)} %get-tuple-element.66), channel_id=1, source_target_pairs={{0,16},{2,18},{4,20},{6,22},{8,24},{10,26},{12,28},{14,30},{16,0},... | collective-permute-start | bytes 196616 | tf_op jit(solution)/shard_map/ppermute | solution.py:434
  57.7 0.0 collective-permute-start.14
  57.7 3.2 %collective-permute-done.12.refs_1_ = bf16[1,16,2048]{2,1,0:T(8,128)(2,1)S(1)} collective-permute-done((bf16[1,16,2048]{2,1,0:T(8,128)(2,1)S(1)}, bf16[1,16,2048]{2,1,0:T(8,128)(2,1)S(1)}, u32[]{:S(2)}, u32[]{:S(2)}) %collective-permute-start.12) | collective-permute-done | bytes 65568 | tf_op jit(solution)/shard_map/ppermute | solution.py:434
  60.9 2.4 %collective-permute-done.13.refs_2_ = bf16[1,16,2048]{2,1,0:T(8,128)(2,1)S(1)} collective-permute-done((bf16[1,16,2048]{2,1,0:T(8,128)(2,1)S(1)}, bf16[1,16,2048]{2,1,0:T(8,128)(2,1)S(1)}, u32[]{:S(2)}, u32[]{:S(2)}) %collective-permute-start.13) | collective-permute-done | bytes 65568 | tf_op jit(solution)/shard_map/ppermute | solution.py:434
  63.3 1.8 %collective-permute-done.14.refs_3_ = bf16[1,16,2048]{2,1,0:T(8,128)(2,1)S(1)} collective-permute-done((bf16[1,16,2048]{2,1,0:T(8,128)(2,1)S(1)}, bf16[1,16,2048]{2,1,0:T(8,128)(2,1)S(1)}, u32[]{:S(2)}, u32[]{:S(2)}) %collective-permute-start.14) | collective-permute-done | bytes 65568 | tf_op jit(solution)/shard_map/ppermute | solution.py:434
  65.2 0.7 %stage_sum.1 = (f32[16,1536]{1,0:T(8,128)}, f32[16,512]{1,0:T(8,128)}) custom-call(f32[1,16,2048]{2,1,0:T(8,128)S(1)} %get-tuple-element.64.refs_0_, bf16[1,16,2048]{2,1,0:T(8,128)(2,1)S(1)} %collective-permute-done.12.refs_1_, bf16[1,16,2048]{2,1,0:T(8,128)(2,1)S(1)} %collective-permute-done.13.refs_2_, bf16[1,16,2048]{2,1,0:T(8,128)(2,1)S(1)} %collective-permute-done.14.refs_3_), custom_call_target="tpu_custom_call" | custom-call | flops 1000000 | bytes 1048576 | tf_op jit(solution)/shard_map/stage_sum/pallas_call | solution.py:32
  65.8 0.0 collective-permute-done.10.refs_1_
  65.8 0.0 collective-permute-done.11.refs_2_
  65.8 0.9 %stage_last.1 = bf16[2,4,32,512]{3,2,1,0:T(8,128)(2,1)} custom-call(f32[2,4,32,512]{3,2,1,0:T(8,128)S(1)} %get-tuple-element.47.refs_0_, bf16[2,3,32,512]{3,2,1,0:T(8,128)(2,1)S(1)} %collective-permute-done.10.refs_1_, bf16[2,3,32,512]{3,2,1,0:T(8,128)(2,1)S(1)} %collective-permute-done.11.refs_2_, ...), custom_call_target="tpu_custom_call" | custom-call | flops 1000000 | bytes 1048576 | tf_op jit(solution)/shard_map/stage_last/pallas_call | solution.py:32
  (15 shorter events, 0.0 us)
Async XLA Ops:
  0.6 7.6 %collective-permute-start.2 = (bf16[2,4,32,512]{3,2,1,0:T(8,128)(2,1)}, bf16[2,4,32,512]{3,2,1,0:T(8,128)(2,1)S(1)}, u32[]{:S(2)}, u32[]{:S(2)}) collective-permute-start(bf16[2,4,32,512]{3,2,1,0:T(8,128)(2,1)} %refs_0_.5), channel_id=1, source_target_pairs={{0,1},{1,0},{2,3},{3,2},{4,5},{5,4},{6,7},{7,6},{8,9},{9,8},{10,11... | collective-permute-start | bytes 786440 | tf_op jit(solution)/shard_map/ppermute | solution.py:355
  2.2 13.3 %collective-permute-start.1 = (bf16[2,3,32,512]{3,2,1,0:T(8,128)(2,1)S(1)}, bf16[2,3,32,512]{3,2,1,0:T(8,128)(2,1)S(1)}, u32[]{:S(2)}, u32[]{:S(2)}) collective-permute-start(bf16[2,3,32,512]{3,2,1,0:T(8,128)(2,1)S(1)} %get-tuple-element.70), channel_id=1, source_target_pairs={{2,4},{4,2},{6,8},{8,6},{10,12},{12,10},{14,16},{16,14},{18,20},{2... | collective-permute-start | bytes 589832 | tf_op jit(solution)/shard_map/ppermute | solution.py:355
  2.9 16.4 %copy-start.9 = (s32[16]{0:T(128)S(1)}, s32[16]{0:T(128)}, u32[]{:S(2)}) copy-start(s32[16]{0:T(128)} %refs_0_.4) | copy-start | bytes 196
  2.9 16.4 %copy-start.11 = (s32[16]{0:T(128)S(1)}, s32[16]{0:T(128)}, u32[]{:S(2)}) copy-start(s32[16]{0:T(128)} %refs_1_.4) | copy-start | bytes 196
  2.9 14.7 %collective-permute-start = (bf16[2,3,32,512]{3,2,1,0:T(8,128)(2,1)S(1)}, bf16[2,3,32,512]{3,2,1,0:T(8,128)(2,1)S(1)}, u32[]{:S(2)}, u32[]{:S(2)}) collective-permute-start(bf16[2,3,32,512]{3,2,1,0:T(8,128)(2,1)S(1)} %get-tuple-element.71), channel_id=1, source_target_pairs={{0,2},{2,0},{4,6},{6,4},{8,10},{10,8},{12,14},{14,12},{16,18},{18,... | collective-permute-start | bytes 589832 | tf_op jit(solution)/shard_map/ppermute | solution.py:355
  8.2 1.0 %copy-start = (bf16[2,4,32,512]{3,2,1,0:T(8,128)(2,1)S(1)}, bf16[2,4,32,512]{3,2,1,0:T(8,128)(2,1)}, u32[]{:S(2)}) copy-start(bf16[2,4,32,512]{3,2,1,0:T(8,128)(2,1)} %refs_0_.5) | copy-start | bytes 786436
  9.2 1.4 %copy-start.2 = (bf16[512,1536]{1,0:T(8,128)(2,1)S(1)}, bf16[512,1536]{1,0:T(8,128)(2,1)}, u32[]{:S(2)}) copy-start(bf16[512,1536]{1,0:T(8,128)(2,1)} %refs_5_.3) | copy-start | bytes 4718596
  10.6 1.0 %copy-start.4 = (bf16[512,512]{1,0:T(8,128)(2,1)S(1)}, bf16[512,512]{1,0:T(8,128)(2,1)}, u32[]{:S(2)}) copy-start(bf16[512,512]{1,0:T(8,128)(2,1)} %refs_6_.1) | copy-start | bytes 1572868
  11.6 0.9 %copy-start.6 = (bf16[2,4,32,512]{3,2,1,0:T(8,128)(2,1)S(1)}, bf16[2,4,32,512]{3,2,1,0:T(8,128)(2,1)}, u32[]{:S(2)}) copy-start(bf16[2,4,32,512]{3,2,1,0:T(8,128)(2,1)} %refs_1_.5) | copy-start | bytes 786436
  12.6 0.7 copy-start.8
  13.2 0.7 copy-start.10
  13.9 5.4 %copy-start.1 = (bf16[2,4,32,512]{3,2,1,0:T(8,128)(2,1)S(1)}, bf16[2,4,32,512]{3,2,1,0:T(8,128)(2,1)}, u32[]{:S(2)}) copy-start(bf16[2,4,32,512]{3,2,1,0:T(8,128)(2,1)} %refs_0_.5) | copy-start | bytes 786436
  13.9 5.4 %copy-start.3 = (bf16[512,1536]{1,0:T(8,128)(2,1)S(1)}, bf16[512,1536]{1,0:T(8,128)(2,1)}, u32[]{:S(2)}) copy-start(bf16[512,1536]{1,0:T(8,128)(2,1)} %refs_5_.3) | copy-start | bytes 4718596
  13.9 5.4 %copy-start.7 = (bf16[2,4,32,512]{3,2,1,0:T(8,128)(2,1)S(1)}, bf16[2,4,32,512]{3,2,1,0:T(8,128)(2,1)}, u32[]{:S(2)}) copy-start(bf16[2,4,32,512]{3,2,1,0:T(8,128)(2,1)} %refs_1_.5) | copy-start | bytes 786436
  17.6 1.4 %collective-permute-start.3 = (bf16[2,3,32,512]{3,2,1,0:T(8,128)(2,1)S(1)}, bf16[2,3,32,512]{3,2,1,0:T(8,128)(2,1)S(1)}, u32[]{:S(2)}, u32[]{:S(2)}) collective-permute-start(bf16[2,3,32,512]{3,2,1,0:T(8,128)(2,1)S(1)} %collective-permute-done.refs_3_), channel_id=1, source_target_pairs={{0,1},{1,0},{2,3},{3,2},{4,5},{5,4},{6,7},{7,6},{8,9},{9,8},{10,11... | collective-permute-start | bytes 589832 | tf_op jit(solution)/shard_map/ppermute | solution.py:355
  17.6 1.7 %collective-permute-start.4 = (bf16[2,3,32,512]{3,2,1,0:T(8,128)(2,1)S(1)}, bf16[2,3,32,512]{3,2,1,0:T(8,128)(2,1)S(1)}, u32[]{:S(2)}, u32[]{:S(2)}) collective-permute-start(bf16[2,3,32,512]{3,2,1,0:T(8,128)(2,1)S(1)} %collective-permute-done.1.refs_4_), channel_id=1, source_target_pairs={{0,1},{1,0},{2,3},{3,2},{4,5},{5,4},{6,7},{7,6},{8,9},{9,8},{10,11... | collective-permute-start | bytes 589832 | tf_op jit(solution)/shard_map/ppermute | solution.py:355
  19.3 11.7 %copy-start.5 = (bf16[512,512]{1,0:T(8,128)(2,1)S(1)}, bf16[512,512]{1,0:T(8,128)(2,1)}, u32[]{:S(2)}) copy-start(bf16[512,512]{1,0:T(8,128)(2,1)} %refs_6_.1) | copy-start | bytes 1572868
  30.8 3.1 %collective-permute-start.6 = (bf16[16,16,2048]{2,1,0:T(8,128)(2,1)S(1)}, bf16[16,16,2048]{2,1,0:T(8,128)(2,1)S(1)}, u32[]{:S(2)}, u32[]{:S(2)}) collective-permute-start(bf16[16,16,2048]{2,1,0:T(8,128)(2,1)S(1)} %get-tuple-element.54), channel_id=1, source_target_pairs={{0,1},{1,0},{2,3},{3,2},{4,5},{5,4},{6,7},{7,6},{8,9},{9,8},{10,11... | collective-permute-start | bytes 3145736 | tf_op jit(solution)/shard_map/ppermute | solution.py:419
  33.5 4.1 %collective-permute-start.5 = (bf16[10,32,512]{2,1,0:T(8,128)(2,1)S(1)}, bf16[10,32,512]{2,1,0:T(8,128)(2,1)S(1)}, u32[]{:S(2)}, u32[]{:S(2)}) collective-permute-start(bf16[10,32,512]{2,1,0:T(8,128)(2,1)S(1)} %get-tuple-element.50), channel_id=1, source_target_pairs={{0,1},{1,0},{2,3},{3,2},{4,5},{5,4},{6,7},{7,6},{8,9},{9,8},{10,11... | collective-permute-start | bytes 983048 | tf_op jit(solution)/shard_map/ppermute | solution.py:355
  34.1 9.2 %collective-permute-start.7 = (bf16[4,16,2048]{2,1,0:T(8,128)(2,1)S(1)}, bf16[4,16,2048]{2,1,0:T(8,128)(2,1)S(1)}, u32[]{:S(2)}, u32[]{:S(2)}) collective-permute-start(bf16[4,16,2048]{2,1,0:T(8,128)(2,1)S(1)} %get-tuple-element.56), channel_id=1, source_target_pairs={{0,2},{2,0},{4,6},{6,4},{8,10},{10,8},{12,14},{14,12},{16,18},{18,... | collective-permute-start | bytes 786440 | tf_op jit(solution)/shard_map/ppermute | solution.py:434
  36.0 13.8 %collective-permute-start.8 = (bf16[4,16,2048]{2,1,0:T(8,128)(2,1)S(1)}, bf16[4,16,2048]{2,1,0:T(8,128)(2,1)S(1)}, u32[]{:S(2)}, u32[]{:S(2)}) collective-permute-start(bf16[4,16,2048]{2,1,0:T(8,128)(2,1)S(1)} %get-tuple-element.57), channel_id=1, source_target_pairs={{0,4},{2,6},{4,0},{6,2},{8,12},{10,14},{12,8},{14,10},{16,20},{18,... | collective-permute-start | bytes 786440 | tf_op jit(solution)/shard_map/ppermute | solution.py:434
  36.1 13.6 %collective-permute-start.9 = (bf16[4,16,2048]{2,1,0:T(8,128)(2,1)S(1)}, bf16[4,16,2048]{2,1,0:T(8,128)(2,1)S(1)}, u32[]{:S(2)}, u32[]{:S(2)}) collective-permute-start(bf16[4,16,2048]{2,1,0:T(8,128)(2,1)S(1)} %get-tuple-element.58), channel_id=1, source_target_pairs={{0,6},{2,4},{4,2},{6,0},{8,14},{10,12},{12,10},{14,8},{16,22},{18,... | collective-permute-start | bytes 786440 | tf_op jit(solution)/shard_map/ppermute | solution.py:434
  49.9 16.0 %collective-permute-start.10 = (bf16[2,3,32,512]{3,2,1,0:T(8,128)(2,1)S(1)}, bf16[2,3,32,512]{3,2,1,0:T(8,128)(2,1)S(1)}, u32[]{:S(2)}, u32[]{:S(2)}) collective-permute-start(bf16[2,3,32,512]{3,2,1,0:T(8,128)(2,1)S(1)} %get-tuple-element.62), channel_id=1, source_target_pairs={{0,2},{2,0},{4,6},{6,4},{8,10},{10,8},{12,14},{14,12},{16,18},{18,... | collective-permute-start | bytes 589832 | tf_op jit(solution)/shard_map/ppermute | solution.py:355
  50.3 15.5 %collective-permute-start.11 = (bf16[2,3,32,512]{3,2,1,0:T(8,128)(2,1)S(1)}, bf16[2,3,32,512]{3,2,1,0:T(8,128)(2,1)S(1)}, u32[]{:S(2)}, u32[]{:S(2)}) collective-permute-start(bf16[2,3,32,512]{3,2,1,0:T(8,128)(2,1)S(1)} %get-tuple-element.63), channel_id=1, source_target_pairs={{2,4},{4,2},{6,8},{8,6},{10,12},{12,10},{14,16},{16,14},{18,20},{2... | collective-permute-start | bytes 589832 | tf_op jit(solution)/shard_map/ppermute | solution.py:355
  51.0 10.0 %collective-permute-start.12 = (bf16[1,16,2048]{2,1,0:T(8,128)(2,1)S(1)}, bf16[1,16,2048]{2,1,0:T(8,128)(2,1)S(1)}, u32[]{:S(2)}, u32[]{:S(2)}) collective-permute-start(bf16[1,16,2048]{2,1,0:T(8,128)(2,1)S(1)} %get-tuple-element.65), channel_id=1, source_target_pairs={{0,8},{2,10},{4,12},{6,14},{8,0},{10,2},{12,4},{14,6},{16,24},{18,... | collective-permute-start | bytes 196616 | tf_op jit(solution)/shard_map/ppermute | solution.py:434
  55.1 8.2 %collective-permute-start.13 = (bf16[1,16,2048]{2,1,0:T(8,128)(2,1)S(1)}, bf16[1,16,2048]{2,1,0:T(8,128)(2,1)S(1)}, u32[]{:S(2)}, u32[]{:S(2)}) collective-permute-start(bf16[1,16,2048]{2,1,0:T(8,128)(2,1)S(1)} %get-tuple-element.66), channel_id=1, source_target_pairs={{0,16},{2,18},{4,20},{6,22},{8,24},{10,26},{12,28},{14,30},{16,0},... | collective-permute-start | bytes 196616 | tf_op jit(solution)/shard_map/ppermute | solution.py:434
  57.7 7.5 %collective-permute-start.14 = (bf16[1,16,2048]{2,1,0:T(8,128)(2,1)S(1)}, bf16[1,16,2048]{2,1,0:T(8,128)(2,1)S(1)}, u32[]{:S(2)}, u32[]{:S(2)}) collective-permute-start(bf16[1,16,2048]{2,1,0:T(8,128)(2,1)S(1)} %get-tuple-element.67), channel_id=1, source_target_pairs={{0,24},{2,26},{4,28},{6,30},{8,16},{10,18},{12,20},{14,22},{16,8},... | collective-permute-start | bytes 196616 | tf_op jit(solution)/shard_map/ppermute | solution.py:434

commit v3 on v2

--- a/solution.py
+++ b/solution.py
@@ -428,12 +428,12 @@
             [(share, F32)] + [(share, BF16)] * (radix - 1),
             [x, *parts],
         )
-        if stride > 1:
-            send_e, send_o, *pieces = lax.optimization_barrier((send_e, send_o, *pieces))
         parts = [
             lax.ppermute(piece, "tile", xor_route(tiles, (k + 1) * stride))
             for k, piece in enumerate(pieces)
         ]
+        if stride == 1:
+            send_e, send_o, parts[2] = lax.optimization_barrier((send_e, send_o, parts[2]))
         stride *= radix
     d_qkv, d_out = call(
         bind(stage_sum, len(parts)),

time: 67 us -> 63.3 us (0.945)
  the two profiles are of different devices: /device:TPU:0 before, /device:TPU:4 now
where the time goes in v3:
time: 63.3 us; the launch traced here: 63 us
  starting transfers between devices  23.5 us (37%)
  Pallas kernels  17.5 us (28%)
  waiting for transfers between devices  14.5 us (23%)
  local copies, waits for them, and re-layouts  6.75 us (11%)
  between operations  0.78 us (1%)
    pallas_call x8, Pallas kernels, call(): pl.pallas_call(body, name=name, out_shape=[jax.ShapeDtypeStruct(shape, ki...  17.5 us
    ppermute x6, waiting for transfers between devices, local(): lax.ppermute(piece, 'tile', xor_route(tiles, (k + 1) * stride))  13.2 us
    ppermute x6, starting transfers between devices, local(): lax.ppermute(piece, 'tile', xor_route(tiles, (k + 1) * stride))  12.3 us
    ppermute x8, starting transfers between devices, swap(): return lax.ppermute(block, axis, swap_pairs(lax.axis_size(axis), first))  10.9 us
    unnamed x24, local copies, waits for them, and re-layouts  5.69 us
    ppermute x8, waiting for transfers between devices, swap(): return lax.ppermute(block, axis, swap_pairs(lax.axis_size(axis), first))  1.27 us
  transfers between devices with their start and end apart: 15, of which 6 were waited for; matrix products, arithmetic and copies ran while one was open for 2% of the time, Pallas kernels for 8%

profile of v3, /device:TPU:4, one launch (start us, length us, event | category | flops | bytes accessed | tf_op | source)
XLA Modules:
  0.0 63.0 jit_solution(8862947095984168359)
XLA Ops:
  0.6 0.1 collective-permute-start.2
  0.7 1.1 %constant_dynamic-slice_fusion = (bf16[2,3,32,512]{3,2,1,0:T(8,128)(2,1)S(1)}, bf16[2,3,32,512]{3,2,1,0:T(8,128)(2,1)S(1)}) fusion(bf16[2,4,32,512]{3,2,1,0:T(8,128)(2,1)} %refs_0_.5, s32[]{:T(128)S(6)} %select_n.10, s32[]{:T(128)S(6)} %select_n.9), kind=kLoop, calls=%fused_computation | loop fusion | bytes 786440 | tf_op jit(solution)/shard_map/dynamic_slice | solution.py:360
  1.8 3.3 %collective-permute-start.1 = (bf16[2,3,32,512]{3,2,1,0:T(8,128)(2,1)S(1)}, bf16[2,3,32,512]{3,2,1,0:T(8,128)(2,1)S(1)}, u32[]{:S(2)}, u32[]{:S(2)}) collective-permute-start(bf16[2,3,32,512]{3,2,1,0:T(8,128)(2,1)S(1)} %get-tuple-element.66), channel_id=1, source_target_pairs={{2,4},{4,2},{6,8},{8,6},{10,12},{12,10},{14,16},{16,14},{18,20},{2... | collective-permute-start | bytes 589832 | tf_op jit(solution)/shard_map/ppermute | solution.py:355
  5.1 0.0 copy-start.9
  5.1 0.0 copy-start.11
  5.2 1.6 %collective-permute-start = (bf16[2,3,32,512]{3,2,1,0:T(8,128)(2,1)S(1)}, bf16[2,3,32,512]{3,2,1,0:T(8,128)(2,1)S(1)}, u32[]{:S(2)}, u32[]{:S(2)}) collective-permute-start(bf16[2,3,32,512]{3,2,1,0:T(8,128)(2,1)S(1)} %get-tuple-element.67), channel_id=1, source_target_pairs={{0,2},{2,0},{4,6},{6,4},{8,10},{10,8},{12,14},{14,12},{16,18},{18,... | collective-permute-start | bytes 589832 | tf_op jit(solution)/shard_map/ppermute | solution.py:355
  6.8 0.0 collective-permute-done.2.refs_6_.refs_10_
  6.8 0.9 %copy-done = bf16[2,4,32,512]{3,2,1,0:T(8,128)(2,1)S(1)} copy-done((bf16[2,4,32,512]{3,2,1,0:T(8,128)(2,1)S(1)}, bf16[2,4,32,512]{3,2,1,0:T(8,128)(2,1)}, u32[]{:S(2)}) %copy-start) | copy-done | bytes 262168
  7.7 1.4 %copy-done.2 = bf16[512,1536]{1,0:T(8,128)(2,1)S(1)} copy-done((bf16[512,1536]{1,0:T(8,128)(2,1)S(1)}, bf16[512,1536]{1,0:T(8,128)(2,1)}, u32[]{:S(2)}) %copy-start.2) | copy-done | bytes 1572888
  9.1 1.0 %copy-done.4 = bf16[512,512]{1,0:T(8,128)(2,1)S(1)} copy-done((bf16[512,512]{1,0:T(8,128)(2,1)S(1)}, bf16[512,512]{1,0:T(8,128)(2,1)}, u32[]{:S(2)}) %copy-start.4) | copy-done | bytes 524312
  10.2 0.9 %copy-done.6 = bf16[2,4,32,512]{3,2,1,0:T(8,128)(2,1)S(1)} copy-done((bf16[2,4,32,512]{3,2,1,0:T(8,128)(2,1)S(1)}, bf16[2,4,32,512]{3,2,1,0:T(8,128)(2,1)}, u32[]{:S(2)}) %copy-start.6) | copy-done | bytes 262168
  11.1 0.7 %copy-done.8 = s32[16]{0:T(128)S(1)} copy-done((s32[16]{0:T(128)S(1)}, s32[16]{0:T(128)}, u32[]{:S(2)}) %copy-start.8) | copy-done | bytes 88
  11.8 0.7 %copy-done.10 = s32[16]{0:T(128)S(1)} copy-done((s32[16]{0:T(128)S(1)}, s32[16]{0:T(128)}, u32[]{:S(2)}) %copy-start.10) | copy-done | bytes 88
  12.4 1.6 %stage_own.1 = (bf16[2,4,32,512]{3,2,1,0:T(8,128)(2,1)S(1)}, bf16[2,4,32,512]{3,2,1,0:T(8,128)(2,1)S(1)}, bf16[3,4,32,1024]{3,2,1,0:T(8,128)(2,1)S(1)}) custom-call(s32[16]{0:T(128)S(1)} %copy-done.8, s32[16]{0:T(128)S(1)} %copy-done.10, bf16[2,4,32,512]{3,2,1,0:T(8,128)(2,1)S(1)} %copy-done, bf16[512,1536]{1,0:T(8,128)(2,1)S(1)} %copy-done.2, ...), custom_call_target="tpu_custom_call" | custom-call | flops 4000000000 | bytes 1048576 | tf_op jit(solution)/shard_map/stage_own/pallas_call | solution.py:32
  14.1 0.0 collective-permute-done.1.refs_4_
  14.1 0.0 collective-permute-done.refs_3_
  14.1 0.0 collective-permute-start.3
  14.2 0.5 collective-permute-start.4
  14.7 0.9 %collective-permute-done.3.refs_11_ = bf16[2,3,32,512]{3,2,1,0:T(8,128)(2,1)S(1)} collective-permute-done((bf16[2,3,32,512]{3,2,1,0:T(8,128)(2,1)S(1)}, bf16[2,3,32,512]{3,2,1,0:T(8,128)(2,1)S(1)}, u32[]{:S(2)}, u32[]{:S(2)}) %collective-permute-start.3) | collective-permute-done | bytes 196640 | tf_op jit(solution)/shard_map/ppermute | solution.py:355
  15.6 0.3 collective-permute-done.4.refs_12_
  15.9 0.0 copy-start.5
  15.9 11.4 %stage_attend.1 = (bf16[2,4,32,512]{3,2,1,0:T(8,128)(2,1)S(1)}, bf16[2,4,32,512]{3,2,1,0:T(8,128)(2,1)S(1)}, bf16[3,10,32,1024]{3,2,1,0:T(8,128)(2,1)S(1)}, f32[...) custom-call(s32[16]{0:T(128)S(1)} %copy-done.9, s32[16]{0:T(128)S(1)} %copy-done.11, ...), custom_call_target="tpu_custom_call" | custom-call | flops 16000000000 | bytes 1048576 | tf_op jit(solution)/shard_map/stage_attend/pallas_call | solution.py:32
  27.4 0.3 collective-permute-start.6
  27.6 2.5 %stage_out.1 = (bf16[2,4,32,512]{3,2,1,0:T(8,128)(2,1)}, f32[2,4,32,512]{3,2,1,0:T(8,128)S(1)}, f32[2,3,32,512]{3,2,1,0:T(8,128)S(1)}, f32[2,3,32,512]{3,2,1,0:T(8,128)S(1)}, bf16[10,32,512]{2,1,0:T(8,128)(2,1)S(1)}) custom-call(bf16[2,4,32,512]{3,2,1,0:T(8,128)(2,1)S(1)} %copy-done.1, bf16[2,4,32,512]{3,2,1,0:T(8,128)(2,1)S(1)} %copy-done.7, ...), custom_call_target="tpu_custom_call" | custom-call | flops 4000000000 | bytes 1048576 | tf_op jit(solution)/shard_map/stage_out/pallas_call | solution.py:32
  30.1 0.3 collective-permute-start.5
  30.4 0.0 collective-permute-done.6.refs_1_
  30.4 0.2 stage_split.2
  30.6 3.8 %collective-permute-start.7 = (bf16[4,16,2048]{2,1,0:T(8,128)(2,1)S(1)}, bf16[4,16,2048]{2,1,0:T(8,128)(2,1)S(1)}, u32[]{:S(2)}, u32[]{:S(2)}) collective-permute-start(bf16[4,16,2048]{2,1,0:T(8,128)(2,1)S(1)} %get-tuple-element.53), channel_id=1, source_target_pairs={{0,6},{2,4},{4,2},{6,0},{8,14},{10,12},{12,10},{14,8},{16,22},{18,... | collective-permute-start | bytes 786440 | tf_op jit(solution)/shard_map/ppermute | solution.py:432
  34.5 0.2 collective-permute-start.10
  34.6 0.5 collective-permute-start.11
  35.1 0.0 collective-permute-done.5.refs_2_.refs_3_
  35.1 0.1 stage_fold.1
  35.3 6.3 %collective-permute-done.7.refs_3_ = bf16[4,16,2048]{2,1,0:T(8,128)(2,1)S(1)} collective-permute-done((bf16[4,16,2048]{2,1,0:T(8,128)(2,1)S(1)}, bf16[4,16,2048]{2,1,0:T(8,128)(2,1)S(1)}, u32[]{:S(2)}, u32[]{:S(2)}) %collective-permute-start.7) | collective-permute-done | bytes 262176 | tf_op jit(solution)/shard_map/ppermute | solution.py:432
  41.6 1.6 %collective-permute-start.8 = (bf16[2,3,32,512]{3,2,1,0:T(8,128)(2,1)S(1)}, bf16[2,3,32,512]{3,2,1,0:T(8,128)(2,1)S(1)}, u32[]{:S(2)}, u32[]{:S(2)}) collective-permute-start(bf16[2,3,32,512]{3,2,1,0:T(8,128)(2,1)S(1)} %get-tuple-element.54), channel_id=1, source_target_pairs={{0,2},{2,0},{4,6},{6,4},{8,10},{10,8},{12,14},{14,12},{16,18},{18,... | collective-permute-start | bytes 589832 | tf_op jit(solution)/shard_map/ppermute | solution.py:355
  43.2 3.4 %collective-permute-start.9 = (bf16[2,3,32,512]{3,2,1,0:T(8,128)(2,1)S(1)}, bf16[2,3,32,512]{3,2,1,0:T(8,128)(2,1)S(1)}, u32[]{:S(2)}, u32[]{:S(2)}) collective-permute-start(bf16[2,3,32,512]{3,2,1,0:T(8,128)(2,1)S(1)} %get-tuple-element.55), channel_id=1, source_target_pairs={{2,4},{4,2},{6,8},{8,6},{10,12},{12,10},{14,16},{16,14},{18,20},{2... | collective-permute-start | bytes 589832 | tf_op jit(solution)/shard_map/ppermute | solution.py:355
  46.6 0.8 %collective-permute-done.10.refs_1_ = bf16[4,16,2048]{2,1,0:T(8,128)(2,1)S(1)} collective-permute-done((bf16[4,16,2048]{2,1,0:T(8,128)(2,1)S(1)}, bf16[4,16,2048]{2,1,0:T(8,128)(2,1)S(1)}, u32[]{:S(2)}, u32[]{:S(2)}) %collective-permute-start.10) | collective-permute-done | bytes 262176 | tf_op jit(solution)/shard_map/ppermute | solution.py:432
  47.4 0.0 collective-permute-done.11.refs_2_
  47.4 0.1 stage_split.3
  47.5 1.7 %collective-permute-start.12 = (bf16[1,16,2048]{2,1,0:T(8,128)(2,1)S(1)}, bf16[1,16,2048]{2,1,0:T(8,128)(2,1)S(1)}, u32[]{:S(2)}, u32[]{:S(2)}) collective-permute-start(bf16[1,16,2048]{2,1,0:T(8,128)(2,1)S(1)} %get-tuple-element.61), channel_id=1, source_target_pairs={{0,8},{2,10},{4,12},{6,14},{8,0},{10,2},{12,4},{14,6},{16,24},{18,... | collective-permute-start | bytes 196616 | tf_op jit(solution)/shard_map/ppermute | solution.py:432
  49.3 6.1 %collective-permute-start.13 = (bf16[1,16,2048]{2,1,0:T(8,128)(2,1)S(1)}, bf16[1,16,2048]{2,1,0:T(8,128)(2,1)S(1)}, u32[]{:S(2)}, u32[]{:S(2)}) collective-permute-start(bf16[1,16,2048]{2,1,0:T(8,128)(2,1)S(1)} %get-tuple-element.62), channel_id=1, source_target_pairs={{0,16},{2,18},{4,20},{6,22},{8,24},{10,26},{12,28},{14,30},{16,0},... | collective-permute-start | bytes 196616 | tf_op jit(solution)/shard_map/ppermute | solution.py:432
  55.4 0.0 collective-permute-start.14
  55.4 0.0 collective-permute-done.12.refs_1_
  55.4 2.9 %collective-permute-done.13.refs_2_ = bf16[1,16,2048]{2,1,0:T(8,128)(2,1)S(1)} collective-permute-done((bf16[1,16,2048]{2,1,0:T(8,128)(2,1)S(1)}, bf16[1,16,2048]{2,1,0:T(8,128)(2,1)S(1)}, u32[]{:S(2)}, u32[]{:S(2)}) %collective-permute-start.13) | collective-permute-done | bytes 65568 | tf_op jit(solution)/shard_map/ppermute | solution.py:432
  58.3 3.1 %collective-permute-done.14.refs_3_ = bf16[1,16,2048]{2,1,0:T(8,128)(2,1)S(1)} collective-permute-done((bf16[1,16,2048]{2,1,0:T(8,128)(2,1)S(1)}, bf16[1,16,2048]{2,1,0:T(8,128)(2,1)S(1)}, u32[]{:S(2)}, u32[]{:S(2)}) %collective-permute-start.14) | collective-permute-done | bytes 65568 | tf_op jit(solution)/shard_map/ppermute | solution.py:432
  61.4 0.7 %stage_sum.1 = (f32[16,1536]{1,0:T(8,128)}, f32[16,512]{1,0:T(8,128)}) custom-call(f32[1,16,2048]{2,1,0:T(8,128)S(1)} %get-tuple-element.60.refs_0_, bf16[1,16,2048]{2,1,0:T(8,128)(2,1)S(1)} %collective-permute-done.12.refs_1_, bf16[1,16,2048]{2,1,0:T(8,128)(2,1)S(1)} %collective-permute-done.13.refs_2_, bf16[1,16,2048]{2,1,0:T(8,128)(2,1)S(1)} %collective-permute-done.14.refs_3_), custom_call_target="tpu_custom_call" | custom-call | flops 1000000 | bytes 1048576 | tf_op jit(solution)/shard_map/stage_sum/pallas_call | solution.py:32
  62.1 0.0 collective-permute-done.8.refs_1_
  62.1 0.0 collective-permute-done.9.refs_2_
  62.1 0.9 %stage_last.1 = bf16[2,4,32,512]{3,2,1,0:T(8,128)(2,1)} custom-call(f32[2,4,32,512]{3,2,1,0:T(8,128)S(1)} %get-tuple-element.45.refs_0_, bf16[2,3,32,512]{3,2,1,0:T(8,128)(2,1)S(1)} %collective-permute-done.8.refs_1_, bf16[2,3,32,512]{3,2,1,0:T(8,128)(2,1)S(1)} %collective-permute-done.9.refs_2_, bf16[10,32,512]{2,1,0:T(8,128)(2,1)S(1)} %collective-permute-done.5.refs_2_.refs_3_), custom_call_target="tpu_custom_call" | custom-call | flops 1000000 | bytes 1048576 | tf_op jit(solution)/shard_map/stage_last/pallas_call | solution.py:32
  (15 shorter events, 0.0 us)
Async XLA Ops:
  0.6 6.1 %collective-permute-start.2 = (bf16[2,4,32,512]{3,2,1,0:T(8,128)(2,1)}, bf16[2,4,32,512]{3,2,1,0:T(8,128)(2,1)S(1)}, u32[]{:S(2)}, u32[]{:S(2)}) collective-permute-start(bf16[2,4,32,512]{3,2,1,0:T(8,128)(2,1)} %refs_0_.5), channel_id=1, source_target_pairs={{0,1},{1,0},{2,3},{3,2},{4,5},{5,4},{6,7},{7,6},{8,9},{9,8},{10,11... | collective-permute-start | bytes 786440 | tf_op jit(solution)/shard_map/ppermute | solution.py:355
  1.8 12.3 %collective-permute-start.1 = (bf16[2,3,32,512]{3,2,1,0:T(8,128)(2,1)S(1)}, bf16[2,3,32,512]{3,2,1,0:T(8,128)(2,1)S(1)}, u32[]{:S(2)}, u32[]{:S(2)}) collective-permute-start(bf16[2,3,32,512]{3,2,1,0:T(8,128)(2,1)S(1)} %get-tuple-element.66), channel_id=1, source_target_pairs={{2,4},{4,2},{6,8},{8,6},{10,12},{12,10},{14,16},{16,14},{18,20},{2... | collective-permute-start | bytes 589832 | tf_op jit(solution)/shard_map/ppermute | solution.py:355
  5.1 10.7 %copy-start.9 = (s32[16]{0:T(128)S(1)}, s32[16]{0:T(128)}, u32[]{:S(2)}) copy-start(s32[16]{0:T(128)} %refs_0_.4) | copy-start | bytes 196
  5.1 10.7 %copy-start.11 = (s32[16]{0:T(128)S(1)}, s32[16]{0:T(128)}, u32[]{:S(2)}) copy-start(s32[16]{0:T(128)} %refs_1_.4) | copy-start | bytes 196
  5.2 9.0 %collective-permute-start = (bf16[2,3,32,512]{3,2,1,0:T(8,128)(2,1)S(1)}, bf16[2,3,32,512]{3,2,1,0:T(8,128)(2,1)S(1)}, u32[]{:S(2)}, u32[]{:S(2)}) collective-permute-start(bf16[2,3,32,512]{3,2,1,0:T(8,128)(2,1)S(1)} %get-tuple-element.67), channel_id=1, source_target_pairs={{0,2},{2,0},{4,6},{6,4},{8,10},{10,8},{12,14},{14,12},{16,18},{18,... | collective-permute-start | bytes 589832 | tf_op jit(solution)/shard_map/ppermute | solution.py:355
  6.8 1.0 %copy-start = (bf16[2,4,32,512]{3,2,1,0:T(8,128)(2,1)S(1)}, bf16[2,4,32,512]{3,2,1,0:T(8,128)(2,1)}, u32[]{:S(2)}) copy-start(bf16[2,4,32,512]{3,2,1,0:T(8,128)(2,1)} %refs_0_.5) | copy-start | bytes 786436
  7.7 1.4 %copy-start.2 = (bf16[512,1536]{1,0:T(8,128)(2,1)S(1)}, bf16[512,1536]{1,0:T(8,128)(2,1)}, u32[]{:S(2)}) copy-start(bf16[512,1536]{1,0:T(8,128)(2,1)} %refs_5_.3) | copy-start | bytes 4718596
  9.1 1.0 %copy-start.4 = (bf16[512,512]{1,0:T(8,128)(2,1)S(1)}, bf16[512,512]{1,0:T(8,128)(2,1)}, u32[]{:S(2)}) copy-start(bf16[512,512]{1,0:T(8,128)(2,1)} %refs_6_.1) | copy-start | bytes 1572868
  10.2 0.9 %copy-start.6 = (bf16[2,4,32,512]{3,2,1,0:T(8,128)(2,1)S(1)}, bf16[2,4,32,512]{3,2,1,0:T(8,128)(2,1)}, u32[]{:S(2)}) copy-start(bf16[2,4,32,512]{3,2,1,0:T(8,128)(2,1)} %refs_1_.5) | copy-start | bytes 786436
  11.1 0.7 %copy-start.8 = (s32[16]{0:T(128)S(1)}, s32[16]{0:T(128)}, u32[]{:S(2)}) copy-start(s32[16]{0:T(128)} %refs_0_.4) | copy-start | bytes 196
  11.8 0.7 %copy-start.10 = (s32[16]{0:T(128)S(1)}, s32[16]{0:T(128)}, u32[]{:S(2)}) copy-start(s32[16]{0:T(128)} %refs_1_.4) | copy-start | bytes 196
  12.4 3.4 %copy-start.1 = (bf16[2,4,32,512]{3,2,1,0:T(8,128)(2,1)S(1)}, bf16[2,4,32,512]{3,2,1,0:T(8,128)(2,1)}, u32[]{:S(2)}) copy-start(bf16[2,4,32,512]{3,2,1,0:T(8,128)(2,1)} %refs_0_.5) | copy-start | bytes 786436
  12.4 3.4 %copy-start.3 = (bf16[512,1536]{1,0:T(8,128)(2,1)S(1)}, bf16[512,1536]{1,0:T(8,128)(2,1)}, u32[]{:S(2)}) copy-start(bf16[512,1536]{1,0:T(8,128)(2,1)} %refs_5_.3) | copy-start | bytes 4718596
  12.4 3.5 %copy-start.7 = (bf16[2,4,32,512]{3,2,1,0:T(8,128)(2,1)S(1)}, bf16[2,4,32,512]{3,2,1,0:T(8,128)(2,1)}, u32[]{:S(2)}) copy-start(bf16[2,4,32,512]{3,2,1,0:T(8,128)(2,1)} %refs_1_.5) | copy-start | bytes 786436
  14.1 1.5 %collective-permute-start.3 = (bf16[2,3,32,512]{3,2,1,0:T(8,128)(2,1)S(1)}, bf16[2,3,32,512]{3,2,1,0:T(8,128)(2,1)S(1)}, u32[]{:S(2)}, u32[]{:S(2)}) collective-permute-start(bf16[2,3,32,512]{3,2,1,0:T(8,128)(2,1)S(1)} %collective-permute-done.refs_3_), channel_id=1, source_target_pairs={{0,1},{1,0},{2,3},{3,2},{4,5},{5,4},{6,7},{7,6},{8,9},{9,8},{10,11... | collective-permute-start | bytes 589832 | tf_op jit(solution)/shard_map/ppermute | solution.py:355
  14.2 1.7 %collective-permute-start.4 = (bf16[2,3,32,512]{3,2,1,0:T(8,128)(2,1)S(1)}, bf16[2,3,32,512]{3,2,1,0:T(8,128)(2,1)S(1)}, u32[]{:S(2)}, u32[]{:S(2)}) collective-permute-start(bf16[2,3,32,512]{3,2,1,0:T(8,128)(2,1)S(1)} %collective-permute-done.1.refs_4_), channel_id=1, source_target_pairs={{0,1},{1,0},{2,3},{3,2},{4,5},{5,4},{6,7},{7,6},{8,9},{9,8},{10,11... | collective-permute-start | bytes 589832 | tf_op jit(solution)/shard_map/ppermute | solution.py:355
  15.9 11.7 %copy-start.5 = (bf16[512,512]{1,0:T(8,128)(2,1)S(1)}, bf16[512,512]{1,0:T(8,128)(2,1)}, u32[]{:S(2)}) copy-start(bf16[512,512]{1,0:T(8,128)(2,1)} %refs_6_.1) | copy-start | bytes 1572868
  27.4 3.1 %collective-permute-start.6 = (bf16[16,16,2048]{2,1,0:T(8,128)(2,1)S(1)}, bf16[16,16,2048]{2,1,0:T(8,128)(2,1)S(1)}, u32[]{:S(2)}, u32[]{:S(2)}) collective-permute-start(bf16[16,16,2048]{2,1,0:T(8,128)(2,1)S(1)} %get-tuple-element.52), channel_id=1, source_target_pairs={{0,1},{1,0},{2,3},{3,2},{4,5},{5,4},{6,7},{7,6},{8,9},{9,8},{10,11... | collective-permute-start | bytes 3145736 | tf_op jit(solution)/shard_map/ppermute | solution.py:419
  30.1 5.0 %collective-permute-start.5 = (bf16[10,32,512]{2,1,0:T(8,128)(2,1)S(1)}, bf16[10,32,512]{2,1,0:T(8,128)(2,1)S(1)}, u32[]{:S(2)}, u32[]{:S(2)}) collective-permute-start(bf16[10,32,512]{2,1,0:T(8,128)(2,1)S(1)} %get-tuple-element.48), channel_id=1, source_target_pairs={{0,1},{1,0},{2,3},{3,2},{4,5},{5,4},{6,7},{7,6},{8,9},{9,8},{10,11... | collective-permute-start | bytes 983048 | tf_op jit(solution)/shard_map/ppermute | solution.py:355
  30.6 11.0 %collective-permute-start.7 = (bf16[4,16,2048]{2,1,0:T(8,128)(2,1)S(1)}, bf16[4,16,2048]{2,1,0:T(8,128)(2,1)S(1)}, u32[]{:S(2)}, u32[]{:S(2)}) collective-permute-start(bf16[4,16,2048]{2,1,0:T(8,128)(2,1)S(1)} %get-tuple-element.53), channel_id=1, source_target_pairs={{0,6},{2,4},{4,2},{6,0},{8,14},{10,12},{12,10},{14,8},{16,22},{18,... | collective-permute-start | bytes 786440 | tf_op jit(solution)/shard_map/ppermute | solution.py:432
  34.5 12.9 %collective-permute-start.10 = (bf16[4,16,2048]{2,1,0:T(8,128)(2,1)S(1)}, bf16[4,16,2048]{2,1,0:T(8,128)(2,1)S(1)}, u32[]{:S(2)}, u32[]{:S(2)}) collective-permute-start(bf16[4,16,2048]{2,1,0:T(8,128)(2,1)S(1)} %get-tuple-element.57), channel_id=1, source_target_pairs={{0,2},{2,0},{4,6},{6,4},{8,10},{10,8},{12,14},{14,12},{16,18},{18,... | collective-permute-start | bytes 786440 | tf_op jit(solution)/shard_map/ppermute | solution.py:432
  34.6 12.8 %collective-permute-start.11 = (bf16[4,16,2048]{2,1,0:T(8,128)(2,1)S(1)}, bf16[4,16,2048]{2,1,0:T(8,128)(2,1)S(1)}, u32[]{:S(2)}, u32[]{:S(2)}) collective-permute-start(bf16[4,16,2048]{2,1,0:T(8,128)(2,1)S(1)} %get-tuple-element.58), channel_id=1, source_target_pairs={{0,4},{2,6},{4,0},{6,2},{8,12},{10,14},{12,8},{14,10},{16,20},{18,... | collective-permute-start | bytes 786440 | tf_op jit(solution)/shard_map/ppermute | solution.py:432
  41.6 20.5 %collective-permute-start.8 = (bf16[2,3,32,512]{3,2,1,0:T(8,128)(2,1)S(1)}, bf16[2,3,32,512]{3,2,1,0:T(8,128)(2,1)S(1)}, u32[]{:S(2)}, u32[]{:S(2)}) collective-permute-start(bf16[2,3,32,512]{3,2,1,0:T(8,128)(2,1)S(1)} %get-tuple-element.54), channel_id=1, source_target_pairs={{0,2},{2,0},{4,6},{6,4},{8,10},{10,8},{12,14},{14,12},{16,18},{18,... | collective-permute-start | bytes 589832 | tf_op jit(solution)/shard_map/ppermute | solution.py:355
  43.2 18.9 %collective-permute-start.9 = (bf16[2,3,32,512]{3,2,1,0:T(8,128)(2,1)S(1)}, bf16[2,3,32,512]{3,2,1,0:T(8,128)(2,1)S(1)}, u32[]{:S(2)}, u32[]{:S(2)}) collective-permute-start(bf16[2,3,32,512]{3,2,1,0:T(8,128)(2,1)S(1)} %get-tuple-element.55), channel_id=1, source_target_pairs={{2,4},{4,2},{6,8},{8,6},{10,12},{12,10},{14,16},{16,14},{18,20},{2... | collective-permute-start | bytes 589832 | tf_op jit(solution)/shard_map/ppermute | solution.py:355
  47.5 7.8 %collective-permute-start.12 = (bf16[1,16,2048]{2,1,0:T(8,128)(2,1)S(1)}, bf16[1,16,2048]{2,1,0:T(8,128)(2,1)S(1)}, u32[]{:S(2)}, u32[]{:S(2)}) collective-permute-start(bf16[1,16,2048]{2,1,0:T(8,128)(2,1)S(1)} %get-tuple-element.61), channel_id=1, source_target_pairs={{0,8},{2,10},{4,12},{6,14},{8,0},{10,2},{12,4},{14,6},{16,24},{18,... | collective-permute-start | bytes 196616 | tf_op jit(solution)/shard_map/ppermute | solution.py:432
  49.3 9.0 %collective-permute-start.13 = (bf16[1,16,2048]{2,1,0:T(8,128)(2,1)S(1)}, bf16[1,16,2048]{2,1,0:T(8,128)(2,1)S(1)}, u32[]{:S(2)}, u32[]{:S(2)}) collective-permute-start(bf16[1,16,2048]{2,1,0:T(8,128)(2,1)S(1)} %get-tuple-element.62), channel_id=1, source_target_pairs={{0,16},{2,18},{4,20},{6,22},{8,24},{10,26},{12,28},{14,30},{16,0},... | collective-permute-start | bytes 196616 | tf_op jit(solution)/shard_map/ppermute | solution.py:432
  55.4 6.1 %collective-permute-start.14 = (bf16[1,16,2048]{2,1,0:T(8,128)(2,1)S(1)}, bf16[1,16,2048]{2,1,0:T(8,128)(2,1)S(1)}, u32[]{:S(2)}, u32[]{:S(2)}) collective-permute-start(bf16[1,16,2048]{2,1,0:T(8,128)(2,1)S(1)} %get-tuple-element.63), channel_id=1, source_target_pairs={{0,24},{2,26},{4,28},{6,30},{8,16},{10,18},{12,20},{14,22},{16,8},... | collective-permute-start | bytes 196616 | tf_op jit(solution)/shard_map/ppermute | solution.py:432

commit v4 on v3

--- a/solution.py
+++ b/solution.py
@@ -28,7 +28,7 @@
     return route
 
 
-def call(body, name, outs, ins, scratch=(), mib=8, cost=10**6):
+def call(body, name, outs, ins, scratch=(), mib=8, cost=10**6, aliases={}):
     return pl.pallas_call(
         body,
         name=name,
@@ -37,6 +37,7 @@
         out_specs=[VMEM] * len(outs),
         scratch_shapes=list(scratch),
         compiler_params=pltpu.CompilerParams(vmem_limit_bytes=mib * 2**20),
+        input_output_aliases=aliases,
         cost_estimate=pl.CostEstimate(flops=cost, bytes_accessed=2**20, transcendentals=0),
     )(*ins)
 
@@ -46,7 +47,10 @@
         self.levels_n, self.height, self.width, self.model = shape
         self.tiles, self.levs = tiles, levs
         self.tall = self.height + 2 * REACH
-        self.compact = levs == 2 and self.levels_n == 2
+        self.compact = levs == 2 and self.levels_n == 2 and self.height == 2 * PAIR
+        self.blocks_n = self.levels_n * self.height // PAIR
+        self.lanes_n = GROUP * self.model // HEADS
+        self.queries_n = GROUP * PAIR * self.width
         self.slots_n = self.levels_n + 2 - self.compact
         self.own = (self.levels_n, self.height, self.width)
         self.wide = (self.slots_n, self.tall, self.width)
@@ -66,6 +70,13 @@
         self.first = 1 - self.off
         self.edge_e = jnp.where(lev_odd == 0, self.levels_n - 1, 0)
         self.edge_o = jnp.where(lev_odd == 0, 0, self.levels_n - 1)
+        if self.compact:
+            far = [(self.edge_o, r0, 2, self.first, 1) for r0 in (0, PAIR)]
+            near = [(self.edge_e, r0, 3, 0, self.off) for r0 in (0, PAIR)]
+            self.blocks = [far[0], near[0], near[1], far[1]]
+        else:
+            rows = range(0, self.height, PAIR)
+            self.blocks = [(l, r0, 3, l, l) for l in range(self.levels_n) for r0 in rows]
 
     def liveness(self, ocean, depth, live):
         tile = lax.axis_index("tile")
@@ -86,6 +97,18 @@
         return live[level * self.tall + row]
 
 
+def stage_cut(plan, state, rows_e, rows_o, sems):
+    top = plan.height - REACH
+    plan.places()
+    at_e, at_o = jnp.where(plan.even, top, 0), jnp.where(plan.even, 0, top)
+    cut_e = pltpu.make_async_copy(state.at[:, pl.ds(at_e, REACH)], rows_e, sems.at[0])
+    cut_o = pltpu.make_async_copy(state.at[:, pl.ds(at_o, REACH)], rows_o, sems.at[1])
+    cut_e.start()
+    cut_o.start()
+    cut_e.wait()
+    cut_o.wait()
+
+
 def stage_own(plan, ocean, depth, state, w_qkv, w_out, cot, *refs):
     near, (qs, us, mid, live) = refs[:-4], refs[-4:]
     height, width, model = plan.own[1:] + (plan.model,)
@@ -112,111 +135,166 @@
         mid[plan.slot_o] = pairs(near[1][plan.edge_e])
 
 
-def stage_attend(plan, sums_n, ocean, depth, state, rows_e, rows_o, qs, us, mid, w_qkv, cot, *refs):
-    sides = 1 if plan.compact else 2
-    lev_in, refs = refs[: 3 * sides], refs[3 * sides :]
-    attn, dq, dkv16 = refs[:3]
-    sums, (ext, kv, dkv, bias, live) = refs[3 : 3 + sums_n], refs[3 + sums_n :]
-    levels_n, height, width = plan.own
-    model, tall = plan.model, plan.tall
+def spread(plan, x):
+    lane_head = lax.broadcasted_iota(jnp.int32, x.shape, 1) // (plan.model // HEADS)
+    return jnp.concatenate(
+        [jnp.where(lane_head == h, x, jnp.zeros_like(x)) for h in range(GROUP)], axis=0
+    )
+
+
+def group_lanes(plan, g):
+    lanes = slice(g * plan.lanes_n, (g + 1) * plan.lanes_n)
+    return lanes, slice(plan.model + lanes.start, plan.model + lanes.stop)
+
+
+def spread_block(plan, x, block, lanes):
+    l, r0 = block[:2]
+    return spread(plan, x[l, r0 : r0 + PAIR, :, lanes].reshape(PAIR * plan.width, plan.lanes_n))
+
+
+def attention(plan, numbers, live, qs, us, kv, bias, prob, grad, attn, dq):
+    width, lanes_n, queries_n = plan.width, plan.lanes_n, plan.queries_n
     span = PAIR + 2 * REACH
-    block = PAIR * width
-    head = model // HEADS
-    lanes_n = GROUP * head
+    block_n = PAIR * width
+    head = plan.model // HEADS
+    lane_head = lax.broadcasted_iota(jnp.int32, (block_n, lanes_n), 1) // head
+    query = lax.broadcasted_iota(jnp.int32, (width, queries_n), 1) % block_n
+    query_row = query // width
+    query_col = query % width
+    key_col = lax.broadcasted_iota(jnp.int32, (width, queries_n), 0)
+    near_col = jnp.abs(key_col - query_col) <= REACH
+
+    def gather(x):
+        total = jnp.where(lane_head == 0, x[:block_n], 0.0)
+        for h in range(1, GROUP):
+            total = jnp.where(lane_head == h, x[h * block_n : (h + 1) * block_n], total)
+        return total
+
+    def scores(slot, number, g):
+        block = plan.blocks[number]
+        l, r0, depth_n, base, _ = block
+        keys_n = depth_n * span * width
+        lanes, lanes_v = group_lanes(plan, g)
+        q = spread_block(plan, qs, block, lanes)
+        u = spread_block(plan, us, block, lanes)
+        k = kv[pl.ds(base, depth_n), r0 : r0 + span, :, lanes].reshape(keys_n, lanes_n)
+        v = kv[pl.ds(base, depth_n), r0 : r0 + span, :, lanes_v].reshape(keys_n, lanes_n)
+        return k, v, dot(k, q, 1, 1) + bias[slot, :keys_n], dot(v, u, 1, 1)
+
+    def weigh(s, dp):
+        e = jnp.exp(s - jnp.max(s, axis=0, keepdims=True))
+        inv = 1.0 / jnp.sum(e, axis=0, keepdims=True)
+        delta = jnp.sum(e * dp, axis=0, keepdims=True) * inv
+        p = e * inv
+        return p.astype(BF16), (p * (dp - delta)).astype(BF16)
+
+    def give(number, g, p16, ds16, k, v):
+        l, r0, depth_n, base, _ = plan.blocks[number]
+        lanes = group_lanes(plan, g)[0]
+        at = slice(number * queries_n, (number + 1) * queries_n)
+        tiled = (depth_n, span, width, queries_n)
+        prob[g, pl.ds(base, depth_n), r0 : r0 + span, :, at] = p16.reshape(tiled)
+        grad[g, pl.ds(base, depth_n), r0 : r0 + span, :, at] = ds16.reshape(tiled)
+        a = gather(dot(p16, v, 0, 0))
+        for r in range(PAIR):
+            alive = plan.alive(live, l + 1, REACH + r0 + r).astype(F32)
+            attn[l, r0 + r, :, lanes] = (a[r * width : (r + 1) * width] * alive).astype(BF16)
+        b = gather(dot(ds16, k, 0, 0)) * (head**-0.5)
+        dq[l, r0 : r0 + PAIR, :, lanes] = b.astype(BF16).reshape(PAIR, width, lanes_n)
+
+    def mask(slot, number):
+        _, r0, depth_n, _, base_level = plan.blocks[number]
+        for dl in range(depth_n):
+            for kr in range(span):
+                alive = plan.alive(live, base_level + dl, r0 + kr) == 1
+                near = near_col & (jnp.abs(query_row + REACH - kr) <= REACH)
+                at = (dl * span + kr) * width
+                bias[slot, at : at + width] = jnp.where(near & alive, 0.0, LOW)
+
+    jobs = []
+    for i, number in enumerate(numbers):
+        mask(i, number)
+        jobs += [(i, number, g) for g in range(HEADS // GROUP)]
+    ready = [scores(*jobs[0])]
+    for i, job in enumerate(jobs):
+        if i + 1 < len(jobs):
+            ready.append(scores(*jobs[i + 1]))
+        k, v, s, dp = ready[i]
+        give(*job[1:], *weigh(s, dp), k, v)
+
+
+def sum_keys(plan, qs, us, prob, grad, dkv16):
+    n = plan.queries_n
+    if plan.compact:
+        own, edge = pl.ds(plan.first, plan.levels_n), pl.ds(plan.slot_e, 1)
+        end = plan.tall
+        parts = [(own, plan.levels_n, 0, PAIR, 0, 2), (own, plan.levels_n, PAIR, end - PAIR, 0, 4)]
+        parts += [(own, plan.levels_n, end - PAIR, end, 2, 4), (edge, 1, 0, PAIR, 1, 2)]
+        parts += [(edge, 1, PAIR, end - PAIR, 1, 3), (edge, 1, end - PAIR, end, 2, 3)]
+    else:
+        parts = [(pl.ds(i, 1), 1, 0, plan.tall, 0, plan.blocks_n) for i in range(plan.slots_n)]
+    for g in range(HEADS // GROUP):
+        lanes, lanes_v = group_lanes(plan, g)
+        for source, weights, at in ((qs, grad, lanes), (us, prob, lanes_v)):
+            x = [spread_block(plan, source, block, lanes) for block in plan.blocks]
+            x = jnp.concatenate(x, axis=0)
+            for slots, slots_n, low, high, k0, k1 in parts:
+                w = weights[g, slots, low:high, :, k0 * n : k1 * n]
+                w = w.reshape(slots_n * (high - low) * plan.width, (k1 - k0) * n)
+                y = dot(w, x[k0 * n : k1 * n], 1, 0).astype(BF16)
+                dkv16[slots, low:high, :, at] = y.reshape(slots_n, high - low, plan.width, plan.lanes_n)
+
+
+def project(plan, slot, ext, mid, w_qkv, kv):
+    height, width = plan.own[1:]
+    model = plan.model
+    edge = REACH * width
+    cells = [ext[slot, :REACH].reshape(edge, model), ext[slot, height + REACH :].reshape(edge, model)]
+    pairs = dot(jnp.concatenate(cells, axis=0), w_qkv[:, model:], 1, 0).astype(BF16)
+    kv[slot, :REACH] = pairs[:edge].reshape(REACH, width, 2 * model)
+    kv[slot, height + REACH :] = pairs[edge:].reshape(REACH, width, 2 * model)
+    kv[slot, REACH : height + REACH] = mid[slot]
+
+
+def stage_inner(plan, ocean, depth, state, rows_e, rows_o, qs, us, mid, w_qkv, *refs):
+    ext, kv, prob, grad, attn, dq, bias, live = refs
+    levels_n, height = plan.own[:2]
     plan.places()
     plan.liveness(ocean, depth, live)
-
     inner = pl.ds(plan.first, levels_n)
     ext[inner, REACH : height + REACH] = state[...]
     ext[inner, pl.ds(plan.at_e, REACH)] = rows_e[...]
     ext[inner, pl.ds(plan.at_o, REACH)] = rows_o[...]
+    for l in range(levels_n):
+        project(plan, plan.first + l, ext, mid, w_qkv, kv)
+    if plan.compact:
+        attention(plan, (0, 3), live, qs, us, kv, bias, prob, grad, attn, dq)
+
+
+def stage_attend(plan, sums_n, ocean, depth, state, qs, us, mid, w_qkv, cot, *refs):
+    sides = 1 if plan.compact else 2
+    lev_in, refs = refs[: 3 * sides], refs[3 * sides + 6 :]
+    ext, kv, prob, grad, attn, dq, dkv16 = refs[:7]
+    sums, (bias, live) = refs[7 : 7 + sums_n], refs[7 + sums_n :]
+    levels_n, height, width = plan.own
+    model, tall = plan.model, plan.tall
+    plan.places()
+    plan.liveness(ocean, depth, live)
     for side, (slot, level) in enumerate(((plan.slot_e, plan.edge_o), (plan.slot_o, plan.edge_e))):
         if side < sides:
             near, far_e, far_o = lev_in[3 * side : 3 * side + 3]
             ext[slot, REACH : height + REACH] = near[level]
             ext[slot, pl.ds(plan.at_e, REACH)] = far_e[level]
             ext[slot, pl.ds(plan.at_o, REACH)] = far_o[level]
-
-    @pl.loop(0, plan.slots_n)
-    def _(l):
-        edge = REACH * width
-        cells = [ext[l, :REACH].reshape(edge, model), ext[l, height + REACH :].reshape(edge, model)]
-        pairs = dot(jnp.concatenate(cells, axis=0), w_qkv[:, model:], 1, 0).astype(BF16)
-        kv[l, :REACH] = pairs[:edge].reshape(REACH, width, 2 * model)
-        kv[l, height + REACH :] = pairs[edge:].reshape(REACH, width, 2 * model)
-        kv[l, REACH : height + REACH] = mid[l]
-        dkv[l] = jnp.zeros((tall, width, 2 * model), F32)
-
-    lane_head = lax.broadcasted_iota(jnp.int32, (block, lanes_n), 1) // head
-    query = lax.broadcasted_iota(jnp.int32, (width, GROUP * block), 1) % block
-    query_row = query // width
-    query_col = query % width
-    key_col = lax.broadcasted_iota(jnp.int32, (width, GROUP * block), 0)
-    near_col = jnp.abs(key_col - query_col) <= REACH
-
-    def spread(x):
-        return jnp.concatenate(
-            [jnp.where(lane_head == h, x, jnp.zeros_like(x)) for h in range(GROUP)], axis=0
-        )
-
-    def gather(x):
-        total = jnp.where(lane_head == 0, x[:block], 0.0)
-        for h in range(1, GROUP):
-            total = jnp.where(lane_head == h, x[h * block : (h + 1) * block], total)
-        return total
-
-    def tile_step(l, r0, depth_n, base, base_level):
-        keys_n = depth_n * span * width
-        for dl in range(depth_n):
-            for kr in range(span):
-                alive = plan.alive(live, base_level + dl, r0 + kr) == 1
-                near = near_col & (jnp.abs(query_row + REACH - kr) <= REACH)
-                at = (dl * span + kr) * width
-                bias[at : at + width] = jnp.where(near & alive, 0.0, LOW)
-        for g in range(HEADS // GROUP):
-            lanes = slice(g * lanes_n, (g + 1) * lanes_n)
-            lanes_v = slice(model + g * lanes_n, model + (g + 1) * lanes_n)
-            q = spread(qs[l, pl.ds(r0, PAIR), :, lanes].reshape(block, lanes_n))
-            u = spread(us[l, pl.ds(r0, PAIR), :, lanes].reshape(block, lanes_n))
-            k = kv[pl.ds(base, depth_n), pl.ds(r0, span), :, lanes].reshape(keys_n, lanes_n)
-            v = kv[pl.ds(base, depth_n), pl.ds(r0, span), :, lanes_v].reshape(keys_n, lanes_n)
-            s = dot(k, q, 1, 1) + bias[:keys_n]
-            e = jnp.exp(s - jnp.max(s, axis=0, keepdims=True))
-            p = e * (1.0 / jnp.sum(e, axis=0, keepdims=True))
-            p16 = p.astype(BF16)
-            dp = dot(v, u, 1, 1)
-            ds = p * (dp - jnp.sum(p * dp, axis=0, keepdims=True))
-            ds16 = ds.astype(BF16)
-            a = gather(dot(p16, v, 0, 0))
-            for r in range(PAIR):
-                alive = plan.alive(live, l + 1, REACH + r0 + r).astype(F32)
-                attn[l, r0 + r, :, lanes] = (a[r * width : (r + 1) * width] * alive).astype(BF16)
-            b = gather(dot(ds16, k, 0, 0)) * (head**-0.5)
-            dq[l, pl.ds(r0, PAIR), :, lanes] = b.astype(BF16).reshape(PAIR, width, lanes_n)
-            dk = dot(ds16, q, 1, 0).reshape(depth_n, span, width, lanes_n)
-            dkv[pl.ds(base, depth_n), pl.ds(r0, span), :, lanes] += dk
-            dv = dot(p16, u, 1, 0).reshape(depth_n, span, width, lanes_n)
-            dkv[pl.ds(base, depth_n), pl.ds(r0, span), :, lanes_v] += dv
-
-    pairs_n = height // PAIR
+            project(plan, slot, ext, mid, w_qkv, kv)
     if plan.compact:
-
-        @pl.loop(0, pairs_n)
-        def _(pair):
-            tile_step(plan.edge_e, pair * PAIR, 3, 0, plan.off)
-            tile_step(plan.edge_o, pair * PAIR, 2, plan.first, 1)
-
+        numbers = (1, 2)
     else:
-
-        @pl.loop(0, levels_n * pairs_n)
-        def _(combo):
-            l = combo // pairs_n
-            tile_step(l, (combo % pairs_n) * PAIR, 3, l, l)
-
-    @pl.loop(0, plan.slots_n)
-    def _(l):
-        dkv16[l] = dkv[l].astype(BF16)
-
+        numbers = range(plan.blocks_n)
+        prob[...] = jnp.zeros(prob.shape, BF16)
+        grad[...] = jnp.zeros(grad.shape, BF16)
+    attention(plan, numbers, live, qs, us, kv, bias, prob, grad, attn, dq)
+    sum_keys(plan, qs, us, prob, grad, dkv16)
     cells = levels_n * height * width
     wide = plan.slots_n * tall * width
 
@@ -274,8 +352,8 @@
         send[...] = acc[...].astype(BF16)
 
 
-def stage_last(plan, own, back_e, back_o, *refs):
-    edges, (d_state, acc) = refs[:-2], refs[-2:]
+def stage_last(plan, parts_n, own, back_e, back_o, x, *refs):
+    parts, edges, (d_state, d_qkv, d_out, acc) = refs[:parts_n], refs[parts_n:-4], refs[-4:]
     plan.places()
     height = plan.height
     acc[...] = own[...]
@@ -285,6 +363,12 @@
     acc[:, pl.ds(jnp.where(plan.even, top, 0), REACH)] += back_e[...].astype(F32)
     acc[:, pl.ds(jnp.where(plan.even, 0, top), REACH)] += back_o[...].astype(F32)
     d_state[...] = acc[...].astype(BF16)
+    y = x[0]
+    for part in parts:
+        y = y + part[0].astype(F32)
+    cut = d_qkv.shape[1]
+    d_qkv[...] = y[:, :cut]
+    d_out[...] = y[:, cut:]
 
 
 def stage_split(parts_n, radix, stride, x, *refs):
@@ -300,16 +384,6 @@
                 own[h] = y
             else:
                 pieces[k - 1][h] = y.astype(BF16)
-
-
-def stage_sum(parts_n, x, *refs):
-    parts, (qkv, rest) = refs[:parts_n], refs[parts_n:]
-    y = x[0]
-    for part in parts:
-        y = y + part[0].astype(F32)
-    cut = qkv.shape[1]
-    qkv[...] = y[:, :cut]
-    rest[...] = y[:, cut:]
 
 
 def digits(count):
@@ -354,11 +428,17 @@
     def swap(block, axis, first):
         return lax.ppermute(block, axis, swap_pairs(lax.axis_size(axis), first))
 
-    top = height - REACH
-    even = lax.rem(lax.axis_index("tile"), 2) == 0
-    rows_e = lax.dynamic_slice_in_dim(state, jnp.where(even, top, 0), REACH, 1)
-    rows_o = lax.dynamic_slice_in_dim(state, jnp.where(even, 0, top), REACH, 1)
-    near = [swap(state, "lev", side) for side in range(sides)]
+    rows_e, rows_o = pl.pallas_call(
+        bind(stage_cut, plan),
+        name="stage_cut",
+        out_shape=[jax.ShapeDtypeStruct(plan.edge, BF16)] * 2,
+        in_specs=[pl.BlockSpec(memory_space=pl.ANY)],
+        out_specs=[VMEM, VMEM],
+        scratch_shapes=[pltpu.SemaphoreType.DMA((2,))],
+        compiler_params=pltpu.CompilerParams(vmem_limit_bytes=2**20),
+    )(state)
+    rows_e, rows_o, held_state = lax.optimization_barrier((rows_e, rows_o, state))
+    near = [swap(held_state, "lev", side) for side in range(sides)]
     rows_e = swap(rows_e, "tile", 0)
     rows_o = swap(rows_o, "tile", 1)
     live = pltpu.SMEM(((plan.levels_n + 2) * plan.tall,), jnp.int32)
@@ -382,20 +462,36 @@
     else:
         sums = [((model, 4 * model), F32)]
     keys_n = 3 * (PAIR + 2 * REACH) * width
-    attn, dq, dkv16, *sums = call(
+    masks_n = 2 if plan.compact else plan.blocks_n
+    masks = pltpu.VMEM((masks_n, keys_n, plan.queries_n), F32)
+    weights = (HEADS // GROUP,) + plan.wide + (plan.blocks_n * plan.queries_n,)
+    carried = [
+        (plan.wide + (model,), BF16),
+        (plan.wide + (2 * model,), BF16),
+        (weights, BF16),
+        (weights, BF16),
+        (own_cells, BF16),
+        (own_cells, BF16),
+    ]
+    held = call(
+        bind(stage_inner, plan),
+        "stage_inner",
+        carried,
+        [ocean, depth, state, rows_e, rows_o, qs, us, mid, w_qkv],
+        [masks, live],
+        mib=16,
+        cost=8 * 10**9,
+    )
+    ins = [ocean, depth, state, qs, us, mid, w_qkv, cotangent, *lev_in, *held]
+    _, _, _, _, attn, dq, dkv16, *sums = call(
         bind(stage_attend, plan, len(sums)),
         "stage_attend",
-        [(own_cells, BF16), (own_cells, BF16), (plan.wide + (2 * model,), BF16)] + sums,
-        [ocean, depth, state, rows_e, rows_o, qs, us, mid, w_qkv, cotangent, *lev_in],
-        [
-            pltpu.VMEM(plan.wide + (model,), BF16),
-            pltpu.VMEM(plan.wide + (2 * model,), BF16),
-            pltpu.VMEM(plan.wide + (2 * model,), F32),
-            pltpu.VMEM((keys_n, GROUP * PAIR * width), F32),
-            live,
-        ],
-        mib=24,
+        carried + [(plan.wide + (2 * model,), BF16)] + sums,
+        ins,
+        [masks, live],
+        mib=20,
         cost=16 * 10**9,
+        aliases={len(ins) - len(held) + i: i for i in range(len(held))},
     )
     edge_kind = (plan.wide[1:] + (model,), BF16)
     out, own, part_e, part_o, *edges = call(
@@ -435,19 +531,13 @@
         if stride == 1:
             send_e, send_o, parts[2] = lax.optimization_barrier((send_e, send_o, parts[2]))
         stride *= radix
-    d_qkv, d_out = call(
-        bind(stage_sum, len(parts)),
-        "stage_sum",
-        [((rows, 3 * model), F32), ((rows, model), F32)],
-        [x, *parts],
-    )
     back_e = swap(send_e, "tile", 0)
     back_o = swap(send_o, "tile", 1)
-    (d_state,) = call(
-        bind(stage_last, plan),
+    d_state, d_qkv, d_out = call(
+        bind(stage_last, plan, len(parts)),
         "stage_last",
-        [(own_cells, BF16)],
-        [own, back_e, back_o, *edges],
+        [(own_cells, BF16), ((rows, 3 * model), F32), ((rows, model), F32)],
+        [own, back_e, back_o, x, *parts, *edges],
         [pltpu.VMEM(own_cells, F32)],
     )
     return (out, d_state, d_qkv, d_out)

time: 63.3 us -> 57.6 us (0.910)
  the two profiles are of different devices: /device:TPU:4 before, /device:TPU:0 now
where the time goes in v4:
time: 57.6 us; the launch traced here: 57.2 us
  starting transfers between devices  19 us (33%)
  Pallas kernels  15.9 us (28%)
  waiting for transfers between devices  14.9 us (26%)
  local copies, waits for them, and re-layouts  6.62 us (11%)
  between operations  0.8 us (1%)
    pallas_call x8, Pallas kernels, call(): pl.pallas_call(body, name=name, out_shape=[jax.ShapeDtypeStruct(shape, ki...  15.7 us
    ppermute x6, waiting for transfers between devices, local(): lax.ppermute(piece, 'tile', xor_route(tiles, (k + 1) * stride))  14.9 us
    ppermute x6, starting transfers between devices, local(): lax.ppermute(piece, 'tile', xor_route(tiles, (k + 1) * stride))  11.3 us
    ppermute x8, starting transfers between devices, swap(): return lax.ppermute(block, axis, swap_pairs(lax.axis_size(axis), first))  7.48 us
    unnamed x24, local copies, waits for them, and re-layouts  6.62 us
  transfers between devices with their start and end apart: 15, of which 3 were waited for; matrix products, arithmetic and copies ran while one was open for 0% of the time, Pallas kernels for 14%

profile of v4, /device:TPU:0, one launch (start us, length us, event | category | flops | bytes accessed | tf_op | source)
XLA Modules:
  0.0 57.2 jit_solution(12306053775193796254)
XLA Ops:
  0.6 0.0 copy-start
  0.6 0.9 %copy-done = bf16[2,4,32,512]{3,2,1,0:T(8,128)(2,1)S(1)} copy-done((bf16[2,4,32,512]{3,2,1,0:T(8,128)(2,1)S(1)}, bf16[2,4,32,512]{3,2,1,0:T(8,128)(2,1)}, u32[]{:S(2)}) %copy-start) | copy-done | bytes 262168
  1.6 0.3 stage_cut.1
  1.9 0.0 copy-start.10
  1.9 0.5 collective-permute-start.2
  2.4 2.6 %collective-permute-start = (bf16[2,3,32,512]{3,2,1,0:T(8,128)(2,1)S(1)}, bf16[2,3,32,512]{3,2,1,0:T(8,128)(2,1)S(1)}, u32[]{:S(2)}, u32[]{:S(2)}) collective-permute-start(bf16[2,3,32,512]{3,2,1,0:T(8,128)(2,1)S(1)} %get-tuple-element.49), channel_id=1, source_target_pairs={{0,2},{2,0},{4,6},{6,4},{8,10},{10,8},{12,14},{14,12},{16,18},{18,... | collective-permute-start | bytes 589832 | tf_op jit(solution)/shard_map/ppermute | solution.py:429
  4.9 0.7 %collective-permute-start.1 = (bf16[2,3,32,512]{3,2,1,0:T(8,128)(2,1)S(1)}, bf16[2,3,32,512]{3,2,1,0:T(8,128)(2,1)S(1)}, u32[]{:S(2)}, u32[]{:S(2)}) collective-permute-start(bf16[2,3,32,512]{3,2,1,0:T(8,128)(2,1)S(1)} %get-tuple-element.50), channel_id=1, source_target_pairs={{2,4},{4,2},{6,8},{8,6},{10,12},{12,10},{14,16},{16,14},{18,20},{2... | collective-permute-start | bytes 589832 | tf_op jit(solution)/shard_map/ppermute | solution.py:429
  5.6 0.0 collective-permute-done.2.refs_6_.refs_8_
  5.6 0.0 copy-start.1
  5.6 0.9 %copy-done.1 = bf16[2,4,32,512]{3,2,1,0:T(8,128)(2,1)S(1)} copy-done((bf16[2,4,32,512]{3,2,1,0:T(8,128)(2,1)S(1)}, bf16[2,4,32,512]{3,2,1,0:T(8,128)(2,1)}, u32[]{:S(2)}) %copy-start.1) | copy-done | bytes 262168
  6.6 1.4 %copy-done.3 = bf16[512,1536]{1,0:T(8,128)(2,1)S(1)} copy-done((bf16[512,1536]{1,0:T(8,128)(2,1)S(1)}, bf16[512,1536]{1,0:T(8,128)(2,1)}, u32[]{:S(2)}) %copy-start.3) | copy-done | bytes 1572888
  8.0 1.0 %copy-done.5 = bf16[512,512]{1,0:T(8,128)(2,1)S(1)} copy-done((bf16[512,512]{1,0:T(8,128)(2,1)S(1)}, bf16[512,512]{1,0:T(8,128)(2,1)}, u32[]{:S(2)}) %copy-start.5) | copy-done | bytes 524312
  9.0 0.9 %copy-done.7 = bf16[2,4,32,512]{3,2,1,0:T(8,128)(2,1)S(1)} copy-done((bf16[2,4,32,512]{3,2,1,0:T(8,128)(2,1)S(1)}, bf16[2,4,32,512]{3,2,1,0:T(8,128)(2,1)}, u32[]{:S(2)}) %copy-start.7) | copy-done | bytes 262168
  10.0 0.7 %copy-done.9 = s32[16]{0:T(128)S(1)} copy-done((s32[16]{0:T(128)S(1)}, s32[16]{0:T(128)}, u32[]{:S(2)}) %copy-start.9) | copy-done | bytes 88
  10.6 0.7 %copy-done.11 = s32[16]{0:T(128)S(1)} copy-done((s32[16]{0:T(128)S(1)}, s32[16]{0:T(128)}, u32[]{:S(2)}) %copy-start.11) | copy-done | bytes 88
  11.3 1.6 %stage_own.1 = (bf16[2,4,32,512]{3,2,1,0:T(8,128)(2,1)S(1)}, bf16[2,4,32,512]{3,2,1,0:T(8,128)(2,1)S(1)}, bf16[3,4,32,1024]{3,2,1,0:T(8,128)(2,1)S(1)}) custom-call(s32[16]{0:T(128)S(1)} %copy-done.9, s32[16]{0:T(128)S(1)} %copy-done.11, bf16[2,4,32,512]{3,2,1,0:T(8,128)(2,1)S(1)} %copy-done.1, bf16[512,1536]{1,0:T(8,128)(2,1)S(1)} %copy-done.3, ...), custom_call_target="tpu_custom_call" | custom-call | flops 4000000000 | bytes 1048576 | tf_op jit(solution)/shard_map/stage_own/pallas_call | solution.py:32
  12.9 0.0 collective-permute-done.refs_3_
  12.9 0.0 collective-permute-done.1.refs_4_
  12.9 0.2 collective-permute-start.3
  13.2 0.3 collective-permute-start.4
  13.5 3.3 %stage_inner.1 = (bf16[3,10,32,512]{3,2,1,0:T(8,128)(2,1)S(1)}, bf16[3,10,32,1024]{3,2,1,0:T(8,128)(2,1)S(1)}, bf16[2,3,10,32,1024]{4,3,2,1,0:T(8,128)(2,1)S(1)}...) custom-call(s32[16]{0:T(128)S(1)} %copy-done.10, ...), custom_call_target="tpu_custom_call" | custom-call | flops 8000000000 | bytes 1048576 | tf_op jit(solution)/shard_map/stage_inner/pallas_call | solution.py:32
  16.8 0.0 collective-permute-done.3.refs_9_
  16.9 0.0 collective-permute-done.4.refs_10_
  16.9 0.0 copy-start.6
  16.9 6.9 %stage_attend.1 = (bf16[3,10,32,512]{3,2,1,0:T(8,128)(2,1)S(1)}, bf16[3,10,32,1024]{3,2,1,0:T(8,128)(2,1)S(1)}, bf16[2,3,10,32,1024]{4,3,2,1,0:T(8,128)(2,1)S(1)...) custom-call(s32[16]{0:T(128)S(1)} %copy-done.10, ...), custom_call_target="tpu_custom_call", output_to_operand_aliasing={{0}: (11, {}), {1}: (12, {}), {2}: (13, {}), {3}: (14, {}),... | custom-call | flops 16000000000 | bytes 1048576 | tf_op jit(solution)/shard_map/stage_attend/pallas_call | solution.py:32
  23.8 0.2 collective-permute-start.6
  24.1 2.5 %stage_out.1 = (bf16[2,4,32,512]{3,2,1,0:T(8,128)(2,1)}, f32[2,4,32,512]{3,2,1,0:T(8,128)S(1)}, f32[2,3,32,512]{3,2,1,0:T(8,128)S(1)}, f32[2,3,32,512]{3,2,1,0:T(8,128)S(1)}, bf16[10,32,512]{2,1,0:T(8,128)(2,1)S(1)}) custom-call(bf16[2,4,32,512]{3,2,1,0:T(8,128)(2,1)S(1)} %copy-done.2, bf16[2,4,32,512]{3,2,1,0:T(8,128)(2,1)S(1)} %copy-done.8, ...), custom_call_target="tpu_custom_call" | custom-call | flops 4000000000 | bytes 1048576 | tf_op jit(solution)/shard_map/stage_out/pallas_call | solution.py:32
  26.5 0.3 collective-permute-start.5
  26.9 0.0 collective-permute-done.6.refs_1_
  26.9 0.2 stage_split.2
  27.1 5.2 %collective-permute-start.7 = (bf16[4,16,2048]{2,1,0:T(8,128)(2,1)S(1)}, bf16[4,16,2048]{2,1,0:T(8,128)(2,1)S(1)}, u32[]{:S(2)}, u32[]{:S(2)}) collective-permute-start(bf16[4,16,2048]{2,1,0:T(8,128)(2,1)S(1)} %get-tuple-element.76), channel_id=1, source_target_pairs={{0,6},{2,4},{4,2},{6,0},{8,14},{10,12},{12,10},{14,8},{16,22},{18,... | collective-permute-start | bytes 786440 | tf_op jit(solution)/shard_map/ppermute | solution.py:528
  32.3 0.0 collective-permute-start.10
  32.3 0.7 %collective-permute-start.11 = (bf16[4,16,2048]{2,1,0:T(8,128)(2,1)S(1)}, bf16[4,16,2048]{2,1,0:T(8,128)(2,1)S(1)}, u32[]{:S(2)}, u32[]{:S(2)}) collective-permute-start(bf16[4,16,2048]{2,1,0:T(8,128)(2,1)S(1)} %get-tuple-element.81), channel_id=1, source_target_pairs={{0,4},{2,6},{4,0},{6,2},{8,12},{10,14},{12,8},{14,10},{16,20},{18,... | collective-permute-start | bytes 786440 | tf_op jit(solution)/shard_map/ppermute | solution.py:528
  33.0 0.0 collective-permute-done.5.refs_2_.refs_7_
  33.0 0.1 stage_fold.1
  33.1 6.3 %collective-permute-done.7.refs_3_ = bf16[4,16,2048]{2,1,0:T(8,128)(2,1)S(1)} collective-permute-done((bf16[4,16,2048]{2,1,0:T(8,128)(2,1)S(1)}, bf16[4,16,2048]{2,1,0:T(8,128)(2,1)S(1)}, u32[]{:S(2)}, u32[]{:S(2)}) %collective-permute-start.7) | collective-permute-done | bytes 262176 | tf_op jit(solution)/shard_map/ppermute | solution.py:528
  39.4 2.2 %collective-permute-start.8 = (bf16[2,3,32,512]{3,2,1,0:T(8,128)(2,1)S(1)}, bf16[2,3,32,512]{3,2,1,0:T(8,128)(2,1)S(1)}, u32[]{:S(2)}, u32[]{:S(2)}) collective-permute-start(bf16[2,3,32,512]{3,2,1,0:T(8,128)(2,1)S(1)} %get-tuple-element.77), channel_id=1, source_target_pairs={{0,2},{2,0},{4,6},{6,4},{8,10},{10,8},{12,14},{14,12},{16,18},{18,... | collective-permute-start | bytes 589832 | tf_op jit(solution)/shard_map/ppermute | solution.py:429
  41.6 0.7 %collective-permute-start.9 = (bf16[2,3,32,512]{3,2,1,0:T(8,128)(2,1)S(1)}, bf16[2,3,32,512]{3,2,1,0:T(8,128)(2,1)S(1)}, u32[]{:S(2)}, u32[]{:S(2)}) collective-permute-start(bf16[2,3,32,512]{3,2,1,0:T(8,128)(2,1)S(1)} %get-tuple-element.78), channel_id=1, source_target_pairs={{2,4},{4,2},{6,8},{8,6},{10,12},{12,10},{14,16},{16,14},{18,20},{2... | collective-permute-start | bytes 589832 | tf_op jit(solution)/shard_map/ppermute | solution.py:429
  42.3 4.5 %collective-permute-done.10.refs_1_ = bf16[4,16,2048]{2,1,0:T(8,128)(2,1)S(1)} collective-permute-done((bf16[4,16,2048]{2,1,0:T(8,128)(2,1)S(1)}, bf16[4,16,2048]{2,1,0:T(8,128)(2,1)S(1)}, u32[]{:S(2)}, u32[]{:S(2)}) %collective-permute-start.10) | collective-permute-done | bytes 262176 | tf_op jit(solution)/shard_map/ppermute | solution.py:528
  46.7 0.1 stage_split.3
  46.8 2.9 %collective-permute-start.12 = (bf16[1,16,2048]{2,1,0:T(8,128)(2,1)S(1)}, bf16[1,16,2048]{2,1,0:T(8,128)(2,1)S(1)}, u32[]{:S(2)}, u32[]{:S(2)}) collective-permute-start(bf16[1,16,2048]{2,1,0:T(8,128)(2,1)S(1)} %get-tuple-element.84), channel_id=1, source_target_pairs={{0,8},{2,10},{4,12},{6,14},{8,0},{10,2},{12,4},{14,6},{16,24},{18,... | collective-permute-start | bytes 196616 | tf_op jit(solution)/shard_map/ppermute | solution.py:528
  49.8 0.0 collective-permute-start.13
  49.8 2.4 %collective-permute-start.14 = (bf16[1,16,2048]{2,1,0:T(8,128)(2,1)S(1)}, bf16[1,16,2048]{2,1,0:T(8,128)(2,1)S(1)}, u32[]{:S(2)}, u32[]{:S(2)}) collective-permute-start(bf16[1,16,2048]{2,1,0:T(8,128)(2,1)S(1)} %get-tuple-element.86), channel_id=1, source_target_pairs={{0,24},{2,26},{4,28},{6,30},{8,16},{10,18},{12,20},{14,22},{16,8},... | collective-permute-start | bytes 196616 | tf_op jit(solution)/shard_map/ppermute | solution.py:528
  52.2 0.0 collective-permute-done.12.refs_4_
  52.2 4.1 %collective-permute-done.13.refs_5_ = bf16[1,16,2048]{2,1,0:T(8,128)(2,1)S(1)} collective-permute-done((bf16[1,16,2048]{2,1,0:T(8,128)(2,1)S(1)}, bf16[1,16,2048]{2,1,0:T(8,128)(2,1)S(1)}, u32[]{:S(2)}, u32[]{:S(2)}) %collective-permute-start.13) | collective-permute-done | bytes 65568 | tf_op jit(solution)/shard_map/ppermute | solution.py:528
  56.3 0.0 collective-permute-done.8.refs_1_
  56.3 0.0 collective-permute-done.9.refs_2_
  56.3 0.9 %stage_last.1 = (bf16[2,4,32,512]{3,2,1,0:T(8,128)(2,1)}, f32[16,1536]{1,0:T(8,128)}, f32[16,512]{1,0:T(8,128)}) custom-call(f32[2,4,32,512]{3,2,1,0:T(8,128)S(1)} %get-tuple-element.68.refs_0_, bf16[2,3,32,512]{3,2,1,0:T(8,128)(2,1)S(1)} %collective-permute-done.8.refs_1_, bf16[2,3,32,512]{3,2,1,0:T(8,128)(2,1)S(1)} %collective-permute-done.9.refs_2_, ...), custom_call_target="tpu_custom_call" | custom-call | flops 1000000 | bytes 1048576 | tf_op jit(solution)/shard_map/stage_last/pallas_call | solution.py:32
  (15 shorter events, 0.0 us)
Async XLA Ops:
  0.6 1.0 %copy-start = (bf16[2,4,32,512]{3,2,1,0:T(8,128)(2,1)S(1)}, bf16[2,4,32,512]{3,2,1,0:T(8,128)(2,1)}, u32[]{:S(2)}) copy-start(bf16[2,4,32,512]{3,2,1,0:T(8,128)(2,1)} %refs_0_.9) | copy-start | bytes 786436
  1.6 11.9 %copy-start.2 = (bf16[2,4,32,512]{3,2,1,0:T(8,128)(2,1)S(1)}, bf16[2,4,32,512]{3,2,1,0:T(8,128)(2,1)}, u32[]{:S(2)}) copy-start(bf16[2,4,32,512]{3,2,1,0:T(8,128)(2,1)} %refs_0_.9) | copy-start | bytes 786436
  1.9 11.7 %copy-start.10 = (s32[16]{0:T(128)S(1)}, s32[16]{0:T(128)}, u32[]{:S(2)}) copy-start(s32[16]{0:T(128)} %refs_0_.8) | copy-start | bytes 196
  1.9 3.8 %collective-permute-start.2 = (bf16[2,4,32,512]{3,2,1,0:T(8,128)(2,1)S(1)}, bf16[2,4,32,512]{3,2,1,0:T(8,128)(2,1)S(1)}, u32[]{:S(2)}, u32[]{:S(2)}) collective-permute-start(bf16[2,4,32,512]{3,2,1,0:T(8,128)(2,1)S(1)} %copy-done), channel_id=1, source_target_pairs={{0,1},{1,0},{2,3},{3,2},{4,5},{5,4},{6,7},{7,6},{8,9},{9,8},{10,11... | collective-permute-start | bytes 786440 | tf_op jit(solution)/shard_map/ppermute | solution.py:429
  2.4 10.5 %collective-permute-start = (bf16[2,3,32,512]{3,2,1,0:T(8,128)(2,1)S(1)}, bf16[2,3,32,512]{3,2,1,0:T(8,128)(2,1)S(1)}, u32[]{:S(2)}, u32[]{:S(2)}) collective-permute-start(bf16[2,3,32,512]{3,2,1,0:T(8,128)(2,1)S(1)} %get-tuple-element.49), channel_id=1, source_target_pairs={{0,2},{2,0},{4,6},{6,4},{8,10},{10,8},{12,14},{14,12},{16,18},{18,... | collective-permute-start | bytes 589832 | tf_op jit(solution)/shard_map/ppermute | solution.py:429
  4.9 8.0 %collective-permute-start.1 = (bf16[2,3,32,512]{3,2,1,0:T(8,128)(2,1)S(1)}, bf16[2,3,32,512]{3,2,1,0:T(8,128)(2,1)S(1)}, u32[]{:S(2)}, u32[]{:S(2)}) collective-permute-start(bf16[2,3,32,512]{3,2,1,0:T(8,128)(2,1)S(1)} %get-tuple-element.50), channel_id=1, source_target_pairs={{2,4},{4,2},{6,8},{8,6},{10,12},{12,10},{14,16},{16,14},{18,20},{2... | collective-permute-start | bytes 589832 | tf_op jit(solution)/shard_map/ppermute | solution.py:429
  5.6 1.0 %copy-start.1 = (bf16[2,4,32,512]{3,2,1,0:T(8,128)(2,1)S(1)}, bf16[2,4,32,512]{3,2,1,0:T(8,128)(2,1)}, u32[]{:S(2)}) copy-start(bf16[2,4,32,512]{3,2,1,0:T(8,128)(2,1)} %refs_0_.9) | copy-start | bytes 786436
  6.6 1.4 %copy-start.3 = (bf16[512,1536]{1,0:T(8,128)(2,1)S(1)}, bf16[512,1536]{1,0:T(8,128)(2,1)}, u32[]{:S(2)}) copy-start(bf16[512,1536]{1,0:T(8,128)(2,1)} %refs_5_.3) | copy-start | bytes 4718596
  8.0 1.0 %copy-start.5 = (bf16[512,512]{1,0:T(8,128)(2,1)S(1)}, bf16[512,512]{1,0:T(8,128)(2,1)}, u32[]{:S(2)}) copy-start(bf16[512,512]{1,0:T(8,128)(2,1)} %refs_6_.3) | copy-start | bytes 1572868
  9.0 0.9 %copy-start.7 = (bf16[2,4,32,512]{3,2,1,0:T(8,128)(2,1)S(1)}, bf16[2,4,32,512]{3,2,1,0:T(8,128)(2,1)}, u32[]{:S(2)}) copy-start(bf16[2,4,32,512]{3,2,1,0:T(8,128)(2,1)} %refs_1_.7) | copy-start | bytes 786436
  10.0 0.7 %copy-start.9 = (s32[16]{0:T(128)S(1)}, s32[16]{0:T(128)}, u32[]{:S(2)}) copy-start(s32[16]{0:T(128)} %refs_0_.8) | copy-start | bytes 196
  10.6 0.7 %copy-start.11 = (s32[16]{0:T(128)S(1)}, s32[16]{0:T(128)}, u32[]{:S(2)}) copy-start(s32[16]{0:T(128)} %refs_1_.6) | copy-start | bytes 196
  11.3 2.2 %copy-start.4 = (bf16[512,1536]{1,0:T(8,128)(2,1)S(1)}, bf16[512,1536]{1,0:T(8,128)(2,1)}, u32[]{:S(2)}) copy-start(bf16[512,1536]{1,0:T(8,128)(2,1)} %refs_5_.3) | copy-start | bytes 4718596
  12.9 3.9 %collective-permute-start.3 = (bf16[2,3,32,512]{3,2,1,0:T(8,128)(2,1)S(1)}, bf16[2,3,32,512]{3,2,1,0:T(8,128)(2,1)S(1)}, u32[]{:S(2)}, u32[]{:S(2)}) collective-permute-start(bf16[2,3,32,512]{3,2,1,0:T(8,128)(2,1)S(1)} %collective-permute-done.refs_3_), channel_id=1, source_target_pairs={{0,1},{1,0},{2,3},{3,2},{4,5},{5,4},{6,7},{7,6},{8,9},{9,8},{10,11... | collective-permute-start | bytes 589832 | tf_op jit(solution)/shard_map/ppermute | solution.py:429
  13.2 3.7 %collective-permute-start.4 = (bf16[2,3,32,512]{3,2,1,0:T(8,128)(2,1)S(1)}, bf16[2,3,32,512]{3,2,1,0:T(8,128)(2,1)S(1)}, u32[]{:S(2)}, u32[]{:S(2)}) collective-permute-start(bf16[2,3,32,512]{3,2,1,0:T(8,128)(2,1)S(1)} %collective-permute-done.1.refs_4_), channel_id=1, source_target_pairs={{0,1},{1,0},{2,3},{3,2},{4,5},{5,4},{6,7},{7,6},{8,9},{9,8},{10,11... | collective-permute-start | bytes 589832 | tf_op jit(solution)/shard_map/ppermute | solution.py:429
  13.5 3.3 %copy-start.8 = (bf16[2,4,32,512]{3,2,1,0:T(8,128)(2,1)S(1)}, bf16[2,4,32,512]{3,2,1,0:T(8,128)(2,1)}, u32[]{:S(2)}) copy-start(bf16[2,4,32,512]{3,2,1,0:T(8,128)(2,1)} %refs_1_.7) | copy-start | bytes 786436
  16.9 7.2 %copy-start.6 = (bf16[512,512]{1,0:T(8,128)(2,1)S(1)}, bf16[512,512]{1,0:T(8,128)(2,1)}, u32[]{:S(2)}) copy-start(bf16[512,512]{1,0:T(8,128)(2,1)} %refs_6_.3) | copy-start | bytes 1572868
  23.8 3.1 %collective-permute-start.6 = (bf16[16,16,2048]{2,1,0:T(8,128)(2,1)S(1)}, bf16[16,16,2048]{2,1,0:T(8,128)(2,1)S(1)}, u32[]{:S(2)}, u32[]{:S(2)}) collective-permute-start(bf16[16,16,2048]{2,1,0:T(8,128)(2,1)S(1)} %get-tuple-element.75), channel_id=1, source_target_pairs={{0,1},{1,0},{2,3},{3,2},{4,5},{5,4},{6,7},{7,6},{8,9},{9,8},{10,11... | collective-permute-start | bytes 3145736 | tf_op jit(solution)/shard_map/ppermute | solution.py:515
  26.5 6.4 %collective-permute-start.5 = (bf16[10,32,512]{2,1,0:T(8,128)(2,1)S(1)}, bf16[10,32,512]{2,1,0:T(8,128)(2,1)S(1)}, u32[]{:S(2)}, u32[]{:S(2)}) collective-permute-start(bf16[10,32,512]{2,1,0:T(8,128)(2,1)S(1)} %get-tuple-element.71), channel_id=1, source_target_pairs={{0,1},{1,0},{2,3},{3,2},{4,5},{5,4},{6,7},{7,6},{8,9},{9,8},{10,11... | collective-permute-start | bytes 983048 | tf_op jit(solution)/shard_map/ppermute | solution.py:429
  27.1 12.4 %collective-permute-start.7 = (bf16[4,16,2048]{2,1,0:T(8,128)(2,1)S(1)}, bf16[4,16,2048]{2,1,0:T(8,128)(2,1)S(1)}, u32[]{:S(2)}, u32[]{:S(2)}) collective-permute-start(bf16[4,16,2048]{2,1,0:T(8,128)(2,1)S(1)} %get-tuple-element.76), channel_id=1, source_target_pairs={{0,6},{2,4},{4,2},{6,0},{8,14},{10,12},{12,10},{14,8},{16,22},{18,... | collective-permute-start | bytes 786440 | tf_op jit(solution)/shard_map/ppermute | solution.py:528
  32.3 14.4 %collective-permute-start.10 = (bf16[4,16,2048]{2,1,0:T(8,128)(2,1)S(1)}, bf16[4,16,2048]{2,1,0:T(8,128)(2,1)S(1)}, u32[]{:S(2)}, u32[]{:S(2)}) collective-permute-start(bf16[4,16,2048]{2,1,0:T(8,128)(2,1)S(1)} %get-tuple-element.80), channel_id=1, source_target_pairs={{0,2},{2,0},{4,6},{6,4},{8,10},{10,8},{12,14},{14,12},{16,18},{18,... | collective-permute-start | bytes 786440 | tf_op jit(solution)/shard_map/ppermute | solution.py:528
  32.3 14.4 %collective-permute-start.11 = (bf16[4,16,2048]{2,1,0:T(8,128)(2,1)S(1)}, bf16[4,16,2048]{2,1,0:T(8,128)(2,1)S(1)}, u32[]{:S(2)}, u32[]{:S(2)}) collective-permute-start(bf16[4,16,2048]{2,1,0:T(8,128)(2,1)S(1)} %get-tuple-element.81), channel_id=1, source_target_pairs={{0,4},{2,6},{4,0},{6,2},{8,12},{10,14},{12,8},{14,10},{16,20},{18,... | collective-permute-start | bytes 786440 | tf_op jit(solution)/shard_map/ppermute | solution.py:528
  39.4 16.9 %collective-permute-start.8 = (bf16[2,3,32,512]{3,2,1,0:T(8,128)(2,1)S(1)}, bf16[2,3,32,512]{3,2,1,0:T(8,128)(2,1)S(1)}, u32[]{:S(2)}, u32[]{:S(2)}) collective-permute-start(bf16[2,3,32,512]{3,2,1,0:T(8,128)(2,1)S(1)} %get-tuple-element.77), channel_id=1, source_target_pairs={{0,2},{2,0},{4,6},{6,4},{8,10},{10,8},{12,14},{14,12},{16,18},{18,... | collective-permute-start | bytes 589832 | tf_op jit(solution)/shard_map/ppermute | solution.py:429
  41.6 14.7 %collective-permute-start.9 = (bf16[2,3,32,512]{3,2,1,0:T(8,128)(2,1)S(1)}, bf16[2,3,32,512]{3,2,1,0:T(8,128)(2,1)S(1)}, u32[]{:S(2)}, u32[]{:S(2)}) collective-permute-start(bf16[2,3,32,512]{3,2,1,0:T(8,128)(2,1)S(1)} %get-tuple-element.78), channel_id=1, source_target_pairs={{2,4},{4,2},{6,8},{8,6},{10,12},{12,10},{14,16},{16,14},{18,20},{2... | collective-permute-start | bytes 589832 | tf_op jit(solution)/shard_map/ppermute | solution.py:429
  46.8 5.4 %collective-permute-start.12 = (bf16[1,16,2048]{2,1,0:T(8,128)(2,1)S(1)}, bf16[1,16,2048]{2,1,0:T(8,128)(2,1)S(1)}, u32[]{:S(2)}, u32[]{:S(2)}) collective-permute-start(bf16[1,16,2048]{2,1,0:T(8,128)(2,1)S(1)} %get-tuple-element.84), channel_id=1, source_target_pairs={{0,8},{2,10},{4,12},{6,14},{8,0},{10,2},{12,4},{14,6},{16,24},{18,... | collective-permute-start | bytes 196616 | tf_op jit(solution)/shard_map/ppermute | solution.py:528
  49.8 6.6 %collective-permute-start.13 = (bf16[1,16,2048]{2,1,0:T(8,128)(2,1)S(1)}, bf16[1,16,2048]{2,1,0:T(8,128)(2,1)S(1)}, u32[]{:S(2)}, u32[]{:S(2)}) collective-permute-start(bf16[1,16,2048]{2,1,0:T(8,128)(2,1)S(1)} %get-tuple-element.85), channel_id=1, source_target_pairs={{0,16},{2,18},{4,20},{6,22},{8,24},{10,26},{12,28},{14,30},{16,0},... | collective-permute-start | bytes 196616 | tf_op jit(solution)/shard_map/ppermute | solution.py:528
  49.8 6.6 %collective-permute-start.14 = (bf16[1,16,2048]{2,1,0:T(8,128)(2,1)S(1)}, bf16[1,16,2048]{2,1,0:T(8,128)(2,1)S(1)}, u32[]{:S(2)}, u32[]{:S(2)}) collective-permute-start(bf16[1,16,2048]{2,1,0:T(8,128)(2,1)S(1)} %get-tuple-element.86), channel_id=1, source_target_pairs={{0,24},{2,26},{4,28},{6,30},{8,16},{10,18},{12,20},{14,22},{16,8},... | collective-permute-start | bytes 196616 | tf_op jit(solution)/shard_map/ppermute | solution.py:528

commit v5 on v4

--- a/solution.py
+++ b/solution.py
@@ -97,16 +97,18 @@
         return live[level * self.tall + row]
 
 
-def stage_cut(plan, state, rows_e, rows_o, sems):
+def stage_cut(plan, state, rows_e, rows_o, *refs):
+    near, sems = refs[:-1], refs[-1]
     top = plan.height - REACH
     plan.places()
     at_e, at_o = jnp.where(plan.even, top, 0), jnp.where(plan.even, 0, top)
-    cut_e = pltpu.make_async_copy(state.at[:, pl.ds(at_e, REACH)], rows_e, sems.at[0])
-    cut_o = pltpu.make_async_copy(state.at[:, pl.ds(at_o, REACH)], rows_o, sems.at[1])
-    cut_e.start()
-    cut_o.start()
-    cut_e.wait()
-    cut_o.wait()
+    cuts = [(state.at[:, pl.ds(at_e, REACH)], rows_e), (state.at[:, pl.ds(at_o, REACH)], rows_o)]
+    cuts += [(state.at[level], edge) for level, edge in zip((plan.edge_e, plan.edge_o), near)]
+    copies = [pltpu.make_async_copy(a, b, sems.at[i]) for i, (a, b) in enumerate(cuts)]
+    for copy in copies:
+        copy.start()
+    for copy in copies:
+        copy.wait()
 
 
 def stage_own(plan, ocean, depth, state, w_qkv, w_out, cot, *refs):
@@ -130,9 +132,9 @@
         u = u.reshape(height, width, model)
         for r in range(height):
             us[l, r] = u[r] * plan.alive(live, l + 1, REACH + r).astype(F32).astype(BF16)
-    mid[plan.slot_e] = pairs(near[0][plan.edge_o])
+    mid[plan.slot_e] = pairs(near[0][...])
     if not plan.compact:
-        mid[plan.slot_o] = pairs(near[1][plan.edge_e])
+        mid[plan.slot_o] = pairs(near[1][...])
 
 
 def spread(plan, x):
@@ -256,17 +258,27 @@
     kv[slot, REACH : height + REACH] = mid[slot]
 
 
-def stage_inner(plan, ocean, depth, state, rows_e, rows_o, qs, us, mid, w_qkv, *refs):
-    ext, kv, prob, grad, attn, dq, bias, live = refs
-    levels_n, height = plan.own[:2]
+def place_rows(plan, rows, at, w_qkv, ext, kv):
+    slots = pl.ds(plan.first, plan.levels_n)
+    ext[slots, pl.ds(at, REACH)] = rows[...]
+    flat = rows[...].reshape(plan.levels_n * REACH * plan.width, plan.model)
+    pairs = dot(flat, w_qkv[:, plan.model :], 1, 0).astype(BF16)
+    kv[slots, pl.ds(at, REACH)] = pairs.reshape(plan.levels_n, REACH, plan.width, 2 * plan.model)
+
+
+def stage_side(plan, state, rows_e, mid, w_qkv, ext, kv):
+    plan.places()
+    slots = pl.ds(plan.first, plan.levels_n)
+    ext[slots, REACH : plan.height + REACH] = state[...]
+    kv[slots, REACH : plan.height + REACH] = mid[slots]
+    place_rows(plan, rows_e, plan.at_e, w_qkv, ext, kv)
+
+
+def stage_inner(plan, ocean, depth, rows_o, qs, us, w_qkv, *refs):
+    ext, kv, prob, grad, attn, dq, bias, live = refs[2:]
     plan.places()
     plan.liveness(ocean, depth, live)
-    inner = pl.ds(plan.first, levels_n)
-    ext[inner, REACH : height + REACH] = state[...]
-    ext[inner, pl.ds(plan.at_e, REACH)] = rows_e[...]
-    ext[inner, pl.ds(plan.at_o, REACH)] = rows_o[...]
-    for l in range(levels_n):
-        project(plan, plan.first + l, ext, mid, w_qkv, kv)
+    place_rows(plan, rows_o, plan.at_o, w_qkv, ext, kv)
     if plan.compact:
         attention(plan, (0, 3), live, qs, us, kv, bias, prob, grad, attn, dq)
 
@@ -283,7 +295,7 @@
     for side, (slot, level) in enumerate(((plan.slot_e, plan.edge_o), (plan.slot_o, plan.edge_e))):
         if side < sides:
             near, far_e, far_o = lev_in[3 * side : 3 * side + 3]
-            ext[slot, REACH : height + REACH] = near[level]
+            ext[slot, REACH : height + REACH] = near[...]
             ext[slot, pl.ds(plan.at_e, REACH)] = far_e[level]
             ext[slot, pl.ds(plan.at_o, REACH)] = far_o[level]
             project(plan, slot, ext, mid, w_qkv, kv)
@@ -317,11 +329,10 @@
         emit((j + 1) * model, dot(ext[...].reshape(wide, model), part, 0, 0))
 
 
-def stage_out(plan, state, cot, attn, dq, dkv16, w_qkv, w_out, out, own, rows_e, rows_o, *refs):
+def stage_out(plan, dkv16, w_qkv, inner, rows_e, rows_o, *refs):
     edges, tmp = refs[:-1], refs[-1]
     levels_n, height, width = plan.own
     model, tall = plan.model, plan.tall
-    cells = height * width
     plan.places()
 
     def back(slot):
@@ -334,22 +345,27 @@
         tmp[...] = back(plan.first + l)
         rows_e[l] = tmp[pl.ds(plan.at_e, REACH)]
         rows_o[l] = tmp[pl.ds(plan.at_o, REACH)]
-        x = cot[l].reshape(cells, model).astype(F32)
-        x = x + dot(dq[l].reshape(cells, model), w_qkv[:, :model], 1, 1)
-        own[l] = x.reshape(height, width, model) + tmp[REACH : REACH + height]
-        x = state[l].reshape(cells, model).astype(F32)
-        x = x + dot(attn[l].reshape(cells, model), w_out[...], 1, 0)
-        out[l] = x.astype(BF16).reshape(height, width, model)
-
-
-def stage_fold(plan, rows_e, rows_o, *refs):
-    edges, (send_e, send_o, acc) = refs[:-3], refs[-3:]
+        inner[l] = tmp[REACH : REACH + height]
+
+
+def stage_fold(plan, rows_e, rows_o, inner, state, cot, attn, dq, w_qkv, w_out, *refs):
+    edges, (send_e, send_o, out, own, acc) = refs[:-5], refs[-5:]
+    levels_n, height, width = plan.own
+    model = plan.model
+    cells = height * width
     plan.places()
     for rows, at, send in ((rows_e, plan.at_e, send_e), (rows_o, plan.at_o, send_o)):
         acc[...] = rows[...]
         for edge, level in zip(edges, (plan.edge_e, plan.edge_o)):
             acc[level] += edge[pl.ds(at, REACH)].astype(F32)
         send[...] = acc[...].astype(BF16)
+    for l in range(levels_n):
+        x = cot[l].reshape(cells, model).astype(F32)
+        x = x + dot(dq[l].reshape(cells, model), w_qkv[:, :model], 1, 1)
+        own[l] = x.reshape(height, width, model) + inner[l]
+        x = state[l].reshape(cells, model).astype(F32)
+        x = x + dot(attn[l].reshape(cells, model), w_out[...], 1, 0)
+        out[l] = x.astype(BF16).reshape(height, width, model)
 
 
 def stage_last(plan, parts_n, own, back_e, back_o, x, *refs):
@@ -428,17 +444,18 @@
     def swap(block, axis, first):
         return lax.ppermute(block, axis, swap_pairs(lax.axis_size(axis), first))
 
-    rows_e, rows_o = pl.pallas_call(
+    rows_e, rows_o, *near = pl.pallas_call(
         bind(stage_cut, plan),
         name="stage_cut",
-        out_shape=[jax.ShapeDtypeStruct(plan.edge, BF16)] * 2,
+        out_shape=[jax.ShapeDtypeStruct(plan.edge, BF16)] * 2
+        + [jax.ShapeDtypeStruct(plan.own[1:] + (model,), BF16)] * sides,
         in_specs=[pl.BlockSpec(memory_space=pl.ANY)],
-        out_specs=[VMEM, VMEM],
-        scratch_shapes=[pltpu.SemaphoreType.DMA((2,))],
+        out_specs=[VMEM] * (2 + sides),
+        scratch_shapes=[pltpu.SemaphoreType.DMA((2 + sides,))],
         compiler_params=pltpu.CompilerParams(vmem_limit_bytes=2**20),
+        cost_estimate=pl.CostEstimate(flops=20 * 10**9, bytes_accessed=2**20, transcendentals=0),
     )(state)
-    rows_e, rows_o, held_state = lax.optimization_barrier((rows_e, rows_o, state))
-    near = [swap(held_state, "lev", side) for side in range(sides)]
+    near = [swap(edge, "lev", side) for side, edge in enumerate(near)]
     rows_e = swap(rows_e, "tile", 0)
     rows_o = swap(rows_o, "tile", 1)
     live = pltpu.SMEM(((plan.levels_n + 2) * plan.tall,), jnp.int32)
@@ -451,10 +468,7 @@
         [live],
         cost=4 * 10**9,
     )
-    rows_e, rows_o, qs = lax.optimization_barrier((rows_e, rows_o, qs))
-    lev_in = []
-    for side in range(sides):
-        lev_in += [near[side], swap(rows_e, "lev", side), swap(rows_o, "lev", side)]
+    rows_e, qs = lax.optimization_barrier((rows_e, qs))
     rows = model // (tiles * levs)
     if levs == 2 and rows % 8 == 0:
         share = (tiles, rows, 4 * model)
@@ -473,14 +487,26 @@
         (own_cells, BF16),
         (own_cells, BF16),
     ]
+    side = call(
+        bind(stage_side, plan),
+        "stage_side",
+        carried[:2],
+        [state, rows_e, mid, w_qkv],
+        cost=2 * 10**9,
+    )
+    rows_o, *side = lax.optimization_barrier((rows_o, *side))
+    lev_in = []
+    for n in range(sides):
+        lev_in += [near[n], swap(rows_e, "lev", n), swap(rows_o, "lev", n)]
     held = call(
         bind(stage_inner, plan),
         "stage_inner",
         carried,
-        [ocean, depth, state, rows_e, rows_o, qs, us, mid, w_qkv],
+        [ocean, depth, rows_o, qs, us, w_qkv, *side],
         [masks, live],
         mib=16,
         cost=8 * 10**9,
+        aliases={6: 0, 7: 1},
     )
     ins = [ocean, depth, state, qs, us, mid, w_qkv, cotangent, *lev_in, *held]
     _, _, _, _, attn, dq, dkv16, *sums = call(
@@ -494,20 +520,20 @@
         aliases={len(ins) - len(held) + i: i for i in range(len(held))},
     )
     edge_kind = (plan.wide[1:] + (model,), BF16)
-    out, own, part_e, part_o, *edges = call(
+    inner, part_e, part_o, *edges = call(
         bind(stage_out, plan),
         "stage_out",
-        [(own_cells, BF16), (own_cells, F32), (plan.edge, F32), (plan.edge, F32)] + [edge_kind] * sides,
-        [state, cotangent, attn, dq, dkv16, w_qkv, w_out],
+        [(own_cells, F32), (plan.edge, F32), (plan.edge, F32)] + [edge_kind] * sides,
+        [dkv16, w_qkv],
         [pltpu.VMEM(plan.wide[1:] + (model,), F32)],
         cost=4 * 10**9,
     )
     edges = [swap(edge, "lev", side) for side, edge in enumerate(edges)]
-    send_e, send_o = call(
+    send_e, send_o, out, own = call(
         bind(stage_fold, plan),
         "stage_fold",
-        [(plan.edge, BF16)] * 2,
-        [part_e, part_o, *edges],
+        [(plan.edge, BF16)] * 2 + [(own_cells, BF16), (own_cells, F32)],
+        [part_e, part_o, inner, state, cotangent, attn, dq, w_qkv, w_out, *edges],
         [pltpu.VMEM(plan.edge, F32)],
     )
 

time: 57.6 us -> 56.8 us (0.986)
  local copies, waits for them, and re-layouts: 6.62 us -> 1.08 us
  starting transfers between devices: 19 us -> 21.6 us
  waiting for transfers between devices: 14.9 us -> 16.5 us
  Pallas kernels: 15.9 us -> 16.6 us
    unnamed x24 -> x14, local copies, waits for them, and re-layouts: 6.62 us -> 1.08 us
    ppermute x8, waiting for transfers between devices: 0.02 us -> 3.15 us  [swap(): return lax.ppermute(block, axis, swap_pairs(lax.axis_size(axis), first))]
    ppermute x6, waiting for transfers between devices: 14.9 us -> 12.6 us  [local(): lax.ppermute(piece, 'tile', xor_route(tiles, (k + 1) * stride))]
    ppermute x6, starting transfers between devices: 11.3 us -> 12.9 us  [local(): lax.ppermute(piece, 'tile', xor_route(tiles, (k + 1) * stride))]
    ppermute x8, starting transfers between devices: 7.48 us -> 8.58 us  [swap(): return lax.ppermute(block, axis, swap_pairs(lax.axis_size(axis), first))]
    ppermute x1, waiting for transfers between devices: 0.01 us -> 0.77 us  [local(): x, parts = (sums[0], [lax.ppermute(sums[1], 'lev', swap_pairs(levs, 0))])]
    pallas_call x8 -> x9, Pallas kernels: 15.7 us -> 16.2 us  [call(): pl.pallas_call(body, name=name, out_shape=[jax.ShapeDtypeStruct(shape, ki...]
  transfers between devices with their start and end apart: 15 -> 15, of which waited for: 3 -> 7; matrix products, arithmetic and copies ran while one was open for 0% -> 0% of each run, Pallas kernels for 14% -> 15%
where the time goes in v5:
time: 56.8 us; the launch traced here: 56.6 us
  starting transfers between devices  21.6 us (38%)
  Pallas kernels  16.6 us (29%)
  waiting for transfers between devices  16.5 us (29%)
  local copies, waits for them, and re-layouts  1.08 us (2%)
  between operations  0.82 us (1%)
    pallas_call x9, Pallas kernels, call(): pl.pallas_call(body, name=name, out_shape=[jax.ShapeDtypeStruct(shape, ki...  16.2 us
    ppermute x6, starting transfers between devices, local(): lax.ppermute(piece, 'tile', xor_route(tiles, (k + 1) * stride))  12.9 us
    ppermute x6, waiting for transfers between devices, local(): lax.ppermute(piece, 'tile', xor_route(tiles, (k + 1) * stride))  12.6 us
    ppermute x8, starting transfers between devices, swap(): return lax.ppermute(block, axis, swap_pairs(lax.axis_size(axis), first))  8.58 us
    ppermute x8, waiting for transfers between devices, swap(): return lax.ppermute(block, axis, swap_pairs(lax.axis_size(axis), first))  3.15 us
  transfers between devices with their start and end apart: 15, of which 7 were waited for; matrix products, arithmetic and copies ran while one was open for 0% of the time, Pallas kernels for 15%

profile of v5, /device:TPU:0, one launch (start us, length us, event | category | flops | bytes accessed | tf_op | source)
XLA Modules:
  0.0 56.6 jit_solution(15350370819402222841)
XLA Ops:
  0.6 0.0 copy-start
  0.6 0.0 copy-start.2
  0.7 1.1 %copy-done.2 = bf16[2,4,32,512]{3,2,1,0:T(8,128)(2,1)S(1)} copy-done((bf16[2,4,32,512]{3,2,1,0:T(8,128)(2,1)S(1)}, bf16[2,4,32,512]{3,2,1,0:T(8,128)(2,1)}, u32[]{:S(2)}) %copy-start.2) | copy-done | bytes 262168
  1.7 0.0 copy-start.6
  1.7 0.5 stage_cut.1
  2.2 0.5 collective-permute-start.1
  2.7 2.6 %collective-permute-start = (bf16[2,3,32,512]{3,2,1,0:T(8,128)(2,1)S(1)}, bf16[2,3,32,512]{3,2,1,0:T(8,128)(2,1)S(1)}, u32[]{:S(2)}, u32[]{:S(2)}) collective-permute-start(bf16[2,3,32,512]{3,2,1,0:T(8,128)(2,1)S(1)} %get-tuple-element.50), channel_id=1, source_target_pairs={{0,2},{2,0},{4,6},{6,4},{8,10},{10,8},{12,14},{14,12},{16,18},{18,... | collective-permute-start | bytes 589832 | tf_op jit(solution)/shard_map/ppermute | solution.py:445
  5.3 0.7 %collective-permute-start.3 = (bf16[2,3,32,512]{3,2,1,0:T(8,128)(2,1)S(1)}, bf16[2,3,32,512]{3,2,1,0:T(8,128)(2,1)S(1)}, u32[]{:S(2)}, u32[]{:S(2)}) collective-permute-start(bf16[2,3,32,512]{3,2,1,0:T(8,128)(2,1)S(1)} %get-tuple-element.57), channel_id=1, source_target_pairs={{2,4},{4,2},{6,8},{8,6},{10,12},{12,10},{14,16},{16,14},{18,20},{2... | collective-permute-start | bytes 589832 | tf_op jit(solution)/shard_map/ppermute | solution.py:445
  6.0 0.0 collective-permute-done.1.refs_6_.refs_8_
  6.0 0.0 copy-done
  6.0 0.0 copy-done.1
  6.0 0.0 copy-done.3
  6.0 0.0 copy-done.4
  6.0 1.6 %stage_own.1 = (bf16[2,4,32,512]{3,2,1,0:T(8,128)(2,1)S(1)}, bf16[2,4,32,512]{3,2,1,0:T(8,128)(2,1)S(1)}, bf16[3,4,32,1024]{3,2,1,0:T(8,128)(2,1)S(1)}) custom-call(s32[16]{0:T(128)S(1)} %copy-done.5, s32[16]{0:T(128)S(1)} %copy-done.6, bf16[2,4,32,512]{3,2,1,0:T(8,128)(2,1)S(1)} %copy-done.3, bf16[512,1536]{1,0:T(8,128)(2,1)S(1)} %copy-done, ...), custom_call_target="tpu_custom_call" | custom-call | flops 4000000000 | bytes 1048576 | tf_op jit(solution)/shard_map/stage_own/pallas_call | solution.py:32
  7.7 3.1 %collective-permute-done.refs_1_ = bf16[2,3,32,512]{3,2,1,0:T(8,128)(2,1)S(1)} collective-permute-done((bf16[2,3,32,512]{3,2,1,0:T(8,128)(2,1)S(1)}, bf16[2,3,32,512]{3,2,1,0:T(8,128)(2,1)S(1)}, u32[]{:S(2)}, u32[]{:S(2)}) %collective-permute-start) | collective-permute-done | bytes 196640 | tf_op jit(solution)/shard_map/ppermute | solution.py:445
  10.8 0.0 collective-permute-start.2
  10.8 0.4 stage_side.1
  11.2 0.0 collective-permute-done.3.refs_2_
  11.2 0.6 %collective-permute-start.4 = (bf16[2,3,32,512]{3,2,1,0:T(8,128)(2,1)S(1)}, bf16[2,3,32,512]{3,2,1,0:T(8,128)(2,1)S(1)}, u32[]{:S(2)}, u32[]{:S(2)}) collective-permute-start(bf16[2,3,32,512]{3,2,1,0:T(8,128)(2,1)S(1)} %collective-permute-done.3.refs_2_), channel_id=1, source_target_pairs={{0,1},{1,0},{2,3},{3,2},{4,5},{5,4},{6,7},{7,6},{8,9},{9,8},{10,11... | collective-permute-start | bytes 589832 | tf_op jit(solution)/shard_map/ppermute | solution.py:445
  11.8 3.1 %stage_inner.1 = (bf16[3,10,32,512]{3,2,1,0:T(8,128)(2,1)S(1)}, bf16[3,10,32,1024]{3,2,1,0:T(8,128)(2,1)S(1)}, bf16[2,3,10,32,1024]{4,3,2,1,0:T(8,128)(2,1)S(1)}...) custom-call(s32[16]{0:T(128)S(1)} %copy-done.5, ...), custom_call_target="tpu_custom_call", output_to_operand_aliasing={{0}: (6, {}), {1}: (7, {})} | custom-call | flops 8000000000 | bytes 1048576 | tf_op jit(solution)/shard_map/stage_inner/pallas_call | solution.py:32
  14.9 0.0 collective-permute-done.2.refs_9_
  14.9 0.0 collective-permute-done.4.refs_10_
  14.9 7.0 %stage_attend.1 = (bf16[3,10,32,512]{3,2,1,0:T(8,128)(2,1)S(1)}, bf16[3,10,32,1024]{3,2,1,0:T(8,128)(2,1)S(1)}, bf16[2,3,10,32,1024]{4,3,2,1,0:T(8,128)(2,1)S(1)...) custom-call(s32[16]{0:T(128)S(1)} %copy-done.5, ...), custom_call_target="tpu_custom_call", output_to_operand_aliasing={{0}: (11, {}), {1}: (12, {}), {2}: (13, {}), {3}: (14, {}),... | custom-call | flops 16000000000 | bytes 1048576 | tf_op jit(solution)/shard_map/stage_attend/pallas_call | solution.py:32
  21.9 0.1 collective-permute-start.6
  22.0 1.3 %stage_out.1 = (f32[2,4,32,512]{3,2,1,0:T(8,128)S(1)}, f32[2,3,32,512]{3,2,1,0:T(8,128)S(1)}, f32[2,3,32,512]{3,2,1,0:T(8,128)S(1)}, bf16[10,32,512]{2,1,0:T(8,128)(2,1)S(1)}) custom-call(bf16[3,10,32,1024]{3,2,1,0:T(8,128)(2,1)S(1)} %get-tuple-element.69.refs_0_, bf16[512,1536]{1,0:T(8,128)(2,1)S(1)} %copy-done), custom_call_target="tpu_custom_call" | custom-call | flops 4000000000 | bytes 1048576 | tf_op jit(solution)/shard_map/stage_out/pallas_call | solution.py:32
  23.3 0.6 collective-permute-start.5
  23.9 0.8 %collective-permute-done.6.refs_1_ = bf16[16,16,2048]{2,1,0:T(8,128)(2,1)S(1)} collective-permute-done((bf16[16,16,2048]{2,1,0:T(8,128)(2,1)S(1)}, bf16[16,16,2048]{2,1,0:T(8,128)(2,1)S(1)}, u32[]{:S(2)}, u32[]{:S(2)}) %collective-permute-start.6) | collective-permute-done | bytes 1048608 | tf_op jit(solution)/shard_map/ppermute | solution.py:541
  24.6 0.2 stage_split.2
  24.9 6.0 %collective-permute-start.7 = (bf16[4,16,2048]{2,1,0:T(8,128)(2,1)S(1)}, bf16[4,16,2048]{2,1,0:T(8,128)(2,1)S(1)}, u32[]{:S(2)}, u32[]{:S(2)}) collective-permute-start(bf16[4,16,2048]{2,1,0:T(8,128)(2,1)S(1)} %get-tuple-element.82), channel_id=1, source_target_pairs={{0,6},{2,4},{4,2},{6,0},{8,14},{10,12},{12,10},{14,8},{16,22},{18,... | collective-permute-start | bytes 786440 | tf_op jit(solution)/shard_map/ppermute | solution.py:554
  30.9 0.5 collective-permute-start.10
  31.4 1.2 %collective-permute-start.11 = (bf16[4,16,2048]{2,1,0:T(8,128)(2,1)S(1)}, bf16[4,16,2048]{2,1,0:T(8,128)(2,1)S(1)}, u32[]{:S(2)}, u32[]{:S(2)}) collective-permute-start(bf16[4,16,2048]{2,1,0:T(8,128)(2,1)S(1)} %get-tuple-element.87), channel_id=1, source_target_pairs={{0,4},{2,6},{4,0},{6,2},{8,12},{10,14},{12,8},{14,10},{16,20},{18,... | collective-permute-start | bytes 786440 | tf_op jit(solution)/shard_map/ppermute | solution.py:554
  32.5 0.0 collective-permute-done.5.refs_9_.refs_7_
  32.5 1.5 %stage_fold.1 = (bf16[2,3,32,512]{3,2,1,0:T(8,128)(2,1)S(1)}, bf16[2,3,32,512]{3,2,1,0:T(8,128)(2,1)S(1)}, bf16[2,4,32,512]{3,2,1,0:T(8,128)(2,1)}, f32[2,4,32,512]{3,2,1,0:T(8,128)S(1)}) custom-call(f32[2,3,32,512]{3,2,1,0:T(8,128)S(1)} %get-tuple-element.70.refs_0_, f32[2,3,32,512]{3,2,1,0:T(8,128)S(1)} %get-tuple-element.71.refs_1_, ...), custom_call_target="tpu_custom_call" | custom-call | flops 1000000 | bytes 1048576 | tf_op jit(solution)/shard_map/stage_fold/pallas_call | solution.py:32
  34.0 4.1 %collective-permute-done.7.refs_3_ = bf16[4,16,2048]{2,1,0:T(8,128)(2,1)S(1)} collective-permute-done((bf16[4,16,2048]{2,1,0:T(8,128)(2,1)S(1)}, bf16[4,16,2048]{2,1,0:T(8,128)(2,1)S(1)}, u32[]{:S(2)}, u32[]{:S(2)}) %collective-permute-start.7) | collective-permute-done | bytes 262176 | tf_op jit(solution)/shard_map/ppermute | solution.py:554
  38.1 3.1 %collective-permute-start.8 = (bf16[2,3,32,512]{3,2,1,0:T(8,128)(2,1)S(1)}, bf16[2,3,32,512]{3,2,1,0:T(8,128)(2,1)S(1)}, u32[]{:S(2)}, u32[]{:S(2)}) collective-permute-start(bf16[2,3,32,512]{3,2,1,0:T(8,128)(2,1)S(1)} %get-tuple-element.83), channel_id=1, source_target_pairs={{0,2},{2,0},{4,6},{6,4},{8,10},{10,8},{12,14},{14,12},{16,18},{18,... | collective-permute-start | bytes 589832 | tf_op jit(solution)/shard_map/ppermute | solution.py:445
  41.1 0.7 %collective-permute-start.9 = (bf16[2,3,32,512]{3,2,1,0:T(8,128)(2,1)S(1)}, bf16[2,3,32,512]{3,2,1,0:T(8,128)(2,1)S(1)}, u32[]{:S(2)}, u32[]{:S(2)}) collective-permute-start(bf16[2,3,32,512]{3,2,1,0:T(8,128)(2,1)S(1)} %get-tuple-element.84), channel_id=1, source_target_pairs={{2,4},{4,2},{6,8},{8,6},{10,12},{12,10},{14,16},{16,14},{18,20},{2... | collective-permute-start | bytes 589832 | tf_op jit(solution)/shard_map/ppermute | solution.py:445
  41.8 2.3 %collective-permute-done.10.refs_1_ = bf16[4,16,2048]{2,1,0:T(8,128)(2,1)S(1)} collective-permute-done((bf16[4,16,2048]{2,1,0:T(8,128)(2,1)S(1)}, bf16[4,16,2048]{2,1,0:T(8,128)(2,1)S(1)}, u32[]{:S(2)}, u32[]{:S(2)}) %collective-permute-start.10) | collective-permute-done | bytes 262176 | tf_op jit(solution)/shard_map/ppermute | solution.py:554
  44.1 0.0 collective-permute-done.11.refs_2_
  44.1 0.1 stage_split.3
  44.2 2.7 %collective-permute-start.12 = (bf16[1,16,2048]{2,1,0:T(8,128)(2,1)S(1)}, bf16[1,16,2048]{2,1,0:T(8,128)(2,1)S(1)}, u32[]{:S(2)}, u32[]{:S(2)}) collective-permute-start(bf16[1,16,2048]{2,1,0:T(8,128)(2,1)S(1)} %get-tuple-element.90), channel_id=1, source_target_pairs={{0,8},{2,10},{4,12},{6,14},{8,0},{10,2},{12,4},{14,6},{16,24},{18,... | collective-permute-start | bytes 196616 | tf_op jit(solution)/shard_map/ppermute | solution.py:554
  47.0 2.6 %collective-permute-start.13 = (bf16[1,16,2048]{2,1,0:T(8,128)(2,1)S(1)}, bf16[1,16,2048]{2,1,0:T(8,128)(2,1)S(1)}, u32[]{:S(2)}, u32[]{:S(2)}) collective-permute-start(bf16[1,16,2048]{2,1,0:T(8,128)(2,1)S(1)} %get-tuple-element.91), channel_id=1, source_target_pairs={{0,16},{2,18},{4,20},{6,22},{8,24},{10,26},{12,28},{14,30},{16,0},... | collective-permute-start | bytes 196616 | tf_op jit(solution)/shard_map/ppermute | solution.py:554
  49.5 0.0 collective-permute-start.14
  49.5 0.6 %collective-permute-done.12.refs_4_ = bf16[1,16,2048]{2,1,0:T(8,128)(2,1)S(1)} collective-permute-done((bf16[1,16,2048]{2,1,0:T(8,128)(2,1)S(1)}, bf16[1,16,2048]{2,1,0:T(8,128)(2,1)S(1)}, u32[]{:S(2)}, u32[]{:S(2)}) %collective-permute-start.12) | collective-permute-done | bytes 65568 | tf_op jit(solution)/shard_map/ppermute | solution.py:554
  50.2 3.8 %collective-permute-done.13.refs_5_ = bf16[1,16,2048]{2,1,0:T(8,128)(2,1)S(1)} collective-permute-done((bf16[1,16,2048]{2,1,0:T(8,128)(2,1)S(1)}, bf16[1,16,2048]{2,1,0:T(8,128)(2,1)S(1)}, u32[]{:S(2)}, u32[]{:S(2)}) %collective-permute-start.13) | collective-permute-done | bytes 65568 | tf_op jit(solution)/shard_map/ppermute | solution.py:554
  54.0 1.8 %collective-permute-done.14.refs_6_ = bf16[1,16,2048]{2,1,0:T(8,128)(2,1)S(1)} collective-permute-done((bf16[1,16,2048]{2,1,0:T(8,128)(2,1)S(1)}, bf16[1,16,2048]{2,1,0:T(8,128)(2,1)S(1)}, u32[]{:S(2)}, u32[]{:S(2)}) %collective-permute-start.14) | collective-permute-done | bytes 65568 | tf_op jit(solution)/shard_map/ppermute | solution.py:554
  55.7 0.0 collective-permute-done.8.refs_1_
  55.7 0.0 collective-permute-done.9.refs_2_
  55.7 0.9 %stage_last.1 = (bf16[2,4,32,512]{3,2,1,0:T(8,128)(2,1)}, f32[16,1536]{1,0:T(8,128)}, f32[16,512]{1,0:T(8,128)}) custom-call(f32[2,4,32,512]{3,2,1,0:T(8,128)S(1)} %get-tuple-element.77.refs_0_, bf16[2,3,32,512]{3,2,1,0:T(8,128)(2,1)S(1)} %collective-permute-done.8.refs_1_, bf16[2,3,32,512]{3,2,1,0:T(8,128)(2,1)S(1)} %collective-permute-done.9.refs_2_, ...), custom_call_target="tpu_custom_call" | custom-call | flops 1000000 | bytes 1048576 | tf_op jit(solution)/shard_map/stage_last/pallas_call | solution.py:32
  (6 shorter events, 0.0 us)
Async XLA Ops:
  0.6 5.3 %copy-start = (bf16[512,1536]{1,0:T(8,128)(2,1)S(1)}, bf16[512,1536]{1,0:T(8,128)(2,1)}, u32[]{:S(2)}) copy-start(bf16[512,1536]{1,0:T(8,128)(2,1)} %refs_7_.3) | copy-start | bytes 4718596
  0.6 1.1 %copy-start.2 = (bf16[2,4,32,512]{3,2,1,0:T(8,128)(2,1)S(1)}, bf16[2,4,32,512]{3,2,1,0:T(8,128)(2,1)}, u32[]{:S(2)}) copy-start(bf16[2,4,32,512]{3,2,1,0:T(8,128)(2,1)} %refs_3_.5) | copy-start | bytes 786436
  1.7 4.3 %copy-start.1 = (bf16[512,512]{1,0:T(8,128)(2,1)S(1)}, bf16[512,512]{1,0:T(8,128)(2,1)}, u32[]{:S(2)}) copy-start(bf16[512,512]{1,0:T(8,128)(2,1)} %refs_8_.1) | copy-start | bytes 1572868
  1.7 4.3 %copy-start.3 = (bf16[2,4,32,512]{3,2,1,0:T(8,128)(2,1)S(1)}, bf16[2,4,32,512]{3,2,1,0:T(8,128)(2,1)}, u32[]{:S(2)}) copy-start(bf16[2,4,32,512]{3,2,1,0:T(8,128)(2,1)} %refs_3_.5) | copy-start | bytes 786436
  1.7 4.3 %copy-start.4 = (bf16[2,4,32,512]{3,2,1,0:T(8,128)(2,1)S(1)}, bf16[2,4,32,512]{3,2,1,0:T(8,128)(2,1)}, u32[]{:S(2)}) copy-start(bf16[2,4,32,512]{3,2,1,0:T(8,128)(2,1)} %refs_4_.3) | copy-start | bytes 786436
  1.7 4.3 %copy-start.5 = (s32[16]{0:T(128)S(1)}, s32[16]{0:T(128)}, u32[]{:S(2)}) copy-start(s32[16]{0:T(128)} %refs_0_.9) | copy-start | bytes 196
  1.7 4.3 %copy-start.6 = (s32[16]{0:T(128)S(1)}, s32[16]{0:T(128)}, u32[]{:S(2)}) copy-start(s32[16]{0:T(128)} %refs_1_.6) | copy-start | bytes 196
  2.2 3.8 %collective-permute-start.1 = (bf16[4,32,512]{2,1,0:T(8,128)(2,1)S(1)}, bf16[4,32,512]{2,1,0:T(8,128)(2,1)S(1)}, u32[]{:S(2)}, u32[]{:S(2)}) collective-permute-start(bf16[4,32,512]{2,1,0:T(8,128)(2,1)S(1)} %get-tuple-element.51), channel_id=1, source_target_pairs={{0,1},{1,0},{2,3},{3,2},{4,5},{5,4},{6,7},{7,6},{8,9},{9,8},{10,11... | collective-permute-start | bytes 393224 | tf_op jit(solution)/shard_map/ppermute | solution.py:445
  2.7 8.1 %collective-permute-start = (bf16[2,3,32,512]{3,2,1,0:T(8,128)(2,1)S(1)}, bf16[2,3,32,512]{3,2,1,0:T(8,128)(2,1)S(1)}, u32[]{:S(2)}, u32[]{:S(2)}) collective-permute-start(bf16[2,3,32,512]{3,2,1,0:T(8,128)(2,1)S(1)} %get-tuple-element.50), channel_id=1, source_target_pairs={{0,2},{2,0},{4,6},{6,4},{8,10},{10,8},{12,14},{14,12},{16,18},{18,... | collective-permute-start | bytes 589832 | tf_op jit(solution)/shard_map/ppermute | solution.py:445
  5.3 5.9 %collective-permute-start.3 = (bf16[2,3,32,512]{3,2,1,0:T(8,128)(2,1)S(1)}, bf16[2,3,32,512]{3,2,1,0:T(8,128)(2,1)S(1)}, u32[]{:S(2)}, u32[]{:S(2)}) collective-permute-start(bf16[2,3,32,512]{3,2,1,0:T(8,128)(2,1)S(1)} %get-tuple-element.57), channel_id=1, source_target_pairs={{2,4},{4,2},{6,8},{8,6},{10,12},{12,10},{14,16},{16,14},{18,20},{2... | collective-permute-start | bytes 589832 | tf_op jit(solution)/shard_map/ppermute | solution.py:445
  10.8 4.1 %collective-permute-start.2 = (bf16[2,3,32,512]{3,2,1,0:T(8,128)(2,1)S(1)}, bf16[2,3,32,512]{3,2,1,0:T(8,128)(2,1)S(1)}, u32[]{:S(2)}, u32[]{:S(2)}) collective-permute-start(bf16[2,3,32,512]{3,2,1,0:T(8,128)(2,1)S(1)} %collective-permute-done.refs_1_), channel_id=1, source_target_pairs={{0,1},{1,0},{2,3},{3,2},{4,5},{5,4},{6,7},{7,6},{8,9},{9,8},{10,11... | collective-permute-start | bytes 589832 | tf_op jit(solution)/shard_map/ppermute | solution.py:445
  11.2 3.7 %collective-permute-start.4 = (bf16[2,3,32,512]{3,2,1,0:T(8,128)(2,1)S(1)}, bf16[2,3,32,512]{3,2,1,0:T(8,128)(2,1)S(1)}, u32[]{:S(2)}, u32[]{:S(2)}) collective-permute-start(bf16[2,3,32,512]{3,2,1,0:T(8,128)(2,1)S(1)} %collective-permute-done.3.refs_2_), channel_id=1, source_target_pairs={{0,1},{1,0},{2,3},{3,2},{4,5},{5,4},{6,7},{7,6},{8,9},{9,8},{10,11... | collective-permute-start | bytes 589832 | tf_op jit(solution)/shard_map/ppermute | solution.py:445
  21.9 2.7 %collective-permute-start.6 = (bf16[16,16,2048]{2,1,0:T(8,128)(2,1)S(1)}, bf16[16,16,2048]{2,1,0:T(8,128)(2,1)S(1)}, u32[]{:S(2)}, u32[]{:S(2)}) collective-permute-start(bf16[16,16,2048]{2,1,0:T(8,128)(2,1)S(1)} %get-tuple-element.81), channel_id=1, source_target_pairs={{0,1},{1,0},{2,3},{3,2},{4,5},{5,4},{6,7},{7,6},{8,9},{9,8},{10,11... | collective-permute-start | bytes 3145736 | tf_op jit(solution)/shard_map/ppermute | solution.py:541
  23.3 9.2 %collective-permute-start.5 = (bf16[10,32,512]{2,1,0:T(8,128)(2,1)S(1)}, bf16[10,32,512]{2,1,0:T(8,128)(2,1)S(1)}, u32[]{:S(2)}, u32[]{:S(2)}) collective-permute-start(bf16[10,32,512]{2,1,0:T(8,128)(2,1)S(1)} %get-tuple-element.75), channel_id=1, source_target_pairs={{0,1},{1,0},{2,3},{3,2},{4,5},{5,4},{6,7},{7,6},{8,9},{9,8},{10,11... | collective-permute-start | bytes 983048 | tf_op jit(solution)/shard_map/ppermute | solution.py:445
  24.9 13.2 %collective-permute-start.7 = (bf16[4,16,2048]{2,1,0:T(8,128)(2,1)S(1)}, bf16[4,16,2048]{2,1,0:T(8,128)(2,1)S(1)}, u32[]{:S(2)}, u32[]{:S(2)}) collective-permute-start(bf16[4,16,2048]{2,1,0:T(8,128)(2,1)S(1)} %get-tuple-element.82), channel_id=1, source_target_pairs={{0,6},{2,4},{4,2},{6,0},{8,14},{10,12},{12,10},{14,8},{16,22},{18,... | collective-permute-start | bytes 786440 | tf_op jit(solution)/shard_map/ppermute | solution.py:554
  30.9 13.2 %collective-permute-start.10 = (bf16[4,16,2048]{2,1,0:T(8,128)(2,1)S(1)}, bf16[4,16,2048]{2,1,0:T(8,128)(2,1)S(1)}, u32[]{:S(2)}, u32[]{:S(2)}) collective-permute-start(bf16[4,16,2048]{2,1,0:T(8,128)(2,1)S(1)} %get-tuple-element.86), channel_id=1, source_target_pairs={{0,2},{2,0},{4,6},{6,4},{8,10},{10,8},{12,14},{14,12},{16,18},{18,... | collective-permute-start | bytes 786440 | tf_op jit(solution)/shard_map/ppermute | solution.py:554
  31.4 12.8 %collective-permute-start.11 = (bf16[4,16,2048]{2,1,0:T(8,128)(2,1)S(1)}, bf16[4,16,2048]{2,1,0:T(8,128)(2,1)S(1)}, u32[]{:S(2)}, u32[]{:S(2)}) collective-permute-start(bf16[4,16,2048]{2,1,0:T(8,128)(2,1)S(1)} %get-tuple-element.87), channel_id=1, source_target_pairs={{0,4},{2,6},{4,0},{6,2},{8,12},{10,14},{12,8},{14,10},{16,20},{18,... | collective-permute-start | bytes 786440 | tf_op jit(solution)/shard_map/ppermute | solution.py:554
  38.1 17.7 %collective-permute-start.8 = (bf16[2,3,32,512]{3,2,1,0:T(8,128)(2,1)S(1)}, bf16[2,3,32,512]{3,2,1,0:T(8,128)(2,1)S(1)}, u32[]{:S(2)}, u32[]{:S(2)}) collective-permute-start(bf16[2,3,32,512]{3,2,1,0:T(8,128)(2,1)S(1)} %get-tuple-element.83), channel_id=1, source_target_pairs={{0,2},{2,0},{4,6},{6,4},{8,10},{10,8},{12,14},{14,12},{16,18},{18,... | collective-permute-start | bytes 589832 | tf_op jit(solution)/shard_map/ppermute | solution.py:445
  41.1 14.6 %collective-permute-start.9 = (bf16[2,3,32,512]{3,2,1,0:T(8,128)(2,1)S(1)}, bf16[2,3,32,512]{3,2,1,0:T(8,128)(2,1)S(1)}, u32[]{:S(2)}, u32[]{:S(2)}) collective-permute-start(bf16[2,3,32,512]{3,2,1,0:T(8,128)(2,1)S(1)} %get-tuple-element.84), channel_id=1, source_target_pairs={{2,4},{4,2},{6,8},{8,6},{10,12},{12,10},{14,16},{16,14},{18,20},{2... | collective-permute-start | bytes 589832 | tf_op jit(solution)/shard_map/ppermute | solution.py:445
  44.2 5.9 %collective-permute-start.12 = (bf16[1,16,2048]{2,1,0:T(8,128)(2,1)S(1)}, bf16[1,16,2048]{2,1,0:T(8,128)(2,1)S(1)}, u32[]{:S(2)}, u32[]{:S(2)}) collective-permute-start(bf16[1,16,2048]{2,1,0:T(8,128)(2,1)S(1)} %get-tuple-element.90), channel_id=1, source_target_pairs={{0,8},{2,10},{4,12},{6,14},{8,0},{10,2},{12,4},{14,6},{16,24},{18,... | collective-permute-start | bytes 196616 | tf_op jit(solution)/shard_map/ppermute | solution.py:554
  47.0 7.0 %collective-permute-start.13 = (bf16[1,16,2048]{2,1,0:T(8,128)(2,1)S(1)}, bf16[1,16,2048]{2,1,0:T(8,128)(2,1)S(1)}, u32[]{:S(2)}, u32[]{:S(2)}) collective-permute-start(bf16[1,16,2048]{2,1,0:T(8,128)(2,1)S(1)} %get-tuple-element.91), channel_id=1, source_target_pairs={{0,16},{2,18},{4,20},{6,22},{8,24},{10,26},{12,28},{14,30},{16,0},... | collective-permute-start | bytes 196616 | tf_op jit(solution)/shard_map/ppermute | solution.py:554
  49.5 6.2 %collective-permute-start.14 = (bf16[1,16,2048]{2,1,0:T(8,128)(2,1)S(1)}, bf16[1,16,2048]{2,1,0:T(8,128)(2,1)S(1)}, u32[]{:S(2)}, u32[]{:S(2)}) collective-permute-start(bf16[1,16,2048]{2,1,0:T(8,128)(2,1)S(1)} %get-tuple-element.92), channel_id=1, source_target_pairs={{0,24},{2,26},{4,28},{6,30},{8,16},{10,18},{12,20},{14,22},{16,8},... | collective-permute-start | bytes 196616 | tf_op jit(solution)/shard_map/ppermute | solution.py:554

commit v6 on v5

--- a/solution.py
+++ b/solution.py
@@ -368,8 +368,8 @@
         out[l] = x.astype(BF16).reshape(height, width, model)
 
 
-def stage_last(plan, parts_n, own, back_e, back_o, x, *refs):
-    parts, edges, (d_state, d_qkv, d_out, acc) = refs[:parts_n], refs[parts_n:-4], refs[-4:]
+def stage_last(plan, own, back_e, back_o, *refs):
+    edges, (d_state, acc) = refs[:-2], refs[-2:]
     plan.places()
     height = plan.height
     acc[...] = own[...]
@@ -379,6 +379,10 @@
     acc[:, pl.ds(jnp.where(plan.even, top, 0), REACH)] += back_e[...].astype(F32)
     acc[:, pl.ds(jnp.where(plan.even, 0, top), REACH)] += back_o[...].astype(F32)
     d_state[...] = acc[...].astype(BF16)
+
+
+def stage_sum(x, *refs):
+    parts, (d_qkv, d_out) = refs[:-2], refs[-2:]
     y = x[0]
     for part in parts:
         y = y + part[0].astype(F32)
@@ -550,21 +554,28 @@
             [(share, F32)] + [(share, BF16)] * (radix - 1),
             [x, *parts],
         )
-        parts = [
-            lax.ppermute(piece, "tile", xor_route(tiles, (k + 1) * stride))
-            for k, piece in enumerate(pieces)
-        ]
+        sent = {}
+        for k in range(len(pieces))[::-1]:
+            sent[k] = lax.ppermute(pieces[k], "tile", xor_route(tiles, (k + 1) * stride))
+        parts = [sent[k] for k in range(len(pieces))]
         if stride == 1:
             send_e, send_o, parts[2] = lax.optimization_barrier((send_e, send_o, parts[2]))
         stride *= radix
     back_e = swap(send_e, "tile", 0)
     back_o = swap(send_o, "tile", 1)
-    d_state, d_qkv, d_out = call(
-        bind(stage_last, plan, len(parts)),
+    (d_state,) = call(
+        bind(stage_last, plan),
         "stage_last",
-        [(own_cells, BF16), ((rows, 3 * model), F32), ((rows, model), F32)],
-        [own, back_e, back_o, x, *parts, *edges],
+        [(own_cells, BF16)],
+        [own, back_e, back_o, *edges],
         [pltpu.VMEM(own_cells, F32)],
+    )
+    d_state, parts[-1] = lax.optimization_barrier((d_state, parts[-1]))
+    d_qkv, d_out = call(
+        stage_sum,
+        "stage_sum",
+        [((rows, 3 * model), F32), ((rows, model), F32)],
+        [x, *parts],
     )
     return (out, d_state, d_qkv, d_out)
 

time: 56.8 us -> 56.9 us (level)
  Pallas kernels: 16.6 us -> 17.3 us
  waiting for transfers between devices: 16.5 us -> 15.9 us
    ppermute x6, waiting for transfers between devices: 12.6 us -> 10.5 us  [local(): lax.ppermute(pieces[k], 'tile', xor_route(tiles, (k + 1) * stride))]
    ppermute x8, waiting for transfers between devices: 3.15 us -> 4.58 us  [swap(): return lax.ppermute(block, axis, swap_pairs(lax.axis_size(axis), first))]
    pallas_call x9 -> x10, Pallas kernels: 16.2 us -> 16.8 us  [call(): pl.pallas_call(body, name=name, out_shape=[jax.ShapeDtypeStruct(shape, ki...]
  transfers between devices with their start and end apart: 15 -> 15, of which waited for: 7 -> 7; matrix products, arithmetic and copies ran while one was open for 0% -> 0% of each run, Pallas kernels for 15% -> 16%
where the time goes in v6:
time: 56.9 us; the launch traced here: 56.7 us
  starting transfers between devices  21.7 us (38%)
  Pallas kernels  17.3 us (30%)
  waiting for transfers between devices  15.9 us (28%)
  local copies, waits for them, and re-layouts  1.08 us (2%)
  between operations  0.82 us (1%)
    pallas_call x10, Pallas kernels, call(): pl.pallas_call(body, name=name, out_shape=[jax.ShapeDtypeStruct(shape, ki...  16.8 us
    ppermute x6, starting transfers between devices, local(): lax.ppermute(pieces[k], 'tile', xor_route(tiles, (k + 1) * stride))  13 us
    ppermute x6, waiting for transfers between devices, local(): lax.ppermute(pieces[k], 'tile', xor_route(tiles, (k + 1) * stride))  10.5 us
    ppermute x8, starting transfers between devices, swap(): return lax.ppermute(block, axis, swap_pairs(lax.axis_size(axis), first))  8.58 us
    ppermute x8, waiting for transfers between devices, swap(): return lax.ppermute(block, axis, swap_pairs(lax.axis_size(axis), first))  4.58 us
  transfers between devices with their start and end apart: 15, of which 7 were waited for; matrix products, arithmetic and copies ran while one was open for 0% of the time, Pallas kernels for 16%

profile of v6, /device:TPU:0, one launch (start us, length us, event | category | flops | bytes accessed | tf_op | source)
XLA Modules:
  0.0 56.7 jit_solution(4006165031218943728)
XLA Ops:
  0.6 0.0 copy-start
  0.6 0.0 copy-start.2
  0.7 1.1 %copy-done.2 = bf16[2,4,32,512]{3,2,1,0:T(8,128)(2,1)S(1)} copy-done((bf16[2,4,32,512]{3,2,1,0:T(8,128)(2,1)S(1)}, bf16[2,4,32,512]{3,2,1,0:T(8,128)(2,1)}, u32[]{:S(2)}) %copy-start.2) | copy-done | bytes 262168
  1.7 0.0 copy-start.6
  1.7 0.5 stage_cut.1
  2.2 0.5 collective-permute-start.1
  2.7 2.6 %collective-permute-start = (bf16[2,3,32,512]{3,2,1,0:T(8,128)(2,1)S(1)}, bf16[2,3,32,512]{3,2,1,0:T(8,128)(2,1)S(1)}, u32[]{:S(2)}, u32[]{:S(2)}) collective-permute-start(bf16[2,3,32,512]{3,2,1,0:T(8,128)(2,1)S(1)} %get-tuple-element.51), channel_id=1, source_target_pairs={{0,2},{2,0},{4,6},{6,4},{8,10},{10,8},{12,14},{14,12},{16,18},{18,... | collective-permute-start | bytes 589832 | tf_op jit(solution)/shard_map/ppermute | solution.py:449
  5.3 0.7 %collective-permute-start.3 = (bf16[2,3,32,512]{3,2,1,0:T(8,128)(2,1)S(1)}, bf16[2,3,32,512]{3,2,1,0:T(8,128)(2,1)S(1)}, u32[]{:S(2)}, u32[]{:S(2)}) collective-permute-start(bf16[2,3,32,512]{3,2,1,0:T(8,128)(2,1)S(1)} %get-tuple-element.58), channel_id=1, source_target_pairs={{2,4},{4,2},{6,8},{8,6},{10,12},{12,10},{14,16},{16,14},{18,20},{2... | collective-permute-start | bytes 589832 | tf_op jit(solution)/shard_map/ppermute | solution.py:449
  6.0 0.0 collective-permute-done.1.refs_6_.refs_8_
  6.0 0.0 copy-done
  6.0 0.0 copy-done.1
  6.0 0.0 copy-done.3
  6.0 1.6 %stage_own.1 = (bf16[2,4,32,512]{3,2,1,0:T(8,128)(2,1)S(1)}, bf16[2,4,32,512]{3,2,1,0:T(8,128)(2,1)S(1)}, bf16[3,4,32,1024]{3,2,1,0:T(8,128)(2,1)S(1)}) custom-call(s32[16]{0:T(128)S(1)} %copy-done.5, s32[16]{0:T(128)S(1)} %copy-done.6, bf16[2,4,32,512]{3,2,1,0:T(8,128)(2,1)S(1)} %copy-done.3, bf16[512,1536]{1,0:T(8,128)(2,1)S(1)} %copy-done, ...), custom_call_target="tpu_custom_call" | custom-call | flops 4000000000 | bytes 1048576 | tf_op jit(solution)/shard_map/stage_own/pallas_call | solution.py:32
  7.7 3.1 %collective-permute-done.refs_1_ = bf16[2,3,32,512]{3,2,1,0:T(8,128)(2,1)S(1)} collective-permute-done((bf16[2,3,32,512]{3,2,1,0:T(8,128)(2,1)S(1)}, bf16[2,3,32,512]{3,2,1,0:T(8,128)(2,1)S(1)}, u32[]{:S(2)}, u32[]{:S(2)}) %collective-permute-start) | collective-permute-done | bytes 196640 | tf_op jit(solution)/shard_map/ppermute | solution.py:449
  10.8 0.0 collective-permute-start.2
  10.8 0.4 stage_side.1
  11.2 0.0 collective-permute-done.3.refs_2_
  11.2 0.6 %collective-permute-start.4 = (bf16[2,3,32,512]{3,2,1,0:T(8,128)(2,1)S(1)}, bf16[2,3,32,512]{3,2,1,0:T(8,128)(2,1)S(1)}, u32[]{:S(2)}, u32[]{:S(2)}) collective-permute-start(bf16[2,3,32,512]{3,2,1,0:T(8,128)(2,1)S(1)} %collective-permute-done.3.refs_2_), channel_id=1, source_target_pairs={{0,1},{1,0},{2,3},{3,2},{4,5},{5,4},{6,7},{7,6},{8,9},{9,8},{10,11... | collective-permute-start | bytes 589832 | tf_op jit(solution)/shard_map/ppermute | solution.py:449
  11.8 3.1 %stage_inner.1 = (bf16[3,10,32,512]{3,2,1,0:T(8,128)(2,1)S(1)}, bf16[3,10,32,1024]{3,2,1,0:T(8,128)(2,1)S(1)}, bf16[2,3,10,32,1024]{4,3,2,1,0:T(8,128)(2,1)S(1)}...) custom-call(s32[16]{0:T(128)S(1)} %copy-done.5, ...), custom_call_target="tpu_custom_call", output_to_operand_aliasing={{0}: (6, {}), {1}: (7, {})} | custom-call | flops 8000000000 | bytes 1048576 | tf_op jit(solution)/shard_map/stage_inner/pallas_call | solution.py:32
  14.9 0.0 collective-permute-done.2.refs_9_
  14.9 0.0 collective-permute-done.4.refs_10_
  14.9 7.0 %stage_attend.1 = (bf16[3,10,32,512]{3,2,1,0:T(8,128)(2,1)S(1)}, bf16[3,10,32,1024]{3,2,1,0:T(8,128)(2,1)S(1)}, bf16[2,3,10,32,1024]{4,3,2,1,0:T(8,128)(2,1)S(1)...) custom-call(s32[16]{0:T(128)S(1)} %copy-done.5, ...), custom_call_target="tpu_custom_call", output_to_operand_aliasing={{0}: (11, {}), {1}: (12, {}), {2}: (13, {}), {3}: (14, {}),... | custom-call | flops 16000000000 | bytes 1048576 | tf_op jit(solution)/shard_map/stage_attend/pallas_call | solution.py:32
  21.9 0.1 collective-permute-start.6
  22.0 1.3 %stage_out.1 = (f32[2,4,32,512]{3,2,1,0:T(8,128)S(1)}, f32[2,3,32,512]{3,2,1,0:T(8,128)S(1)}, f32[2,3,32,512]{3,2,1,0:T(8,128)S(1)}, bf16[10,32,512]{2,1,0:T(8,128)(2,1)S(1)}) custom-call(bf16[3,10,32,1024]{3,2,1,0:T(8,128)(2,1)S(1)} %get-tuple-element.70.refs_0_, bf16[512,1536]{1,0:T(8,128)(2,1)S(1)} %copy-done), custom_call_target="tpu_custom_call" | custom-call | flops 4000000000 | bytes 1048576 | tf_op jit(solution)/shard_map/stage_out/pallas_call | solution.py:32
  23.3 0.6 collective-permute-start.5
  23.9 0.8 %collective-permute-done.6.refs_1_ = bf16[16,16,2048]{2,1,0:T(8,128)(2,1)S(1)} collective-permute-done((bf16[16,16,2048]{2,1,0:T(8,128)(2,1)S(1)}, bf16[16,16,2048]{2,1,0:T(8,128)(2,1)S(1)}, u32[]{:S(2)}, u32[]{:S(2)}) %collective-permute-start.6) | collective-permute-done | bytes 1048608 | tf_op jit(solution)/shard_map/ppermute | solution.py:545
  24.6 0.2 stage_split.2
  24.9 6.0 %collective-permute-start.7 = (bf16[4,16,2048]{2,1,0:T(8,128)(2,1)S(1)}, bf16[4,16,2048]{2,1,0:T(8,128)(2,1)S(1)}, u32[]{:S(2)}, u32[]{:S(2)}) collective-permute-start(bf16[4,16,2048]{2,1,0:T(8,128)(2,1)S(1)} %get-tuple-element.83), channel_id=1, source_target_pairs={{0,6},{2,4},{4,2},{6,0},{8,14},{10,12},{12,10},{14,8},{16,22},{18,... | collective-permute-start | bytes 786440 | tf_op jit(solution)/shard_map/ppermute | solution.py:559
  30.9 0.5 collective-permute-start.10
  31.4 1.2 %collective-permute-start.11 = (bf16[4,16,2048]{2,1,0:T(8,128)(2,1)S(1)}, bf16[4,16,2048]{2,1,0:T(8,128)(2,1)S(1)}, u32[]{:S(2)}, u32[]{:S(2)}) collective-permute-start(bf16[4,16,2048]{2,1,0:T(8,128)(2,1)S(1)} %get-tuple-element.88), channel_id=1, source_target_pairs={{0,4},{2,6},{4,0},{6,2},{8,12},{10,14},{12,8},{14,10},{16,20},{18,... | collective-permute-start | bytes 786440 | tf_op jit(solution)/shard_map/ppermute | solution.py:559
  32.5 0.0 collective-permute-done.5.refs_9_.refs_3_
  32.5 1.5 %stage_fold.1 = (bf16[2,3,32,512]{3,2,1,0:T(8,128)(2,1)S(1)}, bf16[2,3,32,512]{3,2,1,0:T(8,128)(2,1)S(1)}, bf16[2,4,32,512]{3,2,1,0:T(8,128)(2,1)}, f32[2,4,32,512]{3,2,1,0:T(8,128)S(1)}) custom-call(f32[2,3,32,512]{3,2,1,0:T(8,128)S(1)} %get-tuple-element.71.refs_0_, f32[2,3,32,512]{3,2,1,0:T(8,128)S(1)} %get-tuple-element.72.refs_1_, ...), custom_call_target="tpu_custom_call" | custom-call | flops 1000000 | bytes 1048576 | tf_op jit(solution)/shard_map/stage_fold/pallas_call | solution.py:32
  34.0 4.1 %collective-permute-done.7.refs_3_ = bf16[4,16,2048]{2,1,0:T(8,128)(2,1)S(1)} collective-permute-done((bf16[4,16,2048]{2,1,0:T(8,128)(2,1)S(1)}, bf16[4,16,2048]{2,1,0:T(8,128)(2,1)S(1)}, u32[]{:S(2)}, u32[]{:S(2)}) %collective-permute-start.7) | collective-permute-done | bytes 262176 | tf_op jit(solution)/shard_map/ppermute | solution.py:559
  38.1 3.1 %collective-permute-start.8 = (bf16[2,3,32,512]{3,2,1,0:T(8,128)(2,1)S(1)}, bf16[2,3,32,512]{3,2,1,0:T(8,128)(2,1)S(1)}, u32[]{:S(2)}, u32[]{:S(2)}) collective-permute-start(bf16[2,3,32,512]{3,2,1,0:T(8,128)(2,1)S(1)} %get-tuple-element.84), channel_id=1, source_target_pairs={{0,2},{2,0},{4,6},{6,4},{8,10},{10,8},{12,14},{14,12},{16,18},{18,... | collective-permute-start | bytes 589832 | tf_op jit(solution)/shard_map/ppermute | solution.py:449
  41.1 0.7 %collective-permute-start.9 = (bf16[2,3,32,512]{3,2,1,0:T(8,128)(2,1)S(1)}, bf16[2,3,32,512]{3,2,1,0:T(8,128)(2,1)S(1)}, u32[]{:S(2)}, u32[]{:S(2)}) collective-permute-start(bf16[2,3,32,512]{3,2,1,0:T(8,128)(2,1)S(1)} %get-tuple-element.85), channel_id=1, source_target_pairs={{2,4},{4,2},{6,8},{8,6},{10,12},{12,10},{14,16},{16,14},{18,20},{2... | collective-permute-start | bytes 589832 | tf_op jit(solution)/shard_map/ppermute | solution.py:449
  41.8 2.3 %collective-permute-done.10.refs_1_ = bf16[4,16,2048]{2,1,0:T(8,128)(2,1)S(1)} collective-permute-done((bf16[4,16,2048]{2,1,0:T(8,128)(2,1)S(1)}, bf16[4,16,2048]{2,1,0:T(8,128)(2,1)S(1)}, u32[]{:S(2)}, u32[]{:S(2)}) %collective-permute-start.10) | collective-permute-done | bytes 262176 | tf_op jit(solution)/shard_map/ppermute | solution.py:559
  44.1 0.0 collective-permute-done.11.refs_2_
  44.1 0.1 stage_split.3
  44.2 4.7 %collective-permute-start.12 = (bf16[1,16,2048]{2,1,0:T(8,128)(2,1)S(1)}, bf16[1,16,2048]{2,1,0:T(8,128)(2,1)S(1)}, u32[]{:S(2)}, u32[]{:S(2)}) collective-permute-start(bf16[1,16,2048]{2,1,0:T(8,128)(2,1)S(1)} %get-tuple-element.90), channel_id=1, source_target_pairs={{0,24},{2,26},{4,28},{6,30},{8,16},{10,18},{12,20},{14,22},{16,8},... | collective-permute-start | bytes 196616 | tf_op jit(solution)/shard_map/ppermute | solution.py:559
  49.0 0.0 collective-permute-start.13
  49.0 0.6 %collective-permute-start.14 = (bf16[1,16,2048]{2,1,0:T(8,128)(2,1)S(1)}, bf16[1,16,2048]{2,1,0:T(8,128)(2,1)S(1)}, u32[]{:S(2)}, u32[]{:S(2)}) collective-permute-start(bf16[1,16,2048]{2,1,0:T(8,128)(2,1)S(1)} %get-tuple-element.94), channel_id=1, source_target_pairs={{0,16},{2,18},{4,20},{6,22},{8,24},{10,26},{12,28},{14,30},{16,0},... | collective-permute-start | bytes 196616 | tf_op jit(solution)/shard_map/ppermute | solution.py:559
  49.6 1.4 %collective-permute-done.8.refs_1_ = bf16[2,3,32,512]{3,2,1,0:T(8,128)(2,1)S(1)} collective-permute-done((bf16[2,3,32,512]{3,2,1,0:T(8,128)(2,1)S(1)}, bf16[2,3,32,512]{3,2,1,0:T(8,128)(2,1)S(1)}, u32[]{:S(2)}, u32[]{:S(2)}) %collective-permute-start.8) | collective-permute-done | bytes 196640 | tf_op jit(solution)/shard_map/ppermute | solution.py:449
  51.1 0.0 collective-permute-done.9.refs_2_
  51.1 0.9 %stage_last.1 = bf16[2,4,32,512]{3,2,1,0:T(8,128)(2,1)} custom-call(f32[2,4,32,512]{3,2,1,0:T(8,128)S(1)} %get-tuple-element.78.refs_0_, bf16[2,3,32,512]{3,2,1,0:T(8,128)(2,1)S(1)} %collective-permute-done.8.refs_1_, bf16[2,3,32,512]{3,2,1,0:T(8,128)(2,1)S(1)} %collective-permute-done.9.refs_2_, bf16[10,32,512]{2,1,0:T(8,128)(2,1)S(1)} %collective-permute-done.5.refs_9_.refs_3_), custom_call_target="tpu_custom_call" | custom-call | flops 1000000 | bytes 1048576 | tf_op jit(solution)/shard_map/stage_last/pallas_call | solution.py:32
  51.9 2.1 %collective-permute-done.12.refs_2_ = bf16[1,16,2048]{2,1,0:T(8,128)(2,1)S(1)} collective-permute-done((bf16[1,16,2048]{2,1,0:T(8,128)(2,1)S(1)}, bf16[1,16,2048]{2,1,0:T(8,128)(2,1)S(1)}, u32[]{:S(2)}, u32[]{:S(2)}) %collective-permute-start.12) | collective-permute-done | bytes 65568 | tf_op jit(solution)/shard_map/ppermute | solution.py:559
  54.1 0.0 collective-permute-done.13.refs_0_
  54.1 2.0 %collective-permute-done.14.refs_1_ = bf16[1,16,2048]{2,1,0:T(8,128)(2,1)S(1)} collective-permute-done((bf16[1,16,2048]{2,1,0:T(8,128)(2,1)S(1)}, bf16[1,16,2048]{2,1,0:T(8,128)(2,1)S(1)}, u32[]{:S(2)}, u32[]{:S(2)}) %collective-permute-start.14) | collective-permute-done | bytes 65568 | tf_op jit(solution)/shard_map/ppermute | solution.py:559
  56.1 0.7 %stage_sum.1 = (f32[16,1536]{1,0:T(8,128)}, f32[16,512]{1,0:T(8,128)}) custom-call(f32[1,16,2048]{2,1,0:T(8,128)S(1)} %get-tuple-element.92.x, bf16[1,16,2048]{2,1,0:T(8,128)(2,1)S(1)} %collective-permute-done.13.refs_0_, bf16[1,16,2048]{2,1,0:T(8,128)(2,1)S(1)} %collective-permute-done.14.refs_1_, bf16[1,16,2048]{2,1,0:T(8,128)(2,1)S(1)} %collective-permute-done.12.refs_2_), custom_call_target="tpu_custom_call" | custom-call | flops 1000000 | bytes 1048576 | tf_op jit(solution)/shard_map/stage_sum/pallas_call | solution.py:32
  (7 shorter events, 0.0 us)
Async XLA Ops:
  0.6 5.3 %copy-start = (bf16[512,1536]{1,0:T(8,128)(2,1)S(1)}, bf16[512,1536]{1,0:T(8,128)(2,1)}, u32[]{:S(2)}) copy-start(bf16[512,1536]{1,0:T(8,128)(2,1)} %refs_7_.3) | copy-start | bytes 4718596
  0.6 1.1 %copy-start.2 = (bf16[2,4,32,512]{3,2,1,0:T(8,128)(2,1)S(1)}, bf16[2,4,32,512]{3,2,1,0:T(8,128)(2,1)}, u32[]{:S(2)}) copy-start(bf16[2,4,32,512]{3,2,1,0:T(8,128)(2,1)} %refs_3_.5) | copy-start | bytes 786436
  1.7 4.3 %copy-start.1 = (bf16[512,512]{1,0:T(8,128)(2,1)S(1)}, bf16[512,512]{1,0:T(8,128)(2,1)}, u32[]{:S(2)}) copy-start(bf16[512,512]{1,0:T(8,128)(2,1)} %refs_8_.1) | copy-start | bytes 1572868
  1.7 4.3 %copy-start.3 = (bf16[2,4,32,512]{3,2,1,0:T(8,128)(2,1)S(1)}, bf16[2,4,32,512]{3,2,1,0:T(8,128)(2,1)}, u32[]{:S(2)}) copy-start(bf16[2,4,32,512]{3,2,1,0:T(8,128)(2,1)} %refs_3_.5) | copy-start | bytes 786436
  1.7 4.3 %copy-start.4 = (bf16[2,4,32,512]{3,2,1,0:T(8,128)(2,1)S(1)}, bf16[2,4,32,512]{3,2,1,0:T(8,128)(2,1)}, u32[]{:S(2)}) copy-start(bf16[2,4,32,512]{3,2,1,0:T(8,128)(2,1)} %refs_4_.3) | copy-start | bytes 786436
  1.7 4.3 %copy-start.5 = (s32[16]{0:T(128)S(1)}, s32[16]{0:T(128)}, u32[]{:S(2)}) copy-start(s32[16]{0:T(128)} %refs_0_.9) | copy-start | bytes 196
  1.7 4.3 %copy-start.6 = (s32[16]{0:T(128)S(1)}, s32[16]{0:T(128)}, u32[]{:S(2)}) copy-start(s32[16]{0:T(128)} %refs_1_.6) | copy-start | bytes 196
  2.2 3.8 %collective-permute-start.1 = (bf16[4,32,512]{2,1,0:T(8,128)(2,1)S(1)}, bf16[4,32,512]{2,1,0:T(8,128)(2,1)S(1)}, u32[]{:S(2)}, u32[]{:S(2)}) collective-permute-start(bf16[4,32,512]{2,1,0:T(8,128)(2,1)S(1)} %get-tuple-element.52), channel_id=1, source_target_pairs={{0,1},{1,0},{2,3},{3,2},{4,5},{5,4},{6,7},{7,6},{8,9},{9,8},{10,11... | collective-permute-start | bytes 393224 | tf_op jit(solution)/shard_map/ppermute | solution.py:449
  2.7 8.1 %collective-permute-start = (bf16[2,3,32,512]{3,2,1,0:T(8,128)(2,1)S(1)}, bf16[2,3,32,512]{3,2,1,0:T(8,128)(2,1)S(1)}, u32[]{:S(2)}, u32[]{:S(2)}) collective-permute-start(bf16[2,3,32,512]{3,2,1,0:T(8,128)(2,1)S(1)} %get-tuple-element.51), channel_id=1, source_target_pairs={{0,2},{2,0},{4,6},{6,4},{8,10},{10,8},{12,14},{14,12},{16,18},{18,... | collective-permute-start | bytes 589832 | tf_op jit(solution)/shard_map/ppermute | solution.py:449
  5.3 5.9 %collective-permute-start.3 = (bf16[2,3,32,512]{3,2,1,0:T(8,128)(2,1)S(1)}, bf16[2,3,32,512]{3,2,1,0:T(8,128)(2,1)S(1)}, u32[]{:S(2)}, u32[]{:S(2)}) collective-permute-start(bf16[2,3,32,512]{3,2,1,0:T(8,128)(2,1)S(1)} %get-tuple-element.58), channel_id=1, source_target_pairs={{2,4},{4,2},{6,8},{8,6},{10,12},{12,10},{14,16},{16,14},{18,20},{2... | collective-permute-start | bytes 589832 | tf_op jit(solution)/shard_map/ppermute | solution.py:449
  10.8 4.1 %collective-permute-start.2 = (bf16[2,3,32,512]{3,2,1,0:T(8,128)(2,1)S(1)}, bf16[2,3,32,512]{3,2,1,0:T(8,128)(2,1)S(1)}, u32[]{:S(2)}, u32[]{:S(2)}) collective-permute-start(bf16[2,3,32,512]{3,2,1,0:T(8,128)(2,1)S(1)} %collective-permute-done.refs_1_), channel_id=1, source_target_pairs={{0,1},{1,0},{2,3},{3,2},{4,5},{5,4},{6,7},{7,6},{8,9},{9,8},{10,11... | collective-permute-start | bytes 589832 | tf_op jit(solution)/shard_map/ppermute | solution.py:449
  11.2 3.7 %collective-permute-start.4 = (bf16[2,3,32,512]{3,2,1,0:T(8,128)(2,1)S(1)}, bf16[2,3,32,512]{3,2,1,0:T(8,128)(2,1)S(1)}, u32[]{:S(2)}, u32[]{:S(2)}) collective-permute-start(bf16[2,3,32,512]{3,2,1,0:T(8,128)(2,1)S(1)} %collective-permute-done.3.refs_2_), channel_id=1, source_target_pairs={{0,1},{1,0},{2,3},{3,2},{4,5},{5,4},{6,7},{7,6},{8,9},{9,8},{10,11... | collective-permute-start | bytes 589832 | tf_op jit(solution)/shard_map/ppermute | solution.py:449
  21.9 2.7 %collective-permute-start.6 = (bf16[16,16,2048]{2,1,0:T(8,128)(2,1)S(1)}, bf16[16,16,2048]{2,1,0:T(8,128)(2,1)S(1)}, u32[]{:S(2)}, u32[]{:S(2)}) collective-permute-start(bf16[16,16,2048]{2,1,0:T(8,128)(2,1)S(1)} %get-tuple-element.82), channel_id=1, source_target_pairs={{0,1},{1,0},{2,3},{3,2},{4,5},{5,4},{6,7},{7,6},{8,9},{9,8},{10,11... | collective-permute-start | bytes 3145736 | tf_op jit(solution)/shard_map/ppermute | solution.py:545
  23.3 9.2 %collective-permute-start.5 = (bf16[10,32,512]{2,1,0:T(8,128)(2,1)S(1)}, bf16[10,32,512]{2,1,0:T(8,128)(2,1)S(1)}, u32[]{:S(2)}, u32[]{:S(2)}) collective-permute-start(bf16[10,32,512]{2,1,0:T(8,128)(2,1)S(1)} %get-tuple-element.76), channel_id=1, source_target_pairs={{0,1},{1,0},{2,3},{3,2},{4,5},{5,4},{6,7},{7,6},{8,9},{9,8},{10,11... | collective-permute-start | bytes 983048 | tf_op jit(solution)/shard_map/ppermute | solution.py:449
  24.9 13.2 %collective-permute-start.7 = (bf16[4,16,2048]{2,1,0:T(8,128)(2,1)S(1)}, bf16[4,16,2048]{2,1,0:T(8,128)(2,1)S(1)}, u32[]{:S(2)}, u32[]{:S(2)}) collective-permute-start(bf16[4,16,2048]{2,1,0:T(8,128)(2,1)S(1)} %get-tuple-element.83), channel_id=1, source_target_pairs={{0,6},{2,4},{4,2},{6,0},{8,14},{10,12},{12,10},{14,8},{16,22},{18,... | collective-permute-start | bytes 786440 | tf_op jit(solution)/shard_map/ppermute | solution.py:559
  30.9 13.2 %collective-permute-start.10 = (bf16[4,16,2048]{2,1,0:T(8,128)(2,1)S(1)}, bf16[4,16,2048]{2,1,0:T(8,128)(2,1)S(1)}, u32[]{:S(2)}, u32[]{:S(2)}) collective-permute-start(bf16[4,16,2048]{2,1,0:T(8,128)(2,1)S(1)} %get-tuple-element.87), channel_id=1, source_target_pairs={{0,2},{2,0},{4,6},{6,4},{8,10},{10,8},{12,14},{14,12},{16,18},{18,... | collective-permute-start | bytes 786440 | tf_op jit(solution)/shard_map/ppermute | solution.py:559
  31.4 12.8 %collective-permute-start.11 = (bf16[4,16,2048]{2,1,0:T(8,128)(2,1)S(1)}, bf16[4,16,2048]{2,1,0:T(8,128)(2,1)S(1)}, u32[]{:S(2)}, u32[]{:S(2)}) collective-permute-start(bf16[4,16,2048]{2,1,0:T(8,128)(2,1)S(1)} %get-tuple-element.88), channel_id=1, source_target_pairs={{0,4},{2,6},{4,0},{6,2},{8,12},{10,14},{12,8},{14,10},{16,20},{18,... | collective-permute-start | bytes 786440 | tf_op jit(solution)/shard_map/ppermute | solution.py:559
  38.1 13.0 %collective-permute-start.8 = (bf16[2,3,32,512]{3,2,1,0:T(8,128)(2,1)S(1)}, bf16[2,3,32,512]{3,2,1,0:T(8,128)(2,1)S(1)}, u32[]{:S(2)}, u32[]{:S(2)}) collective-permute-start(bf16[2,3,32,512]{3,2,1,0:T(8,128)(2,1)S(1)} %get-tuple-element.84), channel_id=1, source_target_pairs={{0,2},{2,0},{4,6},{6,4},{8,10},{10,8},{12,14},{14,12},{16,18},{18,... | collective-permute-start | bytes 589832 | tf_op jit(solution)/shard_map/ppermute | solution.py:449
  41.1 9.9 %collective-permute-start.9 = (bf16[2,3,32,512]{3,2,1,0:T(8,128)(2,1)S(1)}, bf16[2,3,32,512]{3,2,1,0:T(8,128)(2,1)S(1)}, u32[]{:S(2)}, u32[]{:S(2)}) collective-permute-start(bf16[2,3,32,512]{3,2,1,0:T(8,128)(2,1)S(1)} %get-tuple-element.85), channel_id=1, source_target_pairs={{2,4},{4,2},{6,8},{8,6},{10,12},{12,10},{14,16},{16,14},{18,20},{2... | collective-permute-start | bytes 589832 | tf_op jit(solution)/shard_map/ppermute | solution.py:449
  44.2 9.8 %collective-permute-start.12 = (bf16[1,16,2048]{2,1,0:T(8,128)(2,1)S(1)}, bf16[1,16,2048]{2,1,0:T(8,128)(2,1)S(1)}, u32[]{:S(2)}, u32[]{:S(2)}) collective-permute-start(bf16[1,16,2048]{2,1,0:T(8,128)(2,1)S(1)} %get-tuple-element.90), channel_id=1, source_target_pairs={{0,24},{2,26},{4,28},{6,30},{8,16},{10,18},{12,20},{14,22},{16,8},... | collective-permute-start | bytes 196616 | tf_op jit(solution)/shard_map/ppermute | solution.py:559
  49.0 5.1 %collective-permute-start.13 = (bf16[1,16,2048]{2,1,0:T(8,128)(2,1)S(1)}, bf16[1,16,2048]{2,1,0:T(8,128)(2,1)S(1)}, u32[]{:S(2)}, u32[]{:S(2)}) collective-permute-start(bf16[1,16,2048]{2,1,0:T(8,128)(2,1)S(1)} %get-tuple-element.93), channel_id=1, source_target_pairs={{0,8},{2,10},{4,12},{6,14},{8,0},{10,2},{12,4},{14,6},{16,24},{18,... | collective-permute-start | bytes 196616 | tf_op jit(solution)/shard_map/ppermute | solution.py:559
  49.0 7.1 %collective-permute-start.14 = (bf16[1,16,2048]{2,1,0:T(8,128)(2,1)S(1)}, bf16[1,16,2048]{2,1,0:T(8,128)(2,1)S(1)}, u32[]{:S(2)}, u32[]{:S(2)}) collective-permute-start(bf16[1,16,2048]{2,1,0:T(8,128)(2,1)S(1)} %get-tuple-element.94), channel_id=1, source_target_pairs={{0,16},{2,18},{4,20},{6,22},{8,24},{10,26},{12,28},{14,30},{16,0},... | collective-permute-start | bytes 196616 | tf_op jit(solution)/shard_map/ppermute | solution.py:559

commit v7 on v5

--- a/solution.py
+++ b/solution.py
@@ -550,10 +550,10 @@
             [(share, F32)] + [(share, BF16)] * (radix - 1),
             [x, *parts],
         )
-        parts = [
-            lax.ppermute(piece, "tile", xor_route(tiles, (k + 1) * stride))
-            for k, piece in enumerate(pieces)
-        ]
+        sent = {}
+        for k in range(len(pieces))[::-1]:
+            sent[k] = lax.ppermute(pieces[k], "tile", xor_route(tiles, (k + 1) * stride))
+        parts = [sent[k] for k in range(len(pieces))]
         if stride == 1:
             send_e, send_o, parts[2] = lax.optimization_barrier((send_e, send_o, parts[2]))
         stride *= radix

time: 56.8 us -> 56.8 us (level)
  no operation moved by 1% of the time
where the time goes in v7:
time: 56.8 us; the launch traced here: 56.6 us
  starting transfers between devices  21.6 us (38%)
  Pallas kernels  16.6 us (29%)
  waiting for transfers between devices  16.5 us (29%)
  local copies, waits for them, and re-layouts  1.08 us (2%)
  between operations  0.82 us (1%)
    pallas_call x9, Pallas kernels, call(): pl.pallas_call(body, name=name, out_shape=[jax.ShapeDtypeStruct(shape, ki...  16.2 us
    ppermute x6, starting transfers between devices, local(): lax.ppermute(pieces[k], 'tile', xor_route(tiles, (k + 1) * stride))  12.9 us
    ppermute x6, waiting for transfers between devices, local(): lax.ppermute(pieces[k], 'tile', xor_route(tiles, (k + 1) * stride))  12.6 us
    ppermute x8, starting transfers between devices, swap(): return lax.ppermute(block, axis, swap_pairs(lax.axis_size(axis), first))  8.58 us
    ppermute x8, waiting for transfers between devices, swap(): return lax.ppermute(block, axis, swap_pairs(lax.axis_size(axis), first))  3.15 us
  transfers between devices with their start and end apart: 15, of which 7 were waited for; matrix products, arithmetic and copies ran while one was open for 0% of the time, Pallas kernels for 15%

profile of v7, /device:TPU:0, one launch (start us, length us, event | category | flops | bytes accessed | tf_op | source)
XLA Modules:
  0.0 56.6 jit_solution(15350370819402222841)
XLA Ops:
  0.6 0.0 copy-start
  0.6 0.0 copy-start.2
  0.7 1.1 %copy-done.2 = bf16[2,4,32,512]{3,2,1,0:T(8,128)(2,1)S(1)} copy-done((bf16[2,4,32,512]{3,2,1,0:T(8,128)(2,1)S(1)}, bf16[2,4,32,512]{3,2,1,0:T(8,128)(2,1)}, u32[]{:S(2)}) %copy-start.2) | copy-done | bytes 262168
  1.7 0.0 copy-start.6
  1.7 0.5 stage_cut.1
  2.2 0.5 collective-permute-start.1
  2.7 2.6 %collective-permute-start = (bf16[2,3,32,512]{3,2,1,0:T(8,128)(2,1)S(1)}, bf16[2,3,32,512]{3,2,1,0:T(8,128)(2,1)S(1)}, u32[]{:S(2)}, u32[]{:S(2)}) collective-permute-start(bf16[2,3,32,512]{3,2,1,0:T(8,128)(2,1)S(1)} %get-tuple-element.50), channel_id=1, source_target_pairs={{0,2},{2,0},{4,6},{6,4},{8,10},{10,8},{12,14},{14,12},{16,18},{18,... | collective-permute-start | bytes 589832 | tf_op jit(solution)/shard_map/ppermute | solution.py:445
  5.3 0.7 %collective-permute-start.3 = (bf16[2,3,32,512]{3,2,1,0:T(8,128)(2,1)S(1)}, bf16[2,3,32,512]{3,2,1,0:T(8,128)(2,1)S(1)}, u32[]{:S(2)}, u32[]{:S(2)}) collective-permute-start(bf16[2,3,32,512]{3,2,1,0:T(8,128)(2,1)S(1)} %get-tuple-element.57), channel_id=1, source_target_pairs={{2,4},{4,2},{6,8},{8,6},{10,12},{12,10},{14,16},{16,14},{18,20},{2... | collective-permute-start | bytes 589832 | tf_op jit(solution)/shard_map/ppermute | solution.py:445
  6.0 0.0 collective-permute-done.1.refs_6_.refs_8_
  6.0 0.0 copy-done
  6.0 0.0 copy-done.1
  6.0 0.0 copy-done.3
  6.0 0.0 copy-done.4
  6.0 1.6 %stage_own.1 = (bf16[2,4,32,512]{3,2,1,0:T(8,128)(2,1)S(1)}, bf16[2,4,32,512]{3,2,1,0:T(8,128)(2,1)S(1)}, bf16[3,4,32,1024]{3,2,1,0:T(8,128)(2,1)S(1)}) custom-call(s32[16]{0:T(128)S(1)} %copy-done.5, s32[16]{0:T(128)S(1)} %copy-done.6, bf16[2,4,32,512]{3,2,1,0:T(8,128)(2,1)S(1)} %copy-done.3, bf16[512,1536]{1,0:T(8,128)(2,1)S(1)} %copy-done, ...), custom_call_target="tpu_custom_call" | custom-call | flops 4000000000 | bytes 1048576 | tf_op jit(solution)/shard_map/stage_own/pallas_call | solution.py:32
  7.7 3.1 %collective-permute-done.refs_1_ = bf16[2,3,32,512]{3,2,1,0:T(8,128)(2,1)S(1)} collective-permute-done((bf16[2,3,32,512]{3,2,1,0:T(8,128)(2,1)S(1)}, bf16[2,3,32,512]{3,2,1,0:T(8,128)(2,1)S(1)}, u32[]{:S(2)}, u32[]{:S(2)}) %collective-permute-start) | collective-permute-done | bytes 196640 | tf_op jit(solution)/shard_map/ppermute | solution.py:445
  10.8 0.0 collective-permute-start.2
  10.8 0.4 stage_side.1
  11.2 0.0 collective-permute-done.3.refs_2_
  11.2 0.6 %collective-permute-start.4 = (bf16[2,3,32,512]{3,2,1,0:T(8,128)(2,1)S(1)}, bf16[2,3,32,512]{3,2,1,0:T(8,128)(2,1)S(1)}, u32[]{:S(2)}, u32[]{:S(2)}) collective-permute-start(bf16[2,3,32,512]{3,2,1,0:T(8,128)(2,1)S(1)} %collective-permute-done.3.refs_2_), channel_id=1, source_target_pairs={{0,1},{1,0},{2,3},{3,2},{4,5},{5,4},{6,7},{7,6},{8,9},{9,8},{10,11... | collective-permute-start | bytes 589832 | tf_op jit(solution)/shard_map/ppermute | solution.py:445
  11.8 3.1 %stage_inner.1 = (bf16[3,10,32,512]{3,2,1,0:T(8,128)(2,1)S(1)}, bf16[3,10,32,1024]{3,2,1,0:T(8,128)(2,1)S(1)}, bf16[2,3,10,32,1024]{4,3,2,1,0:T(8,128)(2,1)S(1)}...) custom-call(s32[16]{0:T(128)S(1)} %copy-done.5, ...), custom_call_target="tpu_custom_call", output_to_operand_aliasing={{0}: (6, {}), {1}: (7, {})} | custom-call | flops 8000000000 | bytes 1048576 | tf_op jit(solution)/shard_map/stage_inner/pallas_call | solution.py:32
  14.9 0.0 collective-permute-done.2.refs_9_
  14.9 0.0 collective-permute-done.4.refs_10_
  14.9 7.0 %stage_attend.1 = (bf16[3,10,32,512]{3,2,1,0:T(8,128)(2,1)S(1)}, bf16[3,10,32,1024]{3,2,1,0:T(8,128)(2,1)S(1)}, bf16[2,3,10,32,1024]{4,3,2,1,0:T(8,128)(2,1)S(1)...) custom-call(s32[16]{0:T(128)S(1)} %copy-done.5, ...), custom_call_target="tpu_custom_call", output_to_operand_aliasing={{0}: (11, {}), {1}: (12, {}), {2}: (13, {}), {3}: (14, {}),... | custom-call | flops 16000000000 | bytes 1048576 | tf_op jit(solution)/shard_map/stage_attend/pallas_call | solution.py:32
  21.9 0.1 collective-permute-start.6
  22.0 1.3 %stage_out.1 = (f32[2,4,32,512]{3,2,1,0:T(8,128)S(1)}, f32[2,3,32,512]{3,2,1,0:T(8,128)S(1)}, f32[2,3,32,512]{3,2,1,0:T(8,128)S(1)}, bf16[10,32,512]{2,1,0:T(8,128)(2,1)S(1)}) custom-call(bf16[3,10,32,1024]{3,2,1,0:T(8,128)(2,1)S(1)} %get-tuple-element.69.refs_0_, bf16[512,1536]{1,0:T(8,128)(2,1)S(1)} %copy-done), custom_call_target="tpu_custom_call" | custom-call | flops 4000000000 | bytes 1048576 | tf_op jit(solution)/shard_map/stage_out/pallas_call | solution.py:32
  23.3 0.6 collective-permute-start.5
  23.9 0.8 %collective-permute-done.6.refs_1_ = bf16[16,16,2048]{2,1,0:T(8,128)(2,1)S(1)} collective-permute-done((bf16[16,16,2048]{2,1,0:T(8,128)(2,1)S(1)}, bf16[16,16,2048]{2,1,0:T(8,128)(2,1)S(1)}, u32[]{:S(2)}, u32[]{:S(2)}) %collective-permute-start.6) | collective-permute-done | bytes 1048608 | tf_op jit(solution)/shard_map/ppermute | solution.py:541
  24.6 0.2 stage_split.2
  24.9 6.0 %collective-permute-start.7 = (bf16[4,16,2048]{2,1,0:T(8,128)(2,1)S(1)}, bf16[4,16,2048]{2,1,0:T(8,128)(2,1)S(1)}, u32[]{:S(2)}, u32[]{:S(2)}) collective-permute-start(bf16[4,16,2048]{2,1,0:T(8,128)(2,1)S(1)} %get-tuple-element.82), channel_id=1, source_target_pairs={{0,6},{2,4},{4,2},{6,0},{8,14},{10,12},{12,10},{14,8},{16,22},{18,... | collective-permute-start | bytes 786440 | tf_op jit(solution)/shard_map/ppermute | solution.py:555
  30.9 0.5 collective-permute-start.10
  31.4 1.2 %collective-permute-start.11 = (bf16[4,16,2048]{2,1,0:T(8,128)(2,1)S(1)}, bf16[4,16,2048]{2,1,0:T(8,128)(2,1)S(1)}, u32[]{:S(2)}, u32[]{:S(2)}) collective-permute-start(bf16[4,16,2048]{2,1,0:T(8,128)(2,1)S(1)} %get-tuple-element.87), channel_id=1, source_target_pairs={{0,4},{2,6},{4,0},{6,2},{8,12},{10,14},{12,8},{14,10},{16,20},{18,... | collective-permute-start | bytes 786440 | tf_op jit(solution)/shard_map/ppermute | solution.py:555
  32.5 0.0 collective-permute-done.5.refs_9_.refs_7_
  32.5 1.5 %stage_fold.1 = (bf16[2,3,32,512]{3,2,1,0:T(8,128)(2,1)S(1)}, bf16[2,3,32,512]{3,2,1,0:T(8,128)(2,1)S(1)}, bf16[2,4,32,512]{3,2,1,0:T(8,128)(2,1)}, f32[2,4,32,512]{3,2,1,0:T(8,128)S(1)}) custom-call(f32[2,3,32,512]{3,2,1,0:T(8,128)S(1)} %get-tuple-element.70.refs_0_, f32[2,3,32,512]{3,2,1,0:T(8,128)S(1)} %get-tuple-element.71.refs_1_, ...), custom_call_target="tpu_custom_call" | custom-call | flops 1000000 | bytes 1048576 | tf_op jit(solution)/shard_map/stage_fold/pallas_call | solution.py:32
  34.0 4.1 %collective-permute-done.7.refs_3_ = bf16[4,16,2048]{2,1,0:T(8,128)(2,1)S(1)} collective-permute-done((bf16[4,16,2048]{2,1,0:T(8,128)(2,1)S(1)}, bf16[4,16,2048]{2,1,0:T(8,128)(2,1)S(1)}, u32[]{:S(2)}, u32[]{:S(2)}) %collective-permute-start.7) | collective-permute-done | bytes 262176 | tf_op jit(solution)/shard_map/ppermute | solution.py:555
  38.1 3.1 %collective-permute-start.8 = (bf16[2,3,32,512]{3,2,1,0:T(8,128)(2,1)S(1)}, bf16[2,3,32,512]{3,2,1,0:T(8,128)(2,1)S(1)}, u32[]{:S(2)}, u32[]{:S(2)}) collective-permute-start(bf16[2,3,32,512]{3,2,1,0:T(8,128)(2,1)S(1)} %get-tuple-element.83), channel_id=1, source_target_pairs={{0,2},{2,0},{4,6},{6,4},{8,10},{10,8},{12,14},{14,12},{16,18},{18,... | collective-permute-start | bytes 589832 | tf_op jit(solution)/shard_map/ppermute | solution.py:445
  41.1 0.7 %collective-permute-start.9 = (bf16[2,3,32,512]{3,2,1,0:T(8,128)(2,1)S(1)}, bf16[2,3,32,512]{3,2,1,0:T(8,128)(2,1)S(1)}, u32[]{:S(2)}, u32[]{:S(2)}) collective-permute-start(bf16[2,3,32,512]{3,2,1,0:T(8,128)(2,1)S(1)} %get-tuple-element.84), channel_id=1, source_target_pairs={{2,4},{4,2},{6,8},{8,6},{10,12},{12,10},{14,16},{16,14},{18,20},{2... | collective-permute-start | bytes 589832 | tf_op jit(solution)/shard_map/ppermute | solution.py:445
  41.8 2.3 %collective-permute-done.10.refs_1_ = bf16[4,16,2048]{2,1,0:T(8,128)(2,1)S(1)} collective-permute-done((bf16[4,16,2048]{2,1,0:T(8,128)(2,1)S(1)}, bf16[4,16,2048]{2,1,0:T(8,128)(2,1)S(1)}, u32[]{:S(2)}, u32[]{:S(2)}) %collective-permute-start.10) | collective-permute-done | bytes 262176 | tf_op jit(solution)/shard_map/ppermute | solution.py:555
  44.1 0.0 collective-permute-done.11.refs_2_
  44.1 0.1 stage_split.3
  44.2 2.7 %collective-permute-start.12 = (bf16[1,16,2048]{2,1,0:T(8,128)(2,1)S(1)}, bf16[1,16,2048]{2,1,0:T(8,128)(2,1)S(1)}, u32[]{:S(2)}, u32[]{:S(2)}) collective-permute-start(bf16[1,16,2048]{2,1,0:T(8,128)(2,1)S(1)} %get-tuple-element.90), channel_id=1, source_target_pairs={{0,8},{2,10},{4,12},{6,14},{8,0},{10,2},{12,4},{14,6},{16,24},{18,... | collective-permute-start | bytes 196616 | tf_op jit(solution)/shard_map/ppermute | solution.py:555
  47.0 2.6 %collective-permute-start.13 = (bf16[1,16,2048]{2,1,0:T(8,128)(2,1)S(1)}, bf16[1,16,2048]{2,1,0:T(8,128)(2,1)S(1)}, u32[]{:S(2)}, u32[]{:S(2)}) collective-permute-start(bf16[1,16,2048]{2,1,0:T(8,128)(2,1)S(1)} %get-tuple-element.91), channel_id=1, source_target_pairs={{0,16},{2,18},{4,20},{6,22},{8,24},{10,26},{12,28},{14,30},{16,0},... | collective-permute-start | bytes 196616 | tf_op jit(solution)/shard_map/ppermute | solution.py:555
  49.5 0.0 collective-permute-start.14
  49.5 0.6 %collective-permute-done.12.refs_4_ = bf16[1,16,2048]{2,1,0:T(8,128)(2,1)S(1)} collective-permute-done((bf16[1,16,2048]{2,1,0:T(8,128)(2,1)S(1)}, bf16[1,16,2048]{2,1,0:T(8,128)(2,1)S(1)}, u32[]{:S(2)}, u32[]{:S(2)}) %collective-permute-start.12) | collective-permute-done | bytes 65568 | tf_op jit(solution)/shard_map/ppermute | solution.py:555
  50.2 3.8 %collective-permute-done.13.refs_5_ = bf16[1,16,2048]{2,1,0:T(8,128)(2,1)S(1)} collective-permute-done((bf16[1,16,2048]{2,1,0:T(8,128)(2,1)S(1)}, bf16[1,16,2048]{2,1,0:T(8,128)(2,1)S(1)}, u32[]{:S(2)}, u32[]{:S(2)}) %collective-permute-start.13) | collective-permute-done | bytes 65568 | tf_op jit(solution)/shard_map/ppermute | solution.py:555
  54.0 1.8 %collective-permute-done.14.refs_6_ = bf16[1,16,2048]{2,1,0:T(8,128)(2,1)S(1)} collective-permute-done((bf16[1,16,2048]{2,1,0:T(8,128)(2,1)S(1)}, bf16[1,16,2048]{2,1,0:T(8,128)(2,1)S(1)}, u32[]{:S(2)}, u32[]{:S(2)}) %collective-permute-start.14) | collective-permute-done | bytes 65568 | tf_op jit(solution)/shard_map/ppermute | solution.py:555
  55.7 0.0 collective-permute-done.8.refs_1_
  55.7 0.0 collective-permute-done.9.refs_2_
  55.7 0.9 %stage_last.1 = (bf16[2,4,32,512]{3,2,1,0:T(8,128)(2,1)}, f32[16,1536]{1,0:T(8,128)}, f32[16,512]{1,0:T(8,128)}) custom-call(f32[2,4,32,512]{3,2,1,0:T(8,128)S(1)} %get-tuple-element.77.refs_0_, bf16[2,3,32,512]{3,2,1,0:T(8,128)(2,1)S(1)} %collective-permute-done.8.refs_1_, bf16[2,3,32,512]{3,2,1,0:T(8,128)(2,1)S(1)} %collective-permute-done.9.refs_2_, ...), custom_call_target="tpu_custom_call" | custom-call | flops 1000000 | bytes 1048576 | tf_op jit(solution)/shard_map/stage_last/pallas_call | solution.py:32
  (6 shorter events, 0.0 us)
Async XLA Ops:
  0.6 5.3 %copy-start = (bf16[512,1536]{1,0:T(8,128)(2,1)S(1)}, bf16[512,1536]{1,0:T(8,128)(2,1)}, u32[]{:S(2)}) copy-start(bf16[512,1536]{1,0:T(8,128)(2,1)} %refs_7_.3) | copy-start | bytes 4718596
  0.6 1.1 %copy-start.2 = (bf16[2,4,32,512]{3,2,1,0:T(8,128)(2,1)S(1)}, bf16[2,4,32,512]{3,2,1,0:T(8,128)(2,1)}, u32[]{:S(2)}) copy-start(bf16[2,4,32,512]{3,2,1,0:T(8,128)(2,1)} %refs_3_.5) | copy-start | bytes 786436
  1.7 4.3 %copy-start.1 = (bf16[512,512]{1,0:T(8,128)(2,1)S(1)}, bf16[512,512]{1,0:T(8,128)(2,1)}, u32[]{:S(2)}) copy-start(bf16[512,512]{1,0:T(8,128)(2,1)} %refs_8_.1) | copy-start | bytes 1572868
  1.7 4.3 %copy-start.3 = (bf16[2,4,32,512]{3,2,1,0:T(8,128)(2,1)S(1)}, bf16[2,4,32,512]{3,2,1,0:T(8,128)(2,1)}, u32[]{:S(2)}) copy-start(bf16[2,4,32,512]{3,2,1,0:T(8,128)(2,1)} %refs_3_.5) | copy-start | bytes 786436
  1.7 4.3 %copy-start.4 = (bf16[2,4,32,512]{3,2,1,0:T(8,128)(2,1)S(1)}, bf16[2,4,32,512]{3,2,1,0:T(8,128)(2,1)}, u32[]{:S(2)}) copy-start(bf16[2,4,32,512]{3,2,1,0:T(8,128)(2,1)} %refs_4_.3) | copy-start | bytes 786436
  1.7 4.3 %copy-start.5 = (s32[16]{0:T(128)S(1)}, s32[16]{0:T(128)}, u32[]{:S(2)}) copy-start(s32[16]{0:T(128)} %refs_0_.9) | copy-start | bytes 196
  1.7 4.3 %copy-start.6 = (s32[16]{0:T(128)S(1)}, s32[16]{0:T(128)}, u32[]{:S(2)}) copy-start(s32[16]{0:T(128)} %refs_1_.6) | copy-start | bytes 196
  2.2 3.8 %collective-permute-start.1 = (bf16[4,32,512]{2,1,0:T(8,128)(2,1)S(1)}, bf16[4,32,512]{2,1,0:T(8,128)(2,1)S(1)}, u32[]{:S(2)}, u32[]{:S(2)}) collective-permute-start(bf16[4,32,512]{2,1,0:T(8,128)(2,1)S(1)} %get-tuple-element.51), channel_id=1, source_target_pairs={{0,1},{1,0},{2,3},{3,2},{4,5},{5,4},{6,7},{7,6},{8,9},{9,8},{10,11... | collective-permute-start | bytes 393224 | tf_op jit(solution)/shard_map/ppermute | solution.py:445
  2.7 8.1 %collective-permute-start = (bf16[2,3,32,512]{3,2,1,0:T(8,128)(2,1)S(1)}, bf16[2,3,32,512]{3,2,1,0:T(8,128)(2,1)S(1)}, u32[]{:S(2)}, u32[]{:S(2)}) collective-permute-start(bf16[2,3,32,512]{3,2,1,0:T(8,128)(2,1)S(1)} %get-tuple-element.50), channel_id=1, source_target_pairs={{0,2},{2,0},{4,6},{6,4},{8,10},{10,8},{12,14},{14,12},{16,18},{18,... | collective-permute-start | bytes 589832 | tf_op jit(solution)/shard_map/ppermute | solution.py:445
  5.3 5.9 %collective-permute-start.3 = (bf16[2,3,32,512]{3,2,1,0:T(8,128)(2,1)S(1)}, bf16[2,3,32,512]{3,2,1,0:T(8,128)(2,1)S(1)}, u32[]{:S(2)}, u32[]{:S(2)}) collective-permute-start(bf16[2,3,32,512]{3,2,1,0:T(8,128)(2,1)S(1)} %get-tuple-element.57), channel_id=1, source_target_pairs={{2,4},{4,2},{6,8},{8,6},{10,12},{12,10},{14,16},{16,14},{18,20},{2... | collective-permute-start | bytes 589832 | tf_op jit(solution)/shard_map/ppermute | solution.py:445
  10.8 4.1 %collective-permute-start.2 = (bf16[2,3,32,512]{3,2,1,0:T(8,128)(2,1)S(1)}, bf16[2,3,32,512]{3,2,1,0:T(8,128)(2,1)S(1)}, u32[]{:S(2)}, u32[]{:S(2)}) collective-permute-start(bf16[2,3,32,512]{3,2,1,0:T(8,128)(2,1)S(1)} %collective-permute-done.refs_1_), channel_id=1, source_target_pairs={{0,1},{1,0},{2,3},{3,2},{4,5},{5,4},{6,7},{7,6},{8,9},{9,8},{10,11... | collective-permute-start | bytes 589832 | tf_op jit(solution)/shard_map/ppermute | solution.py:445
  11.2 3.7 %collective-permute-start.4 = (bf16[2,3,32,512]{3,2,1,0:T(8,128)(2,1)S(1)}, bf16[2,3,32,512]{3,2,1,0:T(8,128)(2,1)S(1)}, u32[]{:S(2)}, u32[]{:S(2)}) collective-permute-start(bf16[2,3,32,512]{3,2,1,0:T(8,128)(2,1)S(1)} %collective-permute-done.3.refs_2_), channel_id=1, source_target_pairs={{0,1},{1,0},{2,3},{3,2},{4,5},{5,4},{6,7},{7,6},{8,9},{9,8},{10,11... | collective-permute-start | bytes 589832 | tf_op jit(solution)/shard_map/ppermute | solution.py:445
  21.9 2.7 %collective-permute-start.6 = (bf16[16,16,2048]{2,1,0:T(8,128)(2,1)S(1)}, bf16[16,16,2048]{2,1,0:T(8,128)(2,1)S(1)}, u32[]{:S(2)}, u32[]{:S(2)}) collective-permute-start(bf16[16,16,2048]{2,1,0:T(8,128)(2,1)S(1)} %get-tuple-element.81), channel_id=1, source_target_pairs={{0,1},{1,0},{2,3},{3,2},{4,5},{5,4},{6,7},{7,6},{8,9},{9,8},{10,11... | collective-permute-start | bytes 3145736 | tf_op jit(solution)/shard_map/ppermute | solution.py:541
  23.3 9.2 %collective-permute-start.5 = (bf16[10,32,512]{2,1,0:T(8,128)(2,1)S(1)}, bf16[10,32,512]{2,1,0:T(8,128)(2,1)S(1)}, u32[]{:S(2)}, u32[]{:S(2)}) collective-permute-start(bf16[10,32,512]{2,1,0:T(8,128)(2,1)S(1)} %get-tuple-element.75), channel_id=1, source_target_pairs={{0,1},{1,0},{2,3},{3,2},{4,5},{5,4},{6,7},{7,6},{8,9},{9,8},{10,11... | collective-permute-start | bytes 983048 | tf_op jit(solution)/shard_map/ppermute | solution.py:445
  24.9 13.2 %collective-permute-start.7 = (bf16[4,16,2048]{2,1,0:T(8,128)(2,1)S(1)}, bf16[4,16,2048]{2,1,0:T(8,128)(2,1)S(1)}, u32[]{:S(2)}, u32[]{:S(2)}) collective-permute-start(bf16[4,16,2048]{2,1,0:T(8,128)(2,1)S(1)} %get-tuple-element.82), channel_id=1, source_target_pairs={{0,6},{2,4},{4,2},{6,0},{8,14},{10,12},{12,10},{14,8},{16,22},{18,... | collective-permute-start | bytes 786440 | tf_op jit(solution)/shard_map/ppermute | solution.py:555
  30.9 13.2 %collective-permute-start.10 = (bf16[4,16,2048]{2,1,0:T(8,128)(2,1)S(1)}, bf16[4,16,2048]{2,1,0:T(8,128)(2,1)S(1)}, u32[]{:S(2)}, u32[]{:S(2)}) collective-permute-start(bf16[4,16,2048]{2,1,0:T(8,128)(2,1)S(1)} %get-tuple-element.86), channel_id=1, source_target_pairs={{0,2},{2,0},{4,6},{6,4},{8,10},{10,8},{12,14},{14,12},{16,18},{18,... | collective-permute-start | bytes 786440 | tf_op jit(solution)/shard_map/ppermute | solution.py:555
  31.4 12.8 %collective-permute-start.11 = (bf16[4,16,2048]{2,1,0:T(8,128)(2,1)S(1)}, bf16[4,16,2048]{2,1,0:T(8,128)(2,1)S(1)}, u32[]{:S(2)}, u32[]{:S(2)}) collective-permute-start(bf16[4,16,2048]{2,1,0:T(8,128)(2,1)S(1)} %get-tuple-element.87), channel_id=1, source_target_pairs={{0,4},{2,6},{4,0},{6,2},{8,12},{10,14},{12,8},{14,10},{16,20},{18,... | collective-permute-start | bytes 786440 | tf_op jit(solution)/shard_map/ppermute | solution.py:555
  38.1 17.7 %collective-permute-start.8 = (bf16[2,3,32,512]{3,2,1,0:T(8,128)(2,1)S(1)}, bf16[2,3,32,512]{3,2,1,0:T(8,128)(2,1)S(1)}, u32[]{:S(2)}, u32[]{:S(2)}) collective-permute-start(bf16[2,3,32,512]{3,2,1,0:T(8,128)(2,1)S(1)} %get-tuple-element.83), channel_id=1, source_target_pairs={{0,2},{2,0},{4,6},{6,4},{8,10},{10,8},{12,14},{14,12},{16,18},{18,... | collective-permute-start | bytes 589832 | tf_op jit(solution)/shard_map/ppermute | solution.py:445
  41.1 14.6 %collective-permute-start.9 = (bf16[2,3,32,512]{3,2,1,0:T(8,128)(2,1)S(1)}, bf16[2,3,32,512]{3,2,1,0:T(8,128)(2,1)S(1)}, u32[]{:S(2)}, u32[]{:S(2)}) collective-permute-start(bf16[2,3,32,512]{3,2,1,0:T(8,128)(2,1)S(1)} %get-tuple-element.84), channel_id=1, source_target_pairs={{2,4},{4,2},{6,8},{8,6},{10,12},{12,10},{14,16},{16,14},{18,20},{2... | collective-permute-start | bytes 589832 | tf_op jit(solution)/shard_map/ppermute | solution.py:445
  44.2 5.9 %collective-permute-start.12 = (bf16[1,16,2048]{2,1,0:T(8,128)(2,1)S(1)}, bf16[1,16,2048]{2,1,0:T(8,128)(2,1)S(1)}, u32[]{:S(2)}, u32[]{:S(2)}) collective-permute-start(bf16[1,16,2048]{2,1,0:T(8,128)(2,1)S(1)} %get-tuple-element.90), channel_id=1, source_target_pairs={{0,8},{2,10},{4,12},{6,14},{8,0},{10,2},{12,4},{14,6},{16,24},{18,... | collective-permute-start | bytes 196616 | tf_op jit(solution)/shard_map/ppermute | solution.py:555
  47.0 7.0 %collective-permute-start.13 = (bf16[1,16,2048]{2,1,0:T(8,128)(2,1)S(1)}, bf16[1,16,2048]{2,1,0:T(8,128)(2,1)S(1)}, u32[]{:S(2)}, u32[]{:S(2)}) collective-permute-start(bf16[1,16,2048]{2,1,0:T(8,128)(2,1)S(1)} %get-tuple-element.91), channel_id=1, source_target_pairs={{0,16},{2,18},{4,20},{6,22},{8,24},{10,26},{12,28},{14,30},{16,0},... | collective-permute-start | bytes 196616 | tf_op jit(solution)/shard_map/ppermute | solution.py:555
  49.5 6.2 %collective-permute-start.14 = (bf16[1,16,2048]{2,1,0:T(8,128)(2,1)S(1)}, bf16[1,16,2048]{2,1,0:T(8,128)(2,1)S(1)}, u32[]{:S(2)}, u32[]{:S(2)}) collective-permute-start(bf16[1,16,2048]{2,1,0:T(8,128)(2,1)S(1)} %get-tuple-element.92), channel_id=1, source_target_pairs={{0,24},{2,26},{4,28},{6,30},{8,16},{10,18},{12,20},{14,22},{16,8},... | collective-permute-start | bytes 196616 | tf_op jit(solution)/shard_map/ppermute | solution.py:555
